TPU v7x, 32 devices: a whole 2x2x4 slice. The times are simulated.
32 devices in a mesh: gz: 8 (over y, x, core), xy: 4 (over z).
Axes of the slice: x: 2, y: 2, z: 4, core: 2. Of those that a mesh axis runs over, the one named last changes fastest.
Arguments:
- flux_xface: bfloat16 [8, 2048, 2048], P(None, 'gz', 'xy'), may hold values from -6 to 6
- flux_yspec: bfloat16 [8, 2048, 2048], P(None, 'gz', 'xy'), may hold values from -6 to 6
- flux_zface: bfloat16 [8, 2048, 2048], P(None, 'gz', 'xy'), may hold values from -6 to 6
- frequency_y: int32 [8], replicated, may hold values from 0 to 2047
Outputs:
- potential: float32 [8, 2048, 2, 1024], P('gz', 'xy')
All inputs are finite; a program needn't handle non-finite values.
Results may differ from a plain program's by a relative error of at most 0.0003.
Values may be sent and summed in bfloat16 or wider, within the bound.
No kernel may reach another device: no remote copies, remote signals or barrier semaphores. Data moves between devices by JAX's collectives and lax.ppermute only.
A program may use at most 64 MiB of HBM per device.

v0:
```python
import math

import jax
import jax.numpy as jnp
from jax import lax
from jax.sharding import PartitionSpec as P

NX = 2048
NY = 2048
NZ = 2048


SCREEN_WEIGHT = 0.5


def shifted(block, axis, distance):
    devices = range(lax.axis_size(axis))
    route = [(i - distance, i) for i in devices if i - distance in devices]
    return lax.ppermute(block, axis, route)


def cosine_table(length, parity):
    halved = length // 2
    row_index = lax.broadcasted_iota(jnp.int32, (halved, halved), 0)
    col_index = lax.broadcasted_iota(jnp.int32, (halved, halved), 1)
    frequency = 2 * row_index + parity
    phase = frequency * (2 * col_index + 1) % (4 * length)
    scaling = jnp.where(frequency == 0, math.sqrt(1.0 / length), math.sqrt(2.0 / length)).astype(
        jnp.float32
    )
    return scaling * jnp.cos(phase.astype(jnp.float32) * (math.pi / (2 * length)))


def fold_middle(source):
    length = source.shape[1]
    halved = length // 2
    upper_half = source[:, :halved]
    lower_half = lax.rev(source[:, halved:], (1,))
    even_part = jnp.einsum(
        "kq,fql->fkl",
        cosine_table(length, 0),
        upper_half + lower_half,
        precision=lax.Precision.HIGHEST,
    )
    odd_part = jnp.einsum(
        "kq,fql->fkl",
        cosine_table(length, 1),
        upper_half - lower_half,
        precision=lax.Precision.HIGHEST,
    )
    return jnp.stack([even_part, odd_part], axis=2).reshape(source.shape)


def fold_last(source):
    length = source.shape[2]
    halved = length // 2
    upper_half = source[:, :, :halved]
    lower_half = lax.rev(source[:, :, halved:], (2,))
    even_part = jnp.einsum(
        "yzn,mn->yzm",
        upper_half + lower_half,
        cosine_table(length, 0),
        precision=lax.Precision.HIGHEST,
    )
    odd_part = jnp.einsum(
        "yzn,mn->yzm",
        upper_half - lower_half,
        cosine_table(length, 1),
        precision=lax.Precision.HIGHEST,
    )
    return jnp.stack([even_part, odd_part], axis=2)


def eigenvalue(index, length):
    sine = jnp.sin(index.astype(jnp.float32) * (math.pi / (2 * length)))
    return 4.0 * sine * sine


def shards(flux_xface, flux_yspec, flux_zface, frequency_y):
    x_rank = lax.axis_index("xy")
    x_count = lax.axis_size("xy")
    z_rank = lax.axis_index("gz")
    z_count = lax.axis_size("gz")
    planes = flux_xface.shape[1]
    x_width = flux_xface.shape[2]
    x_position = lax.broadcasted_iota(jnp.int32, flux_xface.shape, 2)
    x_keep = jnp.logical_not((x_rank == x_count - 1) & (x_position == x_width - 1))
    masked_x = jnp.where(x_keep, flux_xface, jnp.zeros_like(flux_xface))
    x_edge = shifted(masked_x[:, :, x_width - 1 :], "xy", 1)
    x_before = jnp.concatenate([x_edge, masked_x[:, :, : x_width - 1]], axis=2)
    weight_y = 2.0 * jnp.sin(frequency_y.astype(jnp.float32) * (math.pi / (2 * NY)))
    partial_value = (
        masked_x.astype(jnp.float32)
        - x_before.astype(jnp.float32)
        + weight_y[:, None, None] * flux_yspec.astype(jnp.float32)
    )
    z_position = lax.broadcasted_iota(jnp.int32, flux_zface.shape, 1)
    z_keep = jnp.logical_not((z_rank == z_count - 1) & (z_position == planes - 1))
    masked_z = jnp.where(z_keep, flux_zface, jnp.zeros_like(flux_zface))
    z_edge = shifted(masked_z[:, planes - 1 :, :], "gz", 1)
    z_before = jnp.concatenate([z_edge, masked_z[:, : planes - 1]], axis=1)
    slab = partial_value + masked_z.astype(jnp.float32) - z_before.astype(jnp.float32)
    totals = lax.all_to_all(slab, "gz", split_axis=0, concat_axis=1, tiled=True)
    spectrum_z = fold_middle(totals)
    x_lines = lax.all_to_all(spectrum_z, "xy", split_axis=1, concat_axis=2, tiled=True)
    spectrum = fold_last(x_lines)
    row_count = spectrum.shape[0]
    kz_count = spectrum.shape[1]
    halved = spectrum.shape[3]
    local_freq = lax.dynamic_slice_in_dim(frequency_y, z_rank * row_count, row_count)
    weight_local = 2.0 * jnp.sin(local_freq.astype(jnp.float32) * (math.pi / (2 * NY)))
    kz_index = x_rank * kz_count + lax.broadcasted_iota(jnp.int32, (kz_count,), 0)
    kx_index = 2 * lax.broadcasted_iota(jnp.int32, (2, halved), 1) + lax.broadcasted_iota(
        jnp.int32, (2, halved), 0
    )
    denominator = (
        (weight_local * weight_local)[:, None, None, None]
        + eigenvalue(kz_index, NZ)[None, :, None, None]
        + eigenvalue(kx_index, NX)[None, None, :, :]
        + SCREEN_WEIGHT
    )
    return -spectrum / denominator


def solution(mesh):
    return jax.shard_map(
        shards,
        mesh=mesh,
        in_specs=(P(None, "gz", "xy"), P(None, "gz", "xy"), P(None, "gz", "xy"), P()),
        out_specs=P("gz", "xy", None, None),
        check_vma=False,
    )
```

profile of v0, /device:TPU:0, one launch (start us, length us, event | category | flops | bytes accessed | tf_op | source)
XLA Modules:
  0.0 356.9 jit_solution(9749636749683457343)
XLA Ops:
  0.0 1.8 broadcast_select_fusion
  1.9 2.4 collective-permute-start.1
  4.3 1.9 broadcast_select_fusion.1
  6.4 4.3 %collective-permute-start = (bf16[8,256,1]{2,1,0:T(8,128)(2,1)S(1)}, bf16[8,256,1]{2,1,0:T(8,128)(2,1)S(1)}, u32[]{:S(2)}, u32[]{:S(2)}) collective-permute-start(bf16[8,256,1]{2,1,0:T(8,128)(2,1)S(1)} %slice.32), channel_id=1, source_target_pairs={{0,1},{1,2},{2,3},{4,5},{5,6},{6,7},{8,9},{9,10},{10,11},{12,13},{... | collective-permute-start | bytes 12296 | tf_op jit(solution)/shard_map/ppermute | solution.py:19
  10.8 11.4 %collective-permute-done = bf16[8,256,1]{2,1,0:T(8,128)(2,1)S(1)} collective-permute-done((bf16[8,256,1]{2,1,0:T(8,128)(2,1)S(1)}, bf16[8,256,1]{2,1,0:T(8,128)(2,1)S(1)}, u32[]{:S(2)}, u32[]{:S(2)}) %collective-permute-start) | collective-permute-done | bytes 4128 | tf_op jit(solution)/shard_map/ppermute | solution.py:19
  22.2 5.5 %convert_subtract_fusion = f32[8,256,512]{2,1,0:T(8,128)} fusion(bf16[8,256,512]{2,1,0:T(8,128)(2,1)} %param.5, bf16[8,256,511]{2,1,0:T(8,128)(2,1)S(1)} %bitcast.46, bf16[8,256,1]{2,1,0:T(8,128)(2,1)S(1)} %collective-permute-done, bf16[8,255,512]{2,1,0:T(8,128)(2,1)S(1)} %bitcast.50, bf16[8,1,512]{2,1,0:T(2,128)(2,1)S(1)} %collective-permute-done.1, ...), kind=kLoop, calls=%fused_computation.23 | loop fusion | flops 18874368 | bytes 14680864 | tf_op jit(solution)/shard_map/sub | solution.py:102
  27.7 4.6 %all-to-all-start = ((f32[8,256,512]{2,1,0:T(8,128)}), f32[8,256,512]{2,1,0:T(8,128)}, u32[]{:S(2)}, u32[]{:S(2)}) async-start(f32[8,256,512]{2,1,0:T(8,128)} %convert_subtract_fusion), calls=%async_computation | async-start | bytes 8388608 | tf_op jit(solution)/shard_map/all_to_all | solution.py:103
  32.3 49.1 %all-to-all-done = f32[8,256,512]{2,1,0:T(8,128)} async-done(((f32[8,256,512]{2,1,0:T(8,128)}), f32[8,256,512]{2,1,0:T(8,128)}, u32[]{:S(2)}, u32[]{:S(2)}) %all-to-all-start) | async-done | bytes 4194336 | tf_op jit(solution)/shard_map/all_to_all | solution.py:103
  81.4 1.8 slice.37
  83.2 10.3 %rev.6 = f32[1,1024,512]{2,1,0:T(8,128)} reverse(f32[1,1024,512]{2,1,0:T(8,128)S(1)} %slice.37), dimensions={1} | reverse | bytes 4194304 | tf_op jit(solution)/shard_map/rev | solution.py:38
  93.5 32.1 %fusion.36 = f32[1,1024,1,512]{1,3,2,0:T(8,128)S(1)} fusion(s32[1024]{0:T(1024)S(1)} %get-tuple-element.6, f32[1024]{0:T(1024)S(1)} %compare_select_fusion, f32[1,1024,512]{2,1,0:T(8,128)} %rev.6, f32[1,2048,512]{2,1,0:T(8,128)} %bitcast), kind=kOutput, calls=%fused_computation.43 | convolution fusion | flops 6458703872 | bytes 6303744 | tf_op jit(solution)/shard_map/kq,fql->fkl/dot_general | solution.py:45
  125.6 30.9 %fusion.31 = f32[1,1024,1,512]{1,3,2,0:T(8,128)S(1)} fusion(s32[1024]{0:T(1024)S(1)} %get-tuple-element.6, s32[1024]{0:T(1024)S(1)} %get-tuple-element.5, f32[1024]{0:T(1024)S(1)} %compare_select_fusion.1, f32[1,1024,512]{2,1,0:T(8,128)S(1)} %copy-done.4, f32[1,2048,512]{2,1,0:T(8,128)} %bitcast), kind=kOutput, calls=%fused_computation.42 | convolution fusion | flops 6458703872 | bytes 6303744 | tf_op jit(solution)/shard_map/kq,fql->fkl/dot_general | solution.py:39
  156.5 2.3 pad_maximum_fusion
  158.8 11.0 %copy.6 = f32[1,1024,2,512]{3,0,2,1:T(1,128)} copy(f32[1,1024,2,512]{1,3,2,0:T(8,128)} %pad_maximum_fusion) | data formatting | bytes 8388608 | tf_op jit(solution)/shard_map/stack | solution.py:51
  169.8 5.8 %all-to-all-start.1 = ((f32[1,2048,512]{2,0,1:T(1,128)}), f32[1,2048,512]{2,0,1:T(1,128)}, u32[]{:S(2)}, u32[]{:S(2)}) async-start(f32[1,2048,512]{2,0,1:T(1,128)} %bitcast.45), calls=%async_computation.1 | async-start | bytes 8388608 | tf_op jit(solution)/shard_map/all_to_all | solution.py:105
  175.5 0.6 dynamic_slice.3
  177.0 89.2 %all-to-all-done.1 = f32[1,2048,512]{2,0,1:T(1,128)} async-done(((f32[1,2048,512]{2,0,1:T(1,128)}), f32[1,2048,512]{2,0,1:T(1,128)}, u32[]{:S(2)}, u32[]{:S(2)}) %all-to-all-start.1) | async-done | bytes 4194336 | tf_op jit(solution)/shard_map/all_to_all | solution.py:105
  266.2 10.9 %copy.7 = f32[1,4,512,512]{2,3,1,0:T(8,128)} copy(f32[1,4,512,512]{3,0,2,1:T(1,128)} %bitcast.10) | data formatting | bytes 8388608 | tf_op jit(solution)/shard_map/all_to_all | solution.py:105
  277.1 1.8 slice.39
  278.9 10.5 %rev.7 = f32[1,512,1024]{1,2,0:T(8,128)} reverse(f32[1,512,1024]{1,2,0:T(8,128)S(1)} %slice.39), dimensions={2} | reverse | bytes 4194304 | tf_op jit(solution)/shard_map/rev | solution.py:58
  289.4 31.6 %fusion.41 = f32[1,512,1,1024]{3,1,2,0:T(8,128)S(1)} fusion(s32[1024]{0:T(1024)S(1)} %get-tuple-element.6, s32[1024]{0:T(1024)S(1)} %get-tuple-element.5, f32[1024]{0:T(1024)S(1)} %compare_select_fusion.1, f32[1,512,1024]{1,2,0:T(8,128)} %rev.7, f32[1,512,2048]{1,2,0:T(8,128)} %bitcast.48), kind=kOutput, calls=%fused_computation.44 | convolution fusion | flops 6458703872 | bytes 6303744 | tf_op jit(solution)/shard_map/yzn,mn->yzm/dot_general | solution.py:59
  321.1 29.4 %fusion.46 = f32[1,512,1,1024]{3,1,2,0:T(8,128)S(1)} fusion(s32[1024]{0:T(1024)S(1)} %get-tuple-element.6, f32[1024]{0:T(1024)S(1)} %compare_select_fusion, f32[1,512,1024]{1,2,0:T(8,128)S(1)} %copy-done.3, f32[1,512,2048]{1,2,0:T(8,128)S(1)} %bitcast.49), kind=kOutput, calls=%fused_computation.45 | convolution fusion | flops 6458703872 | bytes 6303744 | tf_op jit(solution)/shard_map/yzn,mn->yzm/dot_general | solution.py:65
  350.5 0.8 fusion.10
  351.2 5.2 %copy.8 = f32[1,512,2,1024]{3,2,1,0:T(2,128)} copy(f32[1,512,2,1024]{3,1,2,0:T(8,128)S(1)} %fusion.10) | data formatting | bytes 8388608 | tf_op jit(solution)/shard_map/div | solution.py:122
  (23 shorter events, 0.5 us)
Async XLA Ops:
  0.0 10.7 %copy-start.5 = (s32[8]{0:T(128)S(1)}, s32[8]{0:T(128)}, u32[]{:S(2)}) copy-start(s32[8]{0:T(128)} %param.7) | copy-start | bytes 100
  1.9 20.4 %collective-permute-start.1 = (bf16[8,1,512]{2,1,0:T(2,128)(2,1)S(1)}, bf16[8,1,512]{2,1,0:T(2,128)(2,1)S(1)}, u32[]{:S(2)}, u32[]{:S(2)}) collective-permute-start(bf16[8,1,512]{2,1,0:T(2,128)(2,1)S(1)} %slice.34), channel_id=1, source_target_pairs={{0,4},{4,8},{8,12},{12,16},{16,20},{20,24},{24,28},{1,5},{5,9},{9,... | collective-permute-start | bytes 24584 | tf_op jit(solution)/shard_map/ppermute | solution.py:19
  4.2 18.0 %copy-start.1 = (bf16[8,256,512]{2,1,0:T(8,128)(2,1)S(1)}, bf16[8,256,512]{2,1,0:T(8,128)(2,1)}, u32[]{:S(2)}) copy-start(bf16[8,256,512]{2,1,0:T(8,128)(2,1)} %param.4) | copy-start | bytes 6291460
  4.2 18.0 %copy-start.2 = (bf16[8,256,512]{2,1,0:T(8,128)(2,1)S(1)}, bf16[8,256,512]{2,1,0:T(8,128)(2,1)}, u32[]{:S(2)}) copy-start(bf16[8,256,512]{2,1,0:T(8,128)(2,1)} %param.6) | copy-start | bytes 6291460
  6.4 15.8 %collective-permute-start = (bf16[8,256,1]{2,1,0:T(8,128)(2,1)S(1)}, bf16[8,256,1]{2,1,0:T(8,128)(2,1)S(1)}, u32[]{:S(2)}, u32[]{:S(2)}) collective-permute-start(bf16[8,256,1]{2,1,0:T(8,128)(2,1)S(1)} %slice.32), channel_id=1, source_target_pairs={{0,1},{1,2},{2,3},{4,5},{5,6},{6,7},{8,9},{9,10},{10,11},{12,13},{... | collective-permute-start | bytes 12296 | tf_op jit(solution)/shard_map/ppermute | solution.py:19
  27.7 53.7 %all-to-all-start = ((f32[8,256,512]{2,1,0:T(8,128)}), f32[8,256,512]{2,1,0:T(8,128)}, u32[]{:S(2)}, u32[]{:S(2)}) async-start(f32[8,256,512]{2,1,0:T(8,128)} %convert_subtract_fusion), calls=%async_computation | async-start | bytes 8388608 | tf_op jit(solution)/shard_map/all_to_all | solution.py:103
  93.5 32.1 %copy-start.4 = (f32[1,1024,512]{2,1,0:T(8,128)S(1)}, f32[1,1024,512]{2,1,0:T(8,128)}, u32[]{:S(2)}) copy-start(f32[1,1024,512]{2,1,0:T(8,128)} %rev.6) | copy-start | bytes 6291460
  169.8 96.5 %all-to-all-start.1 = ((f32[1,2048,512]{2,0,1:T(1,128)}), f32[1,2048,512]{2,0,1:T(1,128)}, u32[]{:S(2)}, u32[]{:S(2)}) async-start(f32[1,2048,512]{2,0,1:T(1,128)} %bitcast.45), calls=%async_computation.1 | async-start | bytes 8388608 | tf_op jit(solution)/shard_map/all_to_all | solution.py:105
  289.4 31.7 %copy-start = (f32[1,4,512,512]{2,3,1,0:T(8,128)S(1)}, f32[1,4,512,512]{2,3,1,0:T(8,128)}, u32[]{:S(2)}) copy-start(f32[1,4,512,512]{2,3,1,0:T(8,128)} %copy.7) | copy-start | bytes 12582916
  289.4 31.7 %copy-start.3 = (f32[1,512,1024]{1,2,0:T(8,128)S(1)}, f32[1,512,1024]{1,2,0:T(8,128)}, u32[]{:S(2)}) copy-start(f32[1,512,1024]{1,2,0:T(8,128)} %rev.7) | copy-start | bytes 6291460
where the time goes:
time: 361 us; the launch traced here: 357 us
  waiting for transfers between devices  150 us (42%)
  matrix products  124 us (34%)
  local copies, waits for them, and re-layouts  52.3 us (14%)
  starting transfers between devices  17 us (5%)
  other arithmetic  12.5 us (3%)
    all_to_all x1, waiting for transfers between devices, shards(): lax.all_to_all(spectrum_z, 'xy', split_axis=1, concat_axis=2, tiled=True)  89.2 us
    all_to_all x1, waiting for transfers between devices, shards(): totals = lax.all_to_all(slab, 'gz', split_axis=0, concat_axis=1, tiled=True)  49.1 us
    dot_general x1, matrix products, fold_middle(): jnp.einsum('kq,fql->fkl', cosine_table(length, 1), upper_half - lower_hal...  32.1 us
    dot_general x1, matrix products, fold_last(): jnp.einsum('yzn,mn->yzm', upper_half + lower_half, cosine_table(length, 0...  31.6 us
    dot_general x1, matrix products, fold_middle(): jnp.einsum('kq,fql->fkl', cosine_table(length, 0), upper_half + lower_hal...  30.9 us
    dot_general x1, matrix products, fold_last(): jnp.einsum('yzn,mn->yzm', upper_half - lower_half, cosine_table(length, 1...  29.4 us
    ppermute x2, waiting for transfers between devices, shifted(): return lax.ppermute(block, axis, route)  11.4 us
    another operation x1, local copies, waits for them, and re-layouts, fold_middle(): return jnp.stack([even_part, odd_part], axis=2).reshape(source.shape)  11 us
  transfers between devices with their start and end apart: 4, of which 3 were waited for; matrix products, arithmetic and copies ran while one was open for 1% of the time, Pallas kernels for 0%

commit v1 on v0

--- a/solution.py
+++ b/solution.py
@@ -1,8 +1,12 @@
+import functools
 import math
 
 import jax
 import jax.numpy as jnp
+import numpy as np
 from jax import lax
+from jax.experimental import pallas as pl
+from jax.experimental.pallas import tpu as pltpu
 from jax.sharding import PartitionSpec as P
 
 NX = 2048
@@ -76,7 +80,7 @@
     return 4.0 * sine * sine
 
 
-def shards(flux_xface, flux_yspec, flux_zface, frequency_y):
+def plain_shards(flux_xface, flux_yspec, flux_zface, frequency_y):
     x_rank = lax.axis_index("xy")
     x_count = lax.axis_size("xy")
     z_rank = lax.axis_index("gz")
@@ -122,6 +126,412 @@
     return -spectrum / denominator
 
 
+LANES = 128
+GROUP = 32
+META = 16
+STEPS = 64.0
+TOP = 32700.0
+BLOCKS = 8
+RESIDUES = 2 * BLOCKS
+
+
+def split_bf16(table):
+    high = table.astype(jnp.bfloat16)
+    low = (table - high.astype(np.float64)).astype(jnp.bfloat16)
+    return np.stack([high, low])
+
+
+def scaled_cosine(frequency, position, length, wave=np.cos):
+    phase = (frequency[:, None] * (2 * position[None, :] + 1)) % (4 * length)
+    scaling = np.where(frequency == 0, math.sqrt(1.0 / length), math.sqrt(2.0 / length))
+    return scaling[:, None] * wave(phase * (math.pi / (2 * length)))
+
+
+def z_tables(length):
+    inner = np.arange(length // BLOCKS)
+    outer = RESIDUES * np.arange(length // RESIDUES)
+    pairs = []
+    for r in range(1, BLOCKS):
+        upper = [scaled_cosine(outer + r, inner, length), -scaled_cosine(outer + r, inner, length, np.sin)]
+        mirror = outer + RESIDUES - r
+        lower = [scaled_cosine(mirror, inner, length), scaled_cosine(mirror, inner, length, np.sin)]
+        pairs.append(np.concatenate([np.concatenate(upper, axis=1), np.concatenate(lower, axis=1)], axis=0))
+    ends = [scaled_cosine(outer, inner, length), scaled_cosine(outer + BLOCKS, inner, length)]
+    return split_bf16(np.stack(pairs)), split_bf16(np.stack(ends))
+
+
+def x_tables(length, positions):
+    halved = length // 2
+    tables = [scaled_cosine(2 * np.arange(halved) + p, positions, length).T for p in (0, 1)]
+    return split_bf16(np.stack(tables))
+
+
+def steps_of(largest):
+    return jnp.ceil(jnp.log2(jnp.maximum(largest, 2.0**-100)) * STEPS)
+
+
+def encoded(values, extra=None):
+    largest = jnp.max(jnp.abs(values), axis=1)
+    if extra is not None:
+        largest = jnp.maximum(largest, extra)
+    steps = steps_of(largest)
+    factor = TOP * jnp.exp2(steps * (-1.0 / STEPS))
+    return jnp.round(values * factor[:, None, :]).astype(jnp.int32), steps, factor
+
+
+def decoded(codes, steps):
+    scale = jnp.exp2(steps * (1.0 / STEPS)) * (1.0 / TOP)
+    groups = steps.shape[0]
+    values = codes.astype(jnp.int32).astype(jnp.float32).reshape(groups, GROUP, codes.shape[-1])
+    return values * scale[:, None, :], scale
+
+
+def divergence_kernel(tiles, has_edge, *refs):
+    place, weight = refs[0], refs[1]
+    flux_x, flux_y, flux_z = refs[2:5]
+    rest = refs[5:]
+    if has_edge:
+        edge_in, *rest = rest
+    outs = rest[:BLOCKS]
+    z_rank, z_count, x_rank, x_count = place[0], place[1], place[2], place[3]
+    step = pl.program_id(0)
+    y = z_rank ^ step
+    rows, width = flux_x.shape[1], flux_x.shape[2]
+    last_tile = width // LANES - 1
+    reverse = x_rank >= x_count // 2
+    row_at = lax.broadcasted_iota(jnp.int32, (LANES, LANES), 0)
+    col_at = lax.broadcasted_iota(jnp.int32, (LANES, LANES), 1)
+    col_at = jnp.where(reverse, LANES - 1 - col_at, col_at)
+    take = (row_at == col_at).astype(jnp.float32)
+    below = (row_at + 1 == col_at).astype(jnp.float32)
+    wrap = ((row_at == LANES - 1) & (col_at == 0)).astype(jnp.bfloat16)
+    pick = take.astype(jnp.bfloat16)
+    y_weight = weight[y]
+    dot = functools.partial(jnp.dot, preferred_element_type=jnp.float32)
+    z_last = jnp.where(z_rank == z_count - 1, rows - 1, rows)
+    row_id = lax.broadcasted_iota(jnp.int32, (rows, LANES), 0)
+    for at, tile in enumerate(tiles):
+        source = jnp.where(reverse, last_tile - tile, tile)
+        lanes = pl.ds(pl.multiple_of(source * LANES, LANES), LANES)
+        drop_last = (x_rank == x_count - 1) & (source == last_tile)
+        keep = jnp.where(drop_last & (row_at == LANES - 1), 0.0, take)
+        value = dot(flux_x[0, :, lanes], (keep - below).astype(jnp.bfloat16))
+        before = jnp.maximum(source - 1, 0)
+        before_lanes = pl.ds(pl.multiple_of(before * LANES, LANES), LANES)
+        wrap_here = wrap if not has_edge else jnp.where(source == 0, jnp.zeros_like(wrap), wrap)
+        value -= dot(flux_x[0, :, before_lanes], wrap_here)
+        if has_edge:
+            halo_row = lax.broadcasted_iota(jnp.int32, (edge_in.shape[0], LANES), 0)
+            halo_col = lax.broadcasted_iota(jnp.int32, (edge_in.shape[0], LANES), 1)
+            halo_col = jnp.where(reverse, LANES - 1 - halo_col, halo_col)
+            chosen = (halo_row == y) & (halo_col == 0) & (source == 0) & (x_rank > 0)
+            value -= lax.dot_general(
+                edge_in[...].astype(jnp.bfloat16),
+                chosen.astype(jnp.bfloat16),
+                (((0,), (0,)), ((), ())),
+                preferred_element_type=jnp.float32,
+            )
+        value += y_weight * dot(flux_y[0, :, lanes], pick)
+        face = jnp.where(row_id == z_last, 0.0, dot(flux_z[0, :, lanes], pick))
+        face_before = jnp.where(row_id == 0, 0.0, pltpu.roll(face, 1, 0))
+        value += face - face_before
+        halo = -face[rows - 1 :]
+        groups = rows // GROUP
+        at_end = lax.broadcasted_iota(jnp.int32, (groups, LANES), 0) == groups - 1
+        extra = jnp.where(at_end, jnp.abs(halo), 0.0)
+        codes, steps, factor = encoded(value.reshape(groups, GROUP, LANES), extra)
+        halo_code = jnp.round(halo * factor[groups - 1 :])
+        filler = jnp.zeros((META - groups - 1, LANES), jnp.float32)
+        meta = jnp.concatenate([steps, halo_code, filler], axis=0).astype(jnp.int32)
+        message = jnp.concatenate([codes.reshape(rows, LANES), meta], axis=0).astype(jnp.int16)
+        for d in range(BLOCKS):
+
+            @pl.when(step == d)
+            def _(d=d):
+                outs[d][:, at * LANES : (at + 1) * LANES] = message
+
+    if not has_edge:
+        edge_out = rest[BLOCKS]
+        ending = lax.broadcasted_iota(jnp.int32, (8, LANES), 1) == LANES - 1
+        column = lax.dot_general(
+            ending.astype(jnp.bfloat16),
+            flux_x[0, :, width - LANES :],
+            (((1,), (1,)), ((), ())),
+            preferred_element_type=jnp.float32,
+        )
+        edge_out[pl.ds(y, 1), :] = column[:1]
+
+
+def divergence(tiles, place, weight, fluxes, edge=None):
+    y_count, rows, width = fluxes[0].shape
+    chunk = len(tiles) * LANES
+    out_shape = [jax.ShapeDtypeStruct((rows + META, chunk), jnp.int16)] * BLOCKS
+    out_specs = [pl.BlockSpec((rows + META, chunk), lambda d, *_: (0, 0))] * BLOCKS
+    in_specs = [pl.BlockSpec((1, rows, width), lambda d, place, weight: (place[0] ^ d, 0, 0))] * 3
+    operands = list(fluxes)
+    if edge is None:
+        out_shape.append(jax.ShapeDtypeStruct((y_count, rows), jnp.float32))
+        out_specs.append(pl.BlockSpec((y_count, rows), lambda d, *_: (0, 0)))
+    else:
+        in_specs.append(pl.BlockSpec((y_count, rows), lambda d, *_: (0, 0)))
+        operands.append(edge)
+    return pl.pallas_call(
+        functools.partial(divergence_kernel, tiles, edge is not None),
+        grid_spec=pltpu.PrefetchScalarGridSpec(
+            num_scalar_prefetch=2, grid=(BLOCKS,), in_specs=in_specs, out_specs=out_specs
+        ),
+        out_shape=out_shape,
+        compiler_params=pltpu.CompilerParams(vmem_limit_bytes=40 << 20),
+        cost_estimate=pl.CostEstimate(
+            flops=8 * y_count * rows * chunk * LANES, bytes_accessed=8 * y_count * rows * chunk, transcendentals=0
+        ),
+        name="divergence",
+    )(place, weight, *operands)
+
+
+def z_kernel(place, *refs):
+    pieces = refs[:BLOCKS]
+    pair_table, end_table = refs[BLOCKS : BLOCKS + 2]
+    outs = refs[BLOCKS + 2 : -5]
+    blocks, halos, high, low, result = refs[-5:]
+    z_rank, x_rank = place[0], place[2]
+    rows = blocks.shape[1]
+    chunk = blocks.shape[2]
+    groups = rows // GROUP
+    for d in range(BLOCKS):
+        source = z_rank ^ d
+        meta = pieces[d][rows:, :].astype(jnp.int32).astype(jnp.float32)
+        values, scale = decoded(pieces[d][:rows, :], meta[:groups])
+        blocks[source] = values.reshape(rows, chunk)
+        halos[pl.ds(source, 1), :] = meta[groups : groups + 1] * scale[groups - 1 :]
+    for b in range(1, BLOCKS):
+        blocks[b, :1, :] += halos[b - 1 : b, :]
+
+    near, far, mid = math.cos(math.pi / 8), math.sin(math.pi / 8), math.sqrt(0.5)
+    strip = 16
+
+    def keep(r, part, start, value):
+        spot = pl.ds(part * rows + start, strip)
+        rounded = value.astype(jnp.bfloat16)
+        high[r, spot, :] = rounded
+        low[r, spot, :] = (value - rounded.astype(jnp.float32)).astype(jnp.bfloat16)
+
+    def combine(i, carry):
+        start = pl.multiple_of(i * strip, strip)
+        v = [blocks[b, pl.ds(start, strip), :] for b in range(BLOCKS)]
+        p1, p2, p3 = v[1] + v[7], v[2] + v[6], v[3] + v[5]
+        n1, n2, n3 = v[1] - v[7], v[2] - v[6], v[3] - v[5]
+        ends, gap = v[0] + v[4], v[0] - v[4]
+        odd = p1 + p3
+        even = ends + p2
+        keep(0, 0, start, even + odd)
+        keep(8, 0, start, even - odd)
+        keep(4, 0, start, ends - p2)
+        turn = mid * (p1 - p3)
+        keep(2, 0, start, gap + turn)
+        keep(6, 0, start, gap - turn)
+        turn = mid * (n1 + n3)
+        keep(2, 1, start, turn + n2)
+        keep(6, 1, start, turn - n2)
+        keep(4, 1, start, n1 - n3)
+        m2 = mid * n2
+        s, t = v[0] + m2, near * n1 + far * n3
+        keep(1, 0, start, s + t)
+        keep(7, 0, start, s - t)
+        s, t = v[0] - m2, far * n1 - near * n3
+        keep(3, 0, start, s + t)
+        keep(5, 0, start, s - t)
+        m2 = mid * p2
+        s, t = far * p1 + near * p3, m2 + v[4]
+        keep(1, 1, start, s + t)
+        keep(7, 1, start, s - t)
+        s, t = near * p1 - far * p3, m2 - v[4]
+        keep(3, 1, start, s + t)
+        keep(5, 1, start, s - t)
+        return carry
+
+    lax.fori_loop(0, rows // strip, combine, 0)
+    dot = functools.partial(jnp.dot, preferred_element_type=jnp.float32)
+    half = result.shape[1]
+    for r in range(1, BLOCKS):
+        value = dot(pair_table[0, r - 1], high[r])
+        value += dot(pair_table[0, r - 1], low[r])
+        value += dot(pair_table[1, r - 1], high[r])
+        result[r] = value[:half]
+        result[RESIDUES - r] = value[half:]
+    for e, r in enumerate((0, BLOCKS)):
+        value = dot(end_table[0, e], high[r, :rows, :])
+        value += dot(end_table[0, e], low[r, :rows, :])
+        value += dot(end_table[1, e], high[r, :rows, :])
+        result[r] = value
+    share = half // len(outs)
+    per = share // GROUP
+    for e, out in enumerate(outs):
+        first = pl.multiple_of((x_rank ^ e) * share, GROUP)
+        metas = []
+        for r in range(RESIDUES):
+            values = result[r, pl.ds(first, share), :].reshape(per, GROUP, chunk)
+            codes, steps, _ = encoded(values)
+            out[r * share : (r + 1) * share, :] = codes.reshape(share, chunk).astype(jnp.int16)
+            metas.append(steps)
+        out[RESIDUES * share :, :] = jnp.concatenate(metas, axis=0).astype(jnp.int32).astype(jnp.int16)
+
+
+def z_transform(place, pieces, tables, x_count):
+    rows = pieces[0].shape[0] - META
+    chunk = pieces[0].shape[1]
+    length = rows * BLOCKS
+    out_rows = length // x_count + META
+    vmem = pl.BlockSpec(memory_space=pltpu.VMEM)
+    return pl.pallas_call(
+        z_kernel,
+        in_specs=[pl.BlockSpec(memory_space=pltpu.SMEM)] + [vmem] * (BLOCKS + 2),
+        out_specs=[vmem] * x_count,
+        out_shape=[jax.ShapeDtypeStruct((out_rows, chunk), jnp.int16)] * x_count,
+        scratch_shapes=[
+            pltpu.VMEM((BLOCKS, rows, chunk), jnp.float32),
+            pltpu.VMEM((BLOCKS, chunk), jnp.float32),
+            pltpu.VMEM((BLOCKS + 1, 2 * rows, chunk), jnp.bfloat16),
+            pltpu.VMEM((BLOCKS + 1, 2 * rows, chunk), jnp.bfloat16),
+            pltpu.VMEM((RESIDUES, length // RESIDUES, chunk), jnp.float32),
+        ],
+        compiler_params=pltpu.CompilerParams(vmem_limit_bytes=40 << 20),
+        cost_estimate=pl.CostEstimate(
+            flops=3 * length * length // 2 * chunk, bytes_accessed=8 * length * chunk, transcendentals=0
+        ),
+        name="z_transform",
+    )(place, *pieces, *tables)
+
+
+def x_kernel(last, *refs):
+    place = refs[0]
+    refs = refs[1:]
+    x_count = 4
+    pieces = refs[:x_count]
+    table = refs[x_count]
+    refs = refs[x_count + 1 :]
+    if last:
+        total, row_part, col_part, out, values, high, low = refs
+    else:
+        out, values, high, low = refs
+    x_rank = place[2]
+    rows, chunk = values.shape[2], values.shape[1] * LANES
+    per = rows // RESIDUES // GROUP
+    for e in range(x_count):
+        source = x_rank ^ e
+        steps = pieces[e][rows:, :].astype(jnp.int32).astype(jnp.float32)
+        for r in range(RESIDUES):
+            share = rows // RESIDUES
+            part, _ = decoded(pieces[e][r * share : (r + 1) * share, :], steps[r * per : (r + 1) * per])
+            part = part.reshape(share, chunk)
+            for t in range(chunk // LANES):
+                values[source, t, pl.ds(r, share, stride=RESIDUES), :] = part[:, t * LANES : (t + 1) * LANES]
+    half = x_count // 2
+    for j in range(half):
+        for t in range(chunk // LANES):
+            near, far = values[j, t], values[x_count - 1 - j, t]
+            lanes = slice(j * chunk + t * LANES, j * chunk + (t + 1) * LANES)
+            for p, value in enumerate((near + far, near - far)):
+                rounded = value.astype(jnp.bfloat16)
+                high[p, :, lanes] = rounded
+                low[p, :, lanes] = (value - rounded.astype(jnp.float32)).astype(jnp.bfloat16)
+    dot = functools.partial(jnp.dot, preferred_element_type=jnp.float32)
+    count = table.shape[3]
+    width = 256
+    for p in range(2):
+        for c in range(count // width):
+            cols = slice(c * width, (c + 1) * width)
+            value = dot(high[p], table[0, p, :, cols])
+            value += dot(low[p], table[0, p, :, cols])
+            value += dot(high[p], table[1, p, :, cols])
+            if not last:
+                out[p, :, cols] = value
+                continue
+            value += total[p, :, cols]
+            for t in range(width // LANES):
+                tile = c * (width // LANES) + t
+                lanes = slice(tile * LANES, (tile + 1) * LANES)
+                below = row_part[...] + col_part[p : p + 1, lanes]
+                part = value[:, t * LANES : (t + 1) * LANES] / below
+                per_row = 2 * count // LANES
+                out[pl.ds(2 * tile + p, rows, stride=per_row), :] = part
+
+
+def x_transform(place, pieces, table, ending=None):
+    x_count = len(pieces)
+    rows = pieces[0].shape[0] - META
+    chunk = pieces[0].shape[1]
+    count = table.shape[3]
+    vmem = pl.BlockSpec(memory_space=pltpu.VMEM)
+    last = ending is not None
+    extra = list(ending) if last else []
+    shape = (rows * 2 * count // LANES, LANES) if last else (2, rows, count)
+    return pl.pallas_call(
+        functools.partial(x_kernel, last),
+        in_specs=[pl.BlockSpec(memory_space=pltpu.SMEM)] + [vmem] * (x_count + 1 + len(extra)),
+        out_specs=vmem,
+        out_shape=jax.ShapeDtypeStruct(shape, jnp.float32),
+        scratch_shapes=[
+            pltpu.VMEM((x_count, chunk // LANES, rows, LANES), jnp.float32),
+            pltpu.VMEM((2, rows, x_count // 2 * chunk), jnp.bfloat16),
+            pltpu.VMEM((2, rows, x_count // 2 * chunk), jnp.bfloat16),
+        ],
+        compiler_params=pltpu.CompilerParams(vmem_limit_bytes=40 << 20),
+        cost_estimate=pl.CostEstimate(
+            flops=6 * rows * x_count * chunk * count, bytes_accessed=16 * rows * count, transcendentals=0
+        ),
+        name="x_transform",
+    )(place, *pieces, table, *extra)
+
+
+def exchanged(pieces, axis, order):
+    count = len(pieces)
+    received = [pieces[0]] + [None] * (count - 1)
+    for d in order:
+        received[d] = lax.ppermute(pieces[d], axis, [(i, i ^ d) for i in range(count)])
+    return received
+
+
+def shards(flux_xface, flux_yspec, flux_zface, frequency_y):
+    z_count = lax.axis_size("gz")
+    x_count = lax.axis_size("xy")
+    y_count, planes, x_width = flux_xface.shape
+    length_z, length_x = planes * z_count, x_width * x_count
+    fits = z_count == BLOCKS and y_count == BLOCKS and x_count == 4 and x_width == 4 * LANES
+    if not fits or planes % GROUP or planes // GROUP >= META or length_z != RESIDUES * GROUP * x_count:
+        return plain_shards(flux_xface, flux_yspec, flux_zface, frequency_y)
+    z_rank, x_rank = lax.axis_index("gz"), lax.axis_index("xy")
+    place = jnp.stack([z_rank, jnp.int32(z_count), x_rank, jnp.int32(x_count)]).astype(jnp.int32)
+    weight_y = 2.0 * jnp.sin(frequency_y.astype(jnp.float32) * (math.pi / (2 * NY)))
+    fluxes = (flux_xface, flux_yspec, flux_zface)
+    inner, outer = (1, 2), (0, 3)
+    tables_z = z_tables(length_z)
+    order = (6, 7, 2, 4, 3, 5, 1)
+    *first, edge = divergence(inner, place, weight_y, fluxes)
+    edge_before = lax.ppermute(edge, "xy", [(i, i + 1) for i in range(x_count - 1)])
+    lanes = np.arange(LANES)
+
+    def positions(tiles):
+        return np.concatenate([j * x_width + t * LANES + lanes for j in range(x_count // 2) for t in tiles])
+
+    first = exchanged(first, "gz", order)
+    second = divergence(outer, place, weight_y, fluxes, edge_before)
+    second = exchanged(second, "gz", order)
+    first = exchanged(z_transform(place, first, tables_z, x_count), "xy", (3, 2, 1))
+    second = exchanged(z_transform(place, second, tables_z, x_count), "xy", (3, 2, 1))
+    kz_count = length_z // x_count
+    halved = length_x // 2
+    local_weight = weight_y[z_rank]
+    kz_index = x_rank * kz_count + lax.broadcasted_iota(jnp.int32, (kz_count, LANES), 0)
+    row_part = -(local_weight * local_weight + eigenvalue(kz_index, length_z) + SCREEN_WEIGHT)
+    kx_index = 2 * np.arange(halved)[None, :] + np.arange(2)[:, None]
+    col_part = np.asarray(-4.0 * np.sin(kx_index * (math.pi / (2 * length_x))) ** 2, np.float32)
+    total = x_transform(place, first, x_tables(length_x, positions(inner)))
+    flat = x_transform(place, second, x_tables(length_x, positions(outer)), (total, row_part, col_part))
+    tiles = halved // LANES
+    return flat.reshape(1, kz_count, tiles, 2, LANES).transpose(0, 1, 3, 2, 4).reshape(1, kz_count, 2, halved)
+
+
 def solution(mesh):
     return jax.shard_map(
         shards,

time: 361 us -> 105 us (0.29)
  the two profiles are of different devices: /device:TPU:0 before, /device:TPU:17 now
where the time goes in v1:
time: 105 us
  waiting for transfers between devices  35.9 us (34%)
  Pallas kernels  34.6 us (33%)
  starting transfers between devices  24.5 us (23%)
  local copies, waits for them, and re-layouts  7.53 us (7%)
  between operations  1.72 us (2%)
    ppermute x20, waiting for transfers between devices, exchanged(): lax.ppermute(pieces[d], axis, [(i, i ^ d) for i in range(count)])  34.5 us
    ppermute x20, starting transfers between devices, exchanged(): lax.ppermute(pieces[d], axis, [(i, i ^ d) for i in range(count)])  21.3 us
    pallas_call x2, Pallas kernels, x_transform(): pl.pallas_call(functools.partial(x_kernel, last), in_specs=[pl.BlockSpec(...  13.2 us
    pallas_call x2, Pallas kernels, divergence(): pl.pallas_call(functools.partial(divergence_kernel, tiles, edge is not No...  12.8 us
    pallas_call x2, Pallas kernels, z_transform(): pl.pallas_call(z_kernel, in_specs=[pl.BlockSpec(memory_space=pltpu.SMEM)]...  8.62 us
    unnamed x18, local copies, waits for them, and re-layouts  6.83 us
    ppermute x1, starting transfers between devices, shards(): lax.ppermute(edge, 'xy', [(i, i + 1) for i in range(x_count - 1)])  3.19 us
  transfers between devices with their start and end apart: 21, of which 6 were waited for; matrix products, arithmetic and copies ran while one was open for 1% of the time, Pallas kernels for 19%

profile of v1, /device:TPU:17, one launch (start us, length us, event | category | flops | bytes accessed | tf_op | source)
XLA Modules:
  0.0 105.1 jit_solution(10307745032798100707)
XLA Ops:
  0.8 1.6 %copy-done = bf16[8,256,512]{2,1,0:T(8,128)(2,1)S(1)} copy-done((bf16[8,256,512]{2,1,0:T(8,128)(2,1)S(1)}, bf16[8,256,512]{2,1,0:T(8,128)(2,1)}, u32[]{:S(2)}) %copy-start) | copy-done | bytes 2097176
  2.4 1.6 %copy-done.1 = bf16[8,256,512]{2,1,0:T(8,128)(2,1)S(1)} copy-done((bf16[8,256,512]{2,1,0:T(8,128)(2,1)S(1)}, bf16[8,256,512]{2,1,0:T(8,128)(2,1)}, u32[]{:S(2)}) %copy-start.1) | copy-done | bytes 2097176
  4.0 1.6 %copy-done.2 = bf16[8,256,512]{2,1,0:T(8,128)(2,1)S(1)} copy-done((bf16[8,256,512]{2,1,0:T(8,128)(2,1)S(1)}, bf16[8,256,512]{2,1,0:T(8,128)(2,1)}, u32[]{:S(2)}) %copy-start.2) | copy-done | bytes 2097176
  5.6 6.6 %divergence.2 = (s16[272,256]{1,0:T(8,128)(2,1)S(1)}, s16[272,256]{1,0:T(8,128)(2,1)S(1)}, s16[272,256]{1,0:T(8,128)(2,1)S(1)}, s16[272,256]{1,0:T(8,128)(2,1)S(...) custom-call(s32[4]{0:T(128)S(1)} %pad_add_fusion.refs_0_.place, ...), custom_call_target="tpu_custom_call" | custom-call | flops 536870912 | bytes 4194304 | tf_op jit(solution)/shard_map/divergence/pallas_call | solution.py:278
  15.8 3.2 %collective-permute-start = (f32[8,256]{1,0:T(8,128)S(1)}, f32[8,256]{1,0:T(8,128)S(1)}, u32[]{:S(2)}, u32[]{:S(2)}) collective-permute-start(f32[8,256]{1,0:T(8,128)S(1)} %get-tuple-element.30), channel_id=1, source_target_pairs={{0,1},{1,2},{2,3},{4,5},{5,6},{6,7},{8,9},{9,10},{10,11},{12,13},{... | collective-permute-start | bytes 24584 | tf_op jit(solution)/shard_map/ppermute | solution.py:511
  19.0 1.5 %collective-permute-done.refs_5_ = f32[8,256]{1,0:T(8,128)S(1)} collective-permute-done((f32[8,256]{1,0:T(8,128)S(1)}, f32[8,256]{1,0:T(8,128)S(1)}, u32[]{:S(2)}, u32[]{:S(2)}) %collective-permute-start) | collective-permute-done | bytes 8224 | tf_op jit(solution)/shard_map/ppermute | solution.py:511
  20.5 1.4 %collective-permute-start.15 = (s16[272,256]{1,0:T(8,128)(2,1)S(1)}, s16[272,256]{1,0:T(8,128)(2,1)S(1)}, u32[]{:S(2)}, u32[]{:S(2)}) collective-permute-start(s16[272,256]{1,0:T(8,128)(2,1)S(1)} %get-tuple-element.48), channel_id=1, source_target_pairs={{0,20},{4,16},{8,28},{12,24},{16,4},{20,0},{24,12},{28,8},{1,21},{... | collective-permute-start | bytes 417800 | tf_op jit(solution)/shard_map/ppermute | solution.py:491
  21.9 6.2 %divergence.3 = (s16[272,256]{1,0:T(8,128)(2,1)S(1)}, s16[272,256]{1,0:T(8,128)(2,1)S(1)}, s16[272,256]{1,0:T(8,128)(2,1)S(1)}, s16[272,256]{1,0:T(8,128)(2,1)S(...) custom-call(s32[4]{0:T(128)S(1)} %pad_add_fusion.refs_0_.place, ...), custom_call_target="tpu_custom_call" | custom-call | flops 536870912 | bytes 4194304 | tf_op jit(solution)/shard_map/divergence/pallas_call | solution.py:278
  28.1 2.2 %collective-permute-start.16 = (s16[272,256]{1,0:T(8,128)(2,1)S(1)}, s16[272,256]{1,0:T(8,128)(2,1)S(1)}, u32[]{:S(2)}, u32[]{:S(2)}) collective-permute-start(s16[272,256]{1,0:T(8,128)(2,1)S(1)} %get-tuple-element.49), channel_id=1, source_target_pairs={{0,24},{4,28},{8,16},{12,20},{16,8},{20,12},{24,0},{28,4},{1,25},{... | collective-permute-start | bytes 417800 | tf_op jit(solution)/shard_map/ppermute | solution.py:491
  32.7 1.8 %collective-permute-done.16.refs_6_ = s16[272,256]{1,0:T(8,128)(2,1)S(1)} collective-permute-done((s16[272,256]{1,0:T(8,128)(2,1)S(1)}, s16[272,256]{1,0:T(8,128)(2,1)S(1)}, u32[]{:S(2)}, u32[]{:S(2)}) %collective-permute-start.16) | collective-permute-done | bytes 139296 | tf_op jit(solution)/shard_map/ppermute | solution.py:491
  35.7 2.0 %collective-permute-done.17.refs_7_ = s16[272,256]{1,0:T(8,128)(2,1)S(1)} collective-permute-done((s16[272,256]{1,0:T(8,128)(2,1)S(1)}, s16[272,256]{1,0:T(8,128)(2,1)S(1)}, u32[]{:S(2)}, u32[]{:S(2)}) %collective-permute-start.17) | collective-permute-done | bytes 139296 | tf_op jit(solution)/shard_map/ppermute | solution.py:491
  37.7 1.6 %collective-permute-start.5 = (s16[272,256]{1,0:T(8,128)(2,1)S(1)}, s16[272,256]{1,0:T(8,128)(2,1)S(1)}, u32[]{:S(2)}, u32[]{:S(2)}) collective-permute-start(s16[272,256]{1,0:T(8,128)(2,1)S(1)} %get-tuple-element.36), channel_id=1, source_target_pairs={{0,20},{4,16},{8,28},{12,24},{16,4},{20,0},{24,12},{28,8},{1,21},{... | collective-permute-start | bytes 417800 | tf_op jit(solution)/shard_map/ppermute | solution.py:491
  40.8 1.7 %collective-permute-start.7 = (s16[272,256]{1,0:T(8,128)(2,1)S(1)}, s16[272,256]{1,0:T(8,128)(2,1)S(1)}, u32[]{:S(2)}, u32[]{:S(2)}) collective-permute-start(s16[272,256]{1,0:T(8,128)(2,1)S(1)} %get-tuple-element.38), channel_id=1, source_target_pairs={{0,28},{4,24},{8,20},{12,16},{16,12},{20,8},{24,4},{28,0},{1,29},{... | collective-permute-start | bytes 417800 | tf_op jit(solution)/shard_map/ppermute | solution.py:491
  42.4 4.2 %z_transform.3 = (s16[528,256]{1,0:T(8,128)(2,1)S(1)}, s16[528,256]{1,0:T(8,128)(2,1)S(1)}, s16[528,256]{1,0:T(8,128)(2,1)S(1)}, s16[528,256]{1,0:T(8,128)(2,1)S(1)}) custom-call(s32[4]{0:T(128)S(1)} %pad_add_fusion.refs_0_.place, s16[272,256]{1,0:T(8,128)(2,1)S(1)} %get-tuple-element.43.refs_0_, s16[272,256]{1,0:T(8,128)(2,1)S(1)} %collective-permute-done.11.refs_1_, ...), custom_call_target="tpu_custom_call" | custom-call | flops 1610612736 | bytes 4194304 | tf_op jit(solution)/shard_map/z_transform/pallas_call | solution.py:386
  46.7 1.4 %collective-permute-start.18 = (s16[528,256]{1,0:T(8,128)(2,1)S(1)}, s16[528,256]{1,0:T(8,128)(2,1)S(1)}, u32[]{:S(2)}, u32[]{:S(2)}) collective-permute-start(s16[528,256]{1,0:T(8,128)(2,1)S(1)} %get-tuple-element.52), channel_id=1, source_target_pairs={{0,1},{1,0},{2,3},{3,2},{4,5},{5,4},{6,7},{7,6},{8,9},{9,8},{10,11... | collective-permute-start | bytes 811016 | tf_op jit(solution)/shard_map/ppermute | solution.py:491
  48.1 1.3 %collective-permute-start.20 = (s16[528,256]{1,0:T(8,128)(2,1)S(1)}, s16[528,256]{1,0:T(8,128)(2,1)S(1)}, u32[]{:S(2)}, u32[]{:S(2)}) collective-permute-start(s16[528,256]{1,0:T(8,128)(2,1)S(1)} %get-tuple-element.54), channel_id=1, source_target_pairs={{0,3},{1,2},{2,1},{3,0},{4,7},{5,6},{6,5},{7,4},{8,11},{9,10},{10,... | collective-permute-start | bytes 811016 | tf_op jit(solution)/shard_map/ppermute | solution.py:491
  51.7 2.0 %copy-done.7 = bf16[2,7,256,512]{3,2,1,0:T(8,128)(2,1)S(1)} copy-done((bf16[2,7,256,512]{3,2,1,0:T(8,128)(2,1)S(1)}, bf16[2,7,256,512]{3,2,1,0:T(8,128)(2,1)}, u32[]{:S(2)}) %copy-start.7) | copy-done | bytes 3670040
  53.7 4.4 %z_transform.2 = (s16[528,256]{1,0:T(8,128)(2,1)S(1)}, s16[528,256]{1,0:T(8,128)(2,1)S(1)}, s16[528,256]{1,0:T(8,128)(2,1)S(1)}, s16[528,256]{1,0:T(8,128)(2,1)S(1)}) custom-call(s32[4]{0:T(128)S(1)} %pad_add_fusion.refs_0_.place, s16[272,256]{1,0:T(8,128)(2,1)S(1)} %get-tuple-element.31.refs_0_, s16[272,256]{1,0:T(8,128)(2,1)S(1)} %collective-permute-done.1.refs_1_, ...), custom_call_target="tpu_custom_call" | custom-call | flops 1610612736 | bytes 4194304 | tf_op jit(solution)/shard_map/z_transform/pallas_call | solution.py:386
  58.1 2.3 %collective-permute-start.8 = (s16[528,256]{1,0:T(8,128)(2,1)S(1)}, s16[528,256]{1,0:T(8,128)(2,1)S(1)}, u32[]{:S(2)}, u32[]{:S(2)}) collective-permute-start(s16[528,256]{1,0:T(8,128)(2,1)S(1)} %get-tuple-element.40), channel_id=1, source_target_pairs={{0,1},{1,0},{2,3},{3,2},{4,5},{5,4},{6,7},{7,6},{8,9},{9,8},{10,11... | collective-permute-start | bytes 811016 | tf_op jit(solution)/shard_map/ppermute | solution.py:491
  60.4 1.3 %collective-permute-start.10 = (s16[528,256]{1,0:T(8,128)(2,1)S(1)}, s16[528,256]{1,0:T(8,128)(2,1)S(1)}, u32[]{:S(2)}, u32[]{:S(2)}) collective-permute-start(s16[528,256]{1,0:T(8,128)(2,1)S(1)} %get-tuple-element.42), channel_id=1, source_target_pairs={{0,3},{1,2},{2,1},{3,0},{4,7},{5,6},{6,5},{7,4},{8,11},{9,10},{10,... | collective-permute-start | bytes 811016 | tf_op jit(solution)/shard_map/ppermute | solution.py:491
  61.6 23.6 %collective-permute-done.20.refs_4_ = s16[528,256]{1,0:T(8,128)(2,1)S(1)} collective-permute-done((s16[528,256]{1,0:T(8,128)(2,1)S(1)}, s16[528,256]{1,0:T(8,128)(2,1)S(1)}, u32[]{:S(2)}, u32[]{:S(2)}) %collective-permute-start.20) | collective-permute-done | bytes 270368 | tf_op jit(solution)/shard_map/ppermute | solution.py:491
  85.2 5.1 %x_transform.2.refs_6_ = f32[2,512,1024]{2,1,0:T(8,128)S(1)} custom-call(s32[4]{0:T(128)S(1)} %pad_add_fusion.refs_0_.place, s16[528,256]{1,0:T(8,128)(2,1)S(1)} %get-tuple-element.51.refs_1_, s16[528,256]{1,0:T(8,128)(2,1)S(1)} %collective-permute-done.18.refs_2_, s16[528,256]{1,0:T(8,128)(2,1)S(1)} %collective-permute-done.19.refs_3_, ...), custom_call_target="tpu_custom_call" | custom-call | flops 3221225472 | bytes 8388608 | tf_op jit(solution)/shard_map/x_transform/pallas_call | solution.py:469
  90.4 6.5 %collective-permute-done.10.refs_4_ = s16[528,256]{1,0:T(8,128)(2,1)S(1)} collective-permute-done((s16[528,256]{1,0:T(8,128)(2,1)S(1)}, s16[528,256]{1,0:T(8,128)(2,1)S(1)}, u32[]{:S(2)}, u32[]{:S(2)}) %collective-permute-start.10) | collective-permute-done | bytes 270368 | tf_op jit(solution)/shard_map/ppermute | solution.py:491
  97.0 8.1 %x_transform.3 = f32[8192,128]{1,0:T(8,128)} custom-call(s32[4]{0:T(128)S(1)} %pad_add_fusion.refs_0_.place, s16[528,256]{1,0:T(8,128)(2,1)S(1)} %get-tuple-element.39.refs_1_, s16[528,256]{1,0:T(8,128)(2,1)S(1)} %collective-permute-done.8.refs_2_, s16[528,256]{1,0:T(8,128)(2,1)S(1)} %collective-permute-done.9.refs_3_, ...), custom_call_target="tpu_custom_call" | custom-call | flops 3221225472 | bytes 8388608 | tf_op jit(solution)/shard_map/x_transform/pallas_call | solution.py:469
  (47 shorter events, 10.4 us)
Async XLA Ops:
  12.2 30.3 %copy-start.6 = (bf16[2,7,256,512]{3,2,1,0:T(8,128)(2,1)S(1)}, bf16[2,7,256,512]{3,2,1,0:T(8,128)(2,1)}, u32[]{:S(2)}) copy-start(bf16[2,7,256,512]{3,2,1,0:T(8,128)(2,1)} %constant.38.clone.refs_8_) | copy-start | bytes 11010052
  12.2 30.3 %copy-start.8 = (bf16[2,2,128,256]{3,2,1,0:T(8,128)(2,1)S(1)}, bf16[2,2,128,256]{3,2,1,0:T(8,128)(2,1)}, u32[]{:S(2)}) copy-start(bf16[2,2,128,256]{3,2,1,0:T(8,128)(2,1)} %constant.39.clone.refs_9_) | copy-start | bytes 786436
  12.2 15.9 %collective-permute-start.11 = (s16[272,256]{1,0:T(8,128)(2,1)S(1)}, s16[272,256]{1,0:T(8,128)(2,1)S(1)}, u32[]{:S(2)}, u32[]{:S(2)}) collective-permute-start(s16[272,256]{1,0:T(8,128)(2,1)S(1)} %get-tuple-element.44), channel_id=1, source_target_pairs={{0,4},{4,0},{8,12},{12,8},{16,20},{20,16},{24,28},{28,24},{1,5},{5... | collective-permute-start | bytes 417800 | tf_op jit(solution)/shard_map/ppermute | solution.py:491
  12.9 17.4 %collective-permute-start.12 = (s16[272,256]{1,0:T(8,128)(2,1)S(1)}, s16[272,256]{1,0:T(8,128)(2,1)S(1)}, u32[]{:S(2)}, u32[]{:S(2)}) collective-permute-start(s16[272,256]{1,0:T(8,128)(2,1)S(1)} %get-tuple-element.45), channel_id=1, source_target_pairs={{0,8},{4,12},{8,0},{12,4},{16,24},{20,28},{24,16},{28,20},{1,9},{5... | collective-permute-start | bytes 417800 | tf_op jit(solution)/shard_map/ppermute | solution.py:491
  14.1 16.5 %collective-permute-start.13 = (s16[272,256]{1,0:T(8,128)(2,1)S(1)}, s16[272,256]{1,0:T(8,128)(2,1)S(1)}, u32[]{:S(2)}, u32[]{:S(2)}) collective-permute-start(s16[272,256]{1,0:T(8,128)(2,1)S(1)} %get-tuple-element.46), channel_id=1, source_target_pairs={{0,12},{4,8},{8,4},{12,0},{16,28},{20,24},{24,20},{28,16},{1,13},{... | collective-permute-start | bytes 417800 | tf_op jit(solution)/shard_map/ppermute | solution.py:491
  14.6 16.3 %collective-permute-start.14 = (s16[272,256]{1,0:T(8,128)(2,1)S(1)}, s16[272,256]{1,0:T(8,128)(2,1)S(1)}, u32[]{:S(2)}, u32[]{:S(2)}) collective-permute-start(s16[272,256]{1,0:T(8,128)(2,1)S(1)} %get-tuple-element.47), channel_id=1, source_target_pairs={{0,16},{4,20},{8,24},{12,28},{16,0},{20,4},{24,8},{28,12},{1,17},{... | collective-permute-start | bytes 417800 | tf_op jit(solution)/shard_map/ppermute | solution.py:491
  15.8 4.7 %collective-permute-start = (f32[8,256]{1,0:T(8,128)S(1)}, f32[8,256]{1,0:T(8,128)S(1)}, u32[]{:S(2)}, u32[]{:S(2)}) collective-permute-start(f32[8,256]{1,0:T(8,128)S(1)} %get-tuple-element.30), channel_id=1, source_target_pairs={{0,1},{1,2},{2,3},{4,5},{5,6},{6,7},{8,9},{9,10},{10,11},{12,13},{... | collective-permute-start | bytes 24584 | tf_op jit(solution)/shard_map/ppermute | solution.py:511
  20.5 11.6 %collective-permute-start.15 = (s16[272,256]{1,0:T(8,128)(2,1)S(1)}, s16[272,256]{1,0:T(8,128)(2,1)S(1)}, u32[]{:S(2)}, u32[]{:S(2)}) collective-permute-start(s16[272,256]{1,0:T(8,128)(2,1)S(1)} %get-tuple-element.48), channel_id=1, source_target_pairs={{0,20},{4,16},{8,28},{12,24},{16,4},{20,0},{24,12},{28,8},{1,21},{... | collective-permute-start | bytes 417800 | tf_op jit(solution)/shard_map/ppermute | solution.py:491
  28.1 6.4 %collective-permute-start.16 = (s16[272,256]{1,0:T(8,128)(2,1)S(1)}, s16[272,256]{1,0:T(8,128)(2,1)S(1)}, u32[]{:S(2)}, u32[]{:S(2)}) collective-permute-start(s16[272,256]{1,0:T(8,128)(2,1)S(1)} %get-tuple-element.49), channel_id=1, source_target_pairs={{0,24},{4,28},{8,16},{12,20},{16,8},{20,12},{24,0},{28,4},{1,25},{... | collective-permute-start | bytes 417800 | tf_op jit(solution)/shard_map/ppermute | solution.py:491
  30.3 7.4 %collective-permute-start.17 = (s16[272,256]{1,0:T(8,128)(2,1)S(1)}, s16[272,256]{1,0:T(8,128)(2,1)S(1)}, u32[]{:S(2)}, u32[]{:S(2)}) collective-permute-start(s16[272,256]{1,0:T(8,128)(2,1)S(1)} %get-tuple-element.50), channel_id=1, source_target_pairs={{0,28},{4,24},{8,20},{12,16},{16,12},{20,8},{24,4},{28,0},{1,29},{... | collective-permute-start | bytes 417800 | tf_op jit(solution)/shard_map/ppermute | solution.py:491
  30.6 8.7 %collective-permute-start.1 = (s16[272,256]{1,0:T(8,128)(2,1)S(1)}, s16[272,256]{1,0:T(8,128)(2,1)S(1)}, u32[]{:S(2)}, u32[]{:S(2)}) collective-permute-start(s16[272,256]{1,0:T(8,128)(2,1)S(1)} %get-tuple-element.32), channel_id=1, source_target_pairs={{0,4},{4,0},{8,12},{12,8},{16,20},{20,16},{24,28},{28,24},{1,5},{5... | collective-permute-start | bytes 417800 | tf_op jit(solution)/shard_map/ppermute | solution.py:491
  30.9 9.8 %collective-permute-start.2 = (s16[272,256]{1,0:T(8,128)(2,1)S(1)}, s16[272,256]{1,0:T(8,128)(2,1)S(1)}, u32[]{:S(2)}, u32[]{:S(2)}) collective-permute-start(s16[272,256]{1,0:T(8,128)(2,1)S(1)} %get-tuple-element.33), channel_id=1, source_target_pairs={{0,8},{4,12},{8,0},{12,4},{16,24},{20,28},{24,16},{28,20},{1,9},{5... | collective-permute-start | bytes 417800 | tf_op jit(solution)/shard_map/ppermute | solution.py:491
  32.1 14.6 %collective-permute-start.3 = (s16[272,256]{1,0:T(8,128)(2,1)S(1)}, s16[272,256]{1,0:T(8,128)(2,1)S(1)}, u32[]{:S(2)}, u32[]{:S(2)}) collective-permute-start(s16[272,256]{1,0:T(8,128)(2,1)S(1)} %get-tuple-element.34), channel_id=1, source_target_pairs={{0,12},{4,8},{8,4},{12,0},{16,28},{20,24},{24,20},{28,16},{1,13},{... | collective-permute-start | bytes 417800 | tf_op jit(solution)/shard_map/ppermute | solution.py:491
  34.5 13.6 %collective-permute-start.4 = (s16[272,256]{1,0:T(8,128)(2,1)S(1)}, s16[272,256]{1,0:T(8,128)(2,1)S(1)}, u32[]{:S(2)}, u32[]{:S(2)}) collective-permute-start(s16[272,256]{1,0:T(8,128)(2,1)S(1)} %get-tuple-element.35), channel_id=1, source_target_pairs={{0,16},{4,20},{8,24},{12,28},{16,0},{20,4},{24,8},{28,12},{1,17},{... | collective-permute-start | bytes 417800 | tf_op jit(solution)/shard_map/ppermute | solution.py:491
  37.7 10.4 %collective-permute-start.5 = (s16[272,256]{1,0:T(8,128)(2,1)S(1)}, s16[272,256]{1,0:T(8,128)(2,1)S(1)}, u32[]{:S(2)}, u32[]{:S(2)}) collective-permute-start(s16[272,256]{1,0:T(8,128)(2,1)S(1)} %get-tuple-element.36), channel_id=1, source_target_pairs={{0,20},{4,16},{8,28},{12,24},{16,4},{20,0},{24,12},{28,8},{1,21},{... | collective-permute-start | bytes 417800 | tf_op jit(solution)/shard_map/ppermute | solution.py:491
  39.2 12.4 %collective-permute-start.6 = (s16[272,256]{1,0:T(8,128)(2,1)S(1)}, s16[272,256]{1,0:T(8,128)(2,1)S(1)}, u32[]{:S(2)}, u32[]{:S(2)}) collective-permute-start(s16[272,256]{1,0:T(8,128)(2,1)S(1)} %get-tuple-element.37), channel_id=1, source_target_pairs={{0,24},{4,28},{8,16},{12,20},{16,8},{20,12},{24,0},{28,4},{1,25},{... | collective-permute-start | bytes 417800 | tf_op jit(solution)/shard_map/ppermute | solution.py:491
  40.8 10.9 %collective-permute-start.7 = (s16[272,256]{1,0:T(8,128)(2,1)S(1)}, s16[272,256]{1,0:T(8,128)(2,1)S(1)}, u32[]{:S(2)}, u32[]{:S(2)}) collective-permute-start(s16[272,256]{1,0:T(8,128)(2,1)S(1)} %get-tuple-element.38), channel_id=1, source_target_pairs={{0,28},{4,24},{8,20},{12,16},{16,12},{20,8},{24,4},{28,0},{1,29},{... | collective-permute-start | bytes 417800 | tf_op jit(solution)/shard_map/ppermute | solution.py:491
  46.7 13.7 %collective-permute-start.18 = (s16[528,256]{1,0:T(8,128)(2,1)S(1)}, s16[528,256]{1,0:T(8,128)(2,1)S(1)}, u32[]{:S(2)}, u32[]{:S(2)}) collective-permute-start(s16[528,256]{1,0:T(8,128)(2,1)S(1)} %get-tuple-element.52), channel_id=1, source_target_pairs={{0,1},{1,0},{2,3},{3,2},{4,5},{5,4},{6,7},{7,6},{8,9},{9,8},{10,11... | collective-permute-start | bytes 811016 | tf_op jit(solution)/shard_map/ppermute | solution.py:491
  48.0 13.6 %collective-permute-start.19 = (s16[528,256]{1,0:T(8,128)(2,1)S(1)}, s16[528,256]{1,0:T(8,128)(2,1)S(1)}, u32[]{:S(2)}, u32[]{:S(2)}) collective-permute-start(s16[528,256]{1,0:T(8,128)(2,1)S(1)} %get-tuple-element.53), channel_id=1, source_target_pairs={{0,2},{1,3},{2,0},{3,1},{4,6},{5,7},{6,4},{7,5},{8,10},{9,11},{10,... | collective-permute-start | bytes 811016 | tf_op jit(solution)/shard_map/ppermute | solution.py:491
  48.1 37.1 %collective-permute-start.20 = (s16[528,256]{1,0:T(8,128)(2,1)S(1)}, s16[528,256]{1,0:T(8,128)(2,1)S(1)}, u32[]{:S(2)}, u32[]{:S(2)}) collective-permute-start(s16[528,256]{1,0:T(8,128)(2,1)S(1)} %get-tuple-element.54), channel_id=1, source_target_pairs={{0,3},{1,2},{2,1},{3,0},{4,7},{5,6},{6,5},{7,4},{8,11},{9,10},{10,... | collective-permute-start | bytes 811016 | tf_op jit(solution)/shard_map/ppermute | solution.py:491
  49.4 35.8 %copy-start.5 = (bf16[2,2,512,1024]{3,2,1,0:T(8,128)(2,1)S(1)}, bf16[2,2,512,1024]{3,2,1,0:T(8,128)(2,1)}, u32[]{:S(2)}) copy-start(bf16[2,2,512,1024]{3,2,1,0:T(8,128)(2,1)} %constant.40.clone.refs_5_) | copy-start | bytes 12582916
  58.1 32.2 %collective-permute-start.8 = (s16[528,256]{1,0:T(8,128)(2,1)S(1)}, s16[528,256]{1,0:T(8,128)(2,1)S(1)}, u32[]{:S(2)}, u32[]{:S(2)}) collective-permute-start(s16[528,256]{1,0:T(8,128)(2,1)S(1)} %get-tuple-element.40), channel_id=1, source_target_pairs={{0,1},{1,0},{2,3},{3,2},{4,5},{5,4},{6,7},{7,6},{8,9},{9,8},{10,11... | collective-permute-start | bytes 811016 | tf_op jit(solution)/shard_map/ppermute | solution.py:491
  60.4 30.0 %collective-permute-start.9 = (s16[528,256]{1,0:T(8,128)(2,1)S(1)}, s16[528,256]{1,0:T(8,128)(2,1)S(1)}, u32[]{:S(2)}, u32[]{:S(2)}) collective-permute-start(s16[528,256]{1,0:T(8,128)(2,1)S(1)} %get-tuple-element.41), channel_id=1, source_target_pairs={{0,2},{1,3},{2,0},{3,1},{4,6},{5,7},{6,4},{7,5},{8,10},{9,11},{10,... | collective-permute-start | bytes 811016 | tf_op jit(solution)/shard_map/ppermute | solution.py:491
  60.4 36.5 %collective-permute-start.10 = (s16[528,256]{1,0:T(8,128)(2,1)S(1)}, s16[528,256]{1,0:T(8,128)(2,1)S(1)}, u32[]{:S(2)}, u32[]{:S(2)}) collective-permute-start(s16[528,256]{1,0:T(8,128)(2,1)S(1)} %get-tuple-element.42), channel_id=1, source_target_pairs={{0,3},{1,2},{2,1},{3,0},{4,7},{5,6},{6,5},{7,4},{8,11},{9,10},{10,... | collective-permute-start | bytes 811016 | tf_op jit(solution)/shard_map/ppermute | solution.py:491
  (6 other events, 30.3 us)

commit v2 on v0

--- a/solution.py
+++ b/solution.py
@@ -1,8 +1,12 @@
+import functools
 import math
 
 import jax
 import jax.numpy as jnp
+import numpy as np
 from jax import lax
+from jax.experimental import pallas as pl
+from jax.experimental.pallas import tpu as pltpu
 from jax.sharding import PartitionSpec as P
 
 NX = 2048
@@ -76,7 +80,7 @@
     return 4.0 * sine * sine
 
 
-def shards(flux_xface, flux_yspec, flux_zface, frequency_y):
+def plain_shards(flux_xface, flux_yspec, flux_zface, frequency_y):
     x_rank = lax.axis_index("xy")
     x_count = lax.axis_size("xy")
     z_rank = lax.axis_index("gz")
@@ -122,6 +126,502 @@
     return -spectrum / denominator
 
 
+LANES = 128
+GROUP = 32
+META = 16
+STEPS = 64.0
+TOP = 32700.0
+BLOCKS = 8
+RESIDUES = 2 * BLOCKS
+CUT = 6
+SCOPED = 13 << 20
+
+
+def split_bf16(table):
+    high = table.astype(jnp.bfloat16)
+    low = (table - high.astype(np.float64)).astype(jnp.bfloat16)
+    return np.stack([high, low])
+
+
+def scaled_cosine(frequency, position, length, wave=np.cos):
+    phase = (frequency[:, None] * (2 * position[None, :] + 1)) % (4 * length)
+    scaling = np.where(frequency == 0, math.sqrt(1.0 / length), math.sqrt(2.0 / length))
+    return scaling[:, None] * wave(phase * (math.pi / (2 * length)))
+
+
+def z_tables(length):
+    inner = np.arange(length // BLOCKS)
+    outer = RESIDUES * np.arange(length // RESIDUES)
+    pairs = []
+    for r in range(1, BLOCKS):
+        upper = [scaled_cosine(outer + r, inner, length), -scaled_cosine(outer + r, inner, length, np.sin)]
+        mirror = outer + RESIDUES - r
+        lower = [scaled_cosine(mirror, inner, length), scaled_cosine(mirror, inner, length, np.sin)]
+        pairs.append(np.concatenate([np.concatenate(upper, axis=1), np.concatenate(lower, axis=1)], axis=0))
+    ends = [scaled_cosine(outer, inner, length), scaled_cosine(outer + BLOCKS, inner, length)]
+    return split_bf16(np.stack(pairs)), split_bf16(np.stack(ends))
+
+
+def x_tables(length, ranks, width, tiles):
+    halved = length // 2
+    lanes = np.arange(LANES)
+    tables = []
+    for p in (0, 1):
+        positions = [np.concatenate([j * width + t * LANES + lanes for t in tiles]) for j in range(ranks)]
+        tables.append(np.stack([scaled_cosine(2 * np.arange(halved) + p, at, length).T for at in positions]))
+    return split_bf16(np.stack(tables))
+
+
+def lasting(microseconds):
+    return pl.CostEstimate(flops=0, bytes_accessed=int(microseconds * 3.69e6), transcendentals=0)
+
+
+def steps_of(largest):
+    return jnp.ceil(jnp.log2(jnp.maximum(largest, 2.0**-100)) * STEPS)
+
+
+def encoded(values, extra=None):
+    largest = jnp.max(jnp.abs(values), axis=1)
+    if extra is not None:
+        largest = jnp.maximum(largest, extra)
+    steps = steps_of(largest)
+    factor = TOP * jnp.exp2(steps * (-1.0 / STEPS))
+    return jnp.round(values * factor[:, None, :]).astype(jnp.int32), steps, factor
+
+
+def decoded(codes, steps):
+    scale = jnp.exp2(steps * (1.0 / STEPS)) * (1.0 / TOP)
+    groups = steps.shape[0]
+    values = codes.astype(jnp.int32).astype(jnp.float32).reshape(groups, GROUP, codes.shape[-1])
+    return values * scale[:, None, :], scale
+
+
+def divergence_kernel(tiles, spans, order, has_edge, place, frequency_in, flux_x, flux_y, flux_z, *refs):
+    held_x, held_y, held_z, arrived, frequency, frequency_arrived = refs[-6:]
+    if len(refs) - 6 < len(order):
+        outs = [refs[i // 2].at[i % 2] for i in range(len(order))]
+    else:
+        outs = refs[: len(order)]
+    z_rank, z_count, x_rank, x_count = place[0], place[1], place[2], place[3]
+    rows, width = flux_x.shape[1], flux_x.shape[2]
+    last_tile = width // LANES - 1
+    reverse = x_rank >= x_count // 2
+    frequency_copy = pltpu.make_async_copy(frequency_in, frequency, frequency_arrived)
+    frequency_copy.start()
+    copies = []
+    for i, d in enumerate(order):
+        y = z_rank ^ d
+        for n, (flux, held, (start, stop)) in enumerate(
+            ((flux_x, held_x, spans[0]), (flux_y, held_y, spans[1]), (flux_z, held_z, spans[1]))
+        ):
+            copies.append(pltpu.make_async_copy(flux.at[y, :, start:stop], held.at[i], arrived.at[i, n]))
+            copies[-1].start()
+    row_at = lax.broadcasted_iota(jnp.int32, (LANES, LANES), 0)
+    col_at = lax.broadcasted_iota(jnp.int32, (LANES, LANES), 1)
+    col_at = jnp.where(reverse, LANES - 1 - col_at, col_at)
+    take = (row_at == col_at).astype(jnp.float32)
+    below = (row_at + 1 == col_at).astype(jnp.float32)
+    keep = jnp.where((x_rank == x_count - 1) & (row_at == LANES - 1), 0.0, take)
+    pick = take.astype(jnp.bfloat16)
+    change = (take - below).astype(jnp.bfloat16)
+    change_last = (keep - below).astype(jnp.bfloat16)
+    wrap = -((row_at == LANES - 1) & (col_at == 0)).astype(jnp.float32)
+    wrap = wrap.astype(jnp.bfloat16)
+    dot = functools.partial(jnp.dot, preferred_element_type=jnp.float32)
+    groups = rows // GROUP
+    z_last = jnp.where(z_rank == z_count - 1, rows - 1, rows)
+    row_id = lax.broadcasted_iota(jnp.int32, (rows, LANES), 0)
+    at_end = lax.broadcasted_iota(jnp.int32, (groups, LANES), 0) == groups - 1
+    frequency_copy.wait()
+    for i, d in enumerate(order):
+        y = z_rank ^ d
+        angle = jnp.full((8, LANES), frequency[y], jnp.int32).astype(jnp.float32) * (math.pi / (2 * NY))
+        weight = (2.0 * jnp.sin(angle))[:1]
+        for n in range(3):
+            copies[3 * i + n].wait()
+        metas = []
+        for at, tile in enumerate(tiles):
+            lanes = slice(tile * LANES - spans[1][0], (tile + 1) * LANES - spans[1][0])
+            x_lanes = slice(tile * LANES - spans[0][0], (tile + 1) * LANES - spans[0][0])
+            value = dot(held_x[i, :, x_lanes], change_last if tile == last_tile else change)
+            if tile > 0:
+                value += dot(held_x[i, :, x_lanes.start - LANES : x_lanes.start], wrap)
+            value += weight * dot(held_y[i, :, lanes], pick)
+            face = jnp.where(row_id == z_last, 0.0, dot(held_z[i, :, lanes], pick))
+            value += face - jnp.where(row_id == 0, 0.0, pltpu.roll(face, 1, 0))
+            halo = -face[rows - 1 :]
+            extra = jnp.where(at_end, jnp.abs(halo), 0.0)
+            codes, steps, factor = encoded(value.reshape(groups, GROUP, LANES), extra)
+            halo_code = jnp.round(halo * factor[groups - 1 :])
+            metas.append(jnp.concatenate([steps, halo_code], axis=0))
+            spot = pl.ds(pl.multiple_of(jnp.where(reverse, len(tiles) - 1 - at, at) * LANES, LANES), LANES)
+            outs[i][:rows, spot] = codes.reshape(rows, LANES).astype(jnp.int16)
+        meta = jnp.where(reverse, jnp.concatenate(metas[::-1], axis=1), jnp.concatenate(metas, axis=1))
+        filled = [meta]
+        if has_edge:
+            ending = lax.broadcasted_iota(jnp.int32, (8, LANES), 1) == LANES - 1
+            face = lax.dot_general(
+                ending.astype(jnp.bfloat16),
+                held_x[i, :, (last_tile * LANES - spans[0][0]) :],
+                (((1,), (1,)), ((), ())),
+                preferred_element_type=jnp.float32,
+            )[:1]
+            edge_steps = steps_of(jnp.abs(face))
+            filled += [jnp.round(face * (TOP * jnp.exp2(edge_steps * (-1.0 / STEPS)))), edge_steps]
+        filler = META - groups - len(filled)
+        filled.append(jnp.zeros((filler, meta.shape[1]), jnp.float32))
+        outs[i][rows:, :] = jnp.concatenate(filled, axis=0).astype(jnp.int32).astype(jnp.int16)
+
+
+def divergence(tiles, spans, order, place, frequency, fluxes, has_edge, paired=False):
+    y_count, rows, width = fluxes[0].shape
+    chunk = len(tiles) * LANES
+    vmem = pl.BlockSpec(memory_space=pltpu.VMEM)
+    operands = [pltpu.with_memory_space_constraint(a, pltpu.HBM) for a in (frequency, *fluxes)]
+    widths = [stop - start for start, stop in (spans[0], spans[1], spans[1])]
+    scratch = [pltpu.VMEM((len(order), rows, w), jnp.bfloat16) for w in widths]
+    scratch += [pltpu.SemaphoreType.DMA((len(order), 3)), pltpu.SMEM((y_count,), jnp.int32), pltpu.SemaphoreType.DMA]
+    return pl.pallas_call(
+        functools.partial(divergence_kernel, tiles, spans, order, has_edge),
+        in_specs=[pl.BlockSpec(memory_space=pltpu.SMEM)] + [pl.BlockSpec(memory_space=pltpu.HBM)] * 4,
+        out_specs=[vmem] * (len(order) // 2 if paired else len(order)),
+        out_shape=[jax.ShapeDtypeStruct((2, rows + META, chunk), jnp.int16)] * (len(order) // 2)
+        if paired
+        else [jax.ShapeDtypeStruct((rows + META, chunk), jnp.int16)] * len(order),
+        scratch_shapes=scratch,
+        compiler_params=pltpu.CompilerParams(vmem_limit_bytes=SCOPED),
+        cost_estimate=lasting(1.2 + 0.5 * len(order)),
+        name="divergence",
+    )(place, *operands)
+
+
+def part_of(message, row, cut):
+    if not isinstance(message, tuple):
+        return message, row
+    return (message[0], row) if row < cut else (message[1], row - cut)
+
+
+def z_kernel(gives_edge, place, *refs):
+    if gives_edge:
+        pieces, refs = refs[:BLOCKS], refs[BLOCKS:]
+    else:
+        half = BLOCKS // 2
+        pieces = [refs[half].at[d // 2] if d % 2 else refs[d // 2].at[0] for d in range(BLOCKS)]
+        refs = refs[half + 1 :]
+    pair_table, end_table = refs[:2]
+    refs = refs[2:]
+    if not gives_edge:
+        neighbours, refs = refs[:2], refs[2:]
+    outs = refs[:-6]
+    blocks, halos, edges, high, low, result = refs[-6:]
+    z_rank, x_rank = place[0], place[2]
+    rows = blocks.shape[1]
+    chunk = blocks.shape[2]
+    groups = rows // GROUP
+    for d in range(BLOCKS):
+        source = z_rank ^ d
+        meta = pieces[d][rows:, :].astype(jnp.int32).astype(jnp.float32)
+        values, scale = decoded(pieces[d][:rows, :], meta[:groups])
+        blocks[source] = values.reshape(rows, chunk)
+        halos[pl.ds(source, 1), :] = meta[groups : groups + 1] * scale[groups - 1 :]
+        if gives_edge:
+            edges[pl.ds(source, 1), :] = meta[groups + 1 : groups + 2]
+            edges[pl.ds(BLOCKS + source, 1), :] = meta[groups + 2 : groups + 3]
+    if not gives_edge:
+        beside = jnp.where(x_rank % 2 == 1, *(n[n.shape[0] - META :, :].astype(jnp.int32) for n in neighbours))
+        beside = beside.astype(jnp.float32)
+        edge = beside[:BLOCKS] * (jnp.exp2(beside[BLOCKS:] * (1.0 / STEPS)) * (1.0 / TOP))
+        reverse = x_rank >= place[3] // 2
+        spot = pl.ds(pl.multiple_of(jnp.where(reverse, chunk - LANES, 0), LANES), LANES)
+        shape = (BLOCKS, LANES)
+        column = lax.broadcasted_iota(jnp.int32, shape, 1) == jnp.where(reverse, LANES - 1, 0)
+        for b in range(BLOCKS):
+            chosen = column & (lax.broadcasted_iota(jnp.int32, shape, 0) == b) & (x_rank > 0)
+            blocks[b, :, spot] -= lax.dot_general(
+                edge.astype(jnp.bfloat16),
+                chosen.astype(jnp.bfloat16),
+                (((0,), (0,)), ((), ())),
+                preferred_element_type=jnp.float32,
+            )
+    for b in range(1, BLOCKS):
+        blocks[b, :1, :] += halos[b - 1 : b, :]
+
+    near, far, mid = math.cos(math.pi / 8), math.sin(math.pi / 8), math.sqrt(0.5)
+    strip = 16
+
+    def keep(r, part, start, value):
+        spot = pl.ds(part * rows + start, strip)
+        rounded = value.astype(jnp.bfloat16)
+        high[r, spot, :] = rounded
+        low[r, spot, :] = (value - rounded.astype(jnp.float32)).astype(jnp.bfloat16)
+
+    def combine(i, carry):
+        start = pl.multiple_of(i * strip, strip)
+        v = [blocks[b, pl.ds(start, strip), :] for b in range(BLOCKS)]
+        p1, p2, p3 = v[1] + v[7], v[2] + v[6], v[3] + v[5]
+        n1, n2, n3 = v[1] - v[7], v[2] - v[6], v[3] - v[5]
+        ends, gap = v[0] + v[4], v[0] - v[4]
+        odd = p1 + p3
+        even = ends + p2
+        keep(0, 0, start, even + odd)
+        keep(8, 0, start, even - odd)
+        keep(4, 0, start, ends - p2)
+        turn = mid * (p1 - p3)
+        keep(2, 0, start, gap + turn)
+        keep(6, 0, start, gap - turn)
+        turn = mid * (n1 + n3)
+        keep(2, 1, start, turn + n2)
+        keep(6, 1, start, turn - n2)
+        keep(4, 1, start, n1 - n3)
+        m2 = mid * n2
+        s, t = v[0] + m2, near * n1 + far * n3
+        keep(1, 0, start, s + t)
+        keep(7, 0, start, s - t)
+        s, t = v[0] - m2, far * n1 - near * n3
+        keep(3, 0, start, s + t)
+        keep(5, 0, start, s - t)
+        m2 = mid * p2
+        s, t = far * p1 + near * p3, m2 + v[4]
+        keep(1, 1, start, s + t)
+        keep(7, 1, start, s - t)
+        s, t = near * p1 - far * p3, m2 - v[4]
+        keep(3, 1, start, s + t)
+        keep(5, 1, start, s - t)
+        return carry
+
+    lax.fori_loop(0, rows // strip, combine, 0)
+    dot = functools.partial(jnp.dot, preferred_element_type=jnp.float32)
+    half = result.shape[1]
+    for r in range(1, BLOCKS):
+        value = dot(pair_table[0, r - 1], high[r])
+        value += dot(pair_table[0, r - 1], low[r])
+        value += dot(pair_table[1, r - 1], high[r])
+        result[r] = value[:half]
+        result[RESIDUES - r] = value[half:]
+    for e, r in enumerate((0, BLOCKS)):
+        value = dot(end_table[0, e], high[r, :rows, :])
+        value += dot(end_table[0, e], low[r, :rows, :])
+        value += dot(end_table[1, e], high[r, :rows, :])
+        result[r] = value
+    if gives_edge:
+        outs = [outs[0], outs[1], (outs[2], outs[4]), outs[3]]
+    share = half // len(outs)
+    per = share // GROUP
+    for e, out in enumerate(outs):
+        first = pl.multiple_of((x_rank ^ e) * share, GROUP)
+        metas = []
+        for r in range(RESIDUES):
+            values = result[r, pl.ds(first, share), :].reshape(per, GROUP, chunk)
+            codes, steps, _ = encoded(values)
+            ref, first_row = part_of(out, r * share, CUT * share)
+            ref[first_row : first_row + share, :] = codes.reshape(share, chunk).astype(jnp.int16)
+            metas.append(steps)
+        if gives_edge and e % 2:
+            metas.append(edges[...])
+        ref, first_row = part_of(out, RESIDUES * share, CUT * share)
+        ref[first_row:, :] = jnp.concatenate(metas, axis=0).astype(jnp.int32).astype(jnp.int16)
+
+
+def z_transform(place, pieces, tables, x_count, neighbours=()):
+    rows = pieces[0].shape[-2] - META
+    chunk = pieces[0].shape[-1]
+    length = rows * BLOCKS
+    out_rows = [length // x_count + (META if neighbours or e % 2 == 0 else 2 * META) for e in range(x_count)]
+    if not neighbours:
+        share = length // RESIDUES // x_count
+        out_rows = [*out_rows[:2], CUT * share, out_rows[3], out_rows[2] - CUT * share]
+    vmem = pl.BlockSpec(memory_space=pltpu.VMEM)
+    return pl.pallas_call(
+        functools.partial(z_kernel, not neighbours),
+        in_specs=[pl.BlockSpec(memory_space=pltpu.SMEM)] + [vmem] * (len(pieces) + 2 + len(neighbours)),
+        out_specs=[vmem] * len(out_rows),
+        out_shape=[jax.ShapeDtypeStruct((r, chunk), jnp.int16) for r in out_rows],
+        scratch_shapes=[
+            pltpu.VMEM((BLOCKS, rows, chunk), jnp.float32),
+            pltpu.VMEM((BLOCKS, chunk), jnp.float32),
+            pltpu.VMEM((2 * BLOCKS, chunk), jnp.float32),
+            pltpu.VMEM((BLOCKS + 1, 2 * rows, chunk), jnp.bfloat16),
+            pltpu.VMEM((BLOCKS + 1, 2 * rows, chunk), jnp.bfloat16),
+            pltpu.VMEM((RESIDUES, length // RESIDUES, chunk), jnp.float32),
+        ],
+        compiler_params=pltpu.CompilerParams(vmem_limit_bytes=SCOPED),
+        cost_estimate=lasting(4.2),
+        name="z_transform",
+    )(place, *pieces, *tables, *neighbours)
+
+
+def x_kernel(stage, pairs, *refs):
+    place = refs[0]
+    refs = list(refs[1:])
+    pieces = [[refs.pop(0), refs.pop(0)] for _ in pairs]
+    if stage == "first":
+        pieces[1][1] = (pieces[1][1], refs.pop(0))
+    table = refs[0]
+    if stage == "first":
+        frequency, col_part, out, factor_out, values, high, low = refs[1:]
+    elif stage == "last":
+        total, factor, out, values, high, low, finished, sent = refs[1:]
+    else:
+        total, out, values, high, low = refs[1:]
+    x_rank, x_count = place[2], 4
+    rows, chunk = values.shape[3], values.shape[2] * LANES
+    share = rows // RESIDUES
+    per = share // GROUP
+    lefts = []
+    for i, pair in enumerate(pairs):
+        for piece, e in zip(pieces[i], pair):
+            source = x_rank ^ e
+            side = jnp.where(source >= x_count // 2, 1, 0)
+            ref, first_row = part_of(piece, rows, CUT * share)
+            steps = ref[first_row : first_row + META, :].astype(jnp.int32).astype(jnp.float32)
+            for r in range(RESIDUES):
+                ref, first_row = part_of(piece, r * share, CUT * share)
+                part, _ = decoded(ref[first_row : first_row + share, :], steps[r * per : (r + 1) * per])
+                part = part.reshape(share, chunk)
+                for t in range(chunk // LANES):
+                    values[i, side, t, pl.ds(r, share, stride=RESIDUES), :] = part[:, t * LANES : (t + 1) * LANES]
+        left = x_rank ^ pair[0]
+        lefts.append(jnp.minimum(left, x_count - 1 - left))
+        for t in range(chunk // LANES):
+            near, far = values[i, 0, t], values[i, 1, t]
+            lanes = slice(t * LANES, (t + 1) * LANES)
+            for p, value in enumerate((near + far, near - far)):
+                rounded = value.astype(jnp.bfloat16)
+                high[i, p, :, lanes] = rounded
+                low[i, p, :, lanes] = (value - rounded.astype(jnp.float32)).astype(jnp.bfloat16)
+    if stage == "first":
+        turn = jnp.full((8, LANES), frequency[place[0]], jnp.int32).astype(jnp.float32)
+        sine = jnp.sin(turn * (math.pi / (2 * NY)))[:1]
+        kz_index = x_rank * rows + lax.broadcasted_iota(jnp.int32, (rows, LANES), 0)
+        row_part = -(4.0 * sine * sine + eigenvalue(kz_index, rows * x_count) + SCREEN_WEIGHT)
+    dot = functools.partial(jnp.dot, preferred_element_type=jnp.float32)
+    count = table.shape[4]
+    width = 256
+    per_row = 2 * count // LANES
+    bands = 4 if stage == "last" else 1
+    band = rows // bands
+    for n in range(bands):
+        here = slice(n * band, (n + 1) * band)
+        for p in range(2):
+            for c in range(count // width):
+                cols = slice(c * width, (c + 1) * width)
+                value = None if stage == "first" else total[p, here, cols]
+                for i, left in enumerate(lefts):
+                    for data, level in ((high, 0), (low, 0), (high, 1)):
+                        term = dot(data[i, p, here, :], table[level, p, left, :, cols])
+                        value = term if value is None else value + term
+                if stage == "first":
+                    below = jnp.concatenate([row_part] * (width // LANES), axis=1) + col_part[p : p + 1, cols]
+                    factor_out[p, :, cols] = 1.0 / below
+                if stage != "last":
+                    out[p, :, cols] = value
+                    continue
+                value *= factor[p, here, cols]
+                for t in range(width // LANES):
+                    tile = c * (width // LANES) + t
+                    part = value[:, t * LANES : (t + 1) * LANES]
+                    finished[n, pl.ds(2 * tile + p, band, stride=per_row), :] = part
+        if stage == "last":
+            lines = pl.ds(n * band * per_row, band * per_row)
+            pltpu.make_async_copy(finished.at[n], out.at[lines], sent.at[n]).start()
+    if stage == "last":
+        for n in range(bands):
+            lines = pl.ds(n * band * per_row, band * per_row)
+            pltpu.make_async_copy(finished.at[n], out.at[lines], sent.at[n]).wait()
+
+
+def x_transform(stage, place, pairs, pieces, table, extra):
+    chosen = [pieces[e] for pair in pairs for e in pair]
+    rows = chosen[0].shape[0] - META if stage != "last" else chosen[1].shape[0] - META
+    if stage == "first":
+        chosen.append(pieces[4])
+    chunk = chosen[0].shape[1]
+    count = table.shape[4]
+    vmem = pl.BlockSpec(memory_space=pltpu.VMEM)
+    smem = pl.BlockSpec(memory_space=pltpu.SMEM)
+    sums = jax.ShapeDtypeStruct((2, rows, count), jnp.float32)
+    scratch = [
+        pltpu.VMEM((len(pairs), 2, chunk // LANES, rows, LANES), jnp.float32),
+        pltpu.VMEM((len(pairs), 2, rows, chunk), jnp.bfloat16),
+        pltpu.VMEM((len(pairs), 2, rows, chunk), jnp.bfloat16),
+    ]
+    out_shape, out_specs = sums, vmem
+    if stage == "first":
+        out_shape, out_specs = [sums, sums], [vmem, vmem]
+    elif stage == "last":
+        lines = rows * 2 * count // LANES
+        out_shape = jax.ShapeDtypeStruct((lines, LANES), jnp.float32)
+        out_specs = pl.BlockSpec(memory_space=pltpu.HBM)
+        scratch += [pltpu.VMEM((4, lines // 4, LANES), jnp.float32), pltpu.SemaphoreType.DMA((4,))]
+    return pl.pallas_call(
+        functools.partial(x_kernel, stage, pairs),
+        in_specs=[smem] + [vmem] * (len(chosen) + 1) + ([smem, vmem] if stage == "first" else [vmem] * len(extra)),
+        out_specs=out_specs,
+        out_shape=out_shape,
+        scratch_shapes=scratch,
+        compiler_params=pltpu.CompilerParams(vmem_limit_bytes=SCOPED),
+        cost_estimate=pl.CostEstimate(
+            flops=12 * rows * len(pairs) * chunk * count, bytes_accessed=16 * rows * count, transcendentals=0
+        ),
+        name="x_transform",
+    )(place, *chosen, table, *extra)
+
+
+def sent(piece, axis, d):
+    return lax.ppermute(piece, axis, [(i, i ^ d) for i in range(lax.axis_size(axis))])
+
+
+def shards(flux_xface, flux_yspec, flux_zface, frequency_y):
+    z_count = lax.axis_size("gz")
+    x_count = lax.axis_size("xy")
+    y_count, planes, x_width = flux_xface.shape
+    length_z, length_x = planes * z_count, x_width * x_count
+    fits = z_count == BLOCKS and y_count == BLOCKS and x_count == 4 and x_width == 4 * LANES
+    if not fits or planes % GROUP or planes // GROUP + 3 > META or planes != 2 * LANES or length_z != RESIDUES * GROUP * x_count:
+        return plain_shards(flux_xface, flux_yspec, flux_zface, frequency_y)
+    z_rank, x_rank = lax.axis_index("gz"), lax.axis_index("xy")
+    place = jnp.stack([z_rank, jnp.int32(z_count), x_rank, jnp.int32(x_count)]).astype(jnp.int32)
+    fluxes = (flux_xface, flux_yspec, flux_zface)
+    inner, outer = (1, 2), (0, 3)
+    whole = (0, x_width)
+    inner_spans, outer_spans = (whole, (LANES, 3 * LANES)), (whole, whole)
+    tables_z = z_tables(length_z)
+    early, late = (6, 7, 2, 4), (3, 5, 1, 0)
+    pieces = divergence(inner, inner_spans, early, place, frequency_y, fluxes, True)
+    place_later, *pieces = lax.optimization_barrier((place, *pieces))
+    first = {d: sent(piece, "gz", d) for d, piece in zip(early, pieces)}
+    pieces = divergence(inner, inner_spans, late, place_later, frequency_y, fluxes, True)
+    place_later, *pieces = lax.optimization_barrier((place, *pieces))
+    first |= {d: sent(piece, "gz", d) if d else piece for d, piece in zip(late, pieces)}
+    ahead = divergence(outer, outer_spans, range(BLOCKS), place_later, frequency_y, fluxes, False, True)
+    first = z_transform(place, [first[d] for d in range(BLOCKS)], tables_z, x_count)
+    ahead, first = lax.optimization_barrier((ahead, first))
+    first = {0: first[0], 1: sent(first[1], "xy", 1), 2: sent(first[2], "xy", 2), 3: sent(first[3], "xy", 3), 4: first[4]}
+    second = [ahead[0]] + [sent(ahead[u], "gz", 2 * u) for u in (1, 2)]
+    last, second[1], first[1] = lax.optimization_barrier((ahead[3], second[1], first[1]))
+    second.append(sent(last, "gz", 6))
+    second, first[3], first[2] = lax.optimization_barrier((second, first[3], first[2]))
+    first[4] = sent(first[4], "xy", 2)
+    second.append(sent(jnp.concatenate([a[1:] for a in second], axis=0), "gz", 1))
+    second = z_transform(place, second, tables_z, x_count, (first[1], first[3]))
+    later = second[2]
+    second = {0: second[0]} | {e: sent(second[e], "xy", e) for e in (3, 1)}
+    kz_count = length_z // x_count
+    halved = length_x // 2
+    kx_index = 2 * np.arange(halved)[None, :] + np.arange(2)[:, None]
+    col_part = np.asarray(-4.0 * np.sin(kx_index * (math.pi / (2 * length_x))) ** 2, np.float32)
+    outside, inside = (0, 3), (1, 2)
+    inner_table = x_tables(length_x, x_count // 2, x_width, inner)
+    outer_table = x_tables(length_x, x_count // 2, x_width, outer)
+    total, factor = x_transform("first", place, (outside, inside), first, inner_table, (frequency_y, col_part))
+    later, total = lax.optimization_barrier((later, total))
+    second |= {2: sent(later, "xy", 2)}
+    total = x_transform("more", place, (outside,), second, outer_table, (total,))
+    flat = x_transform("last", place, (inside,), second, outer_table, (total, factor))
+    tiles = halved // LANES
+    return flat.reshape(1, kz_count, tiles, 2, LANES).transpose(0, 1, 3, 2, 4).reshape(1, kz_count, 2, halved)
+
+
 def solution(mesh):
     return jax.shard_map(
         shards,

time: 361 us -> 90.3 us (0.25); the launches traced: 357 us -> 90.2 us
  matrix products: 124 us -> 0 us
  waiting for transfers between devices: 150 us -> 27.7 us
  local copies, waits for them, and re-layouts: 52.3 us -> 0.08 us
  Pallas kernels: 0 us -> 34.3 us
  other arithmetic: 12.5 us -> 0.12 us
  starting transfers between devices: 17 us -> 27.6 us
    all_to_all x2 -> x0, waiting for transfers between devices: 138 us -> none  [the longest x1 89.2 us: shards(): lax.all_to_all(spectrum_z, 'xy', split_axis=1, concat_axis=2, tiled=True)]
    dot_general x4 -> x0, matrix products: 124 us -> none  [the longest x1 32.1 us: fold_middle(): jnp.einsum('kq,fql->fkl', cosine_table(length, 1), upper_half - lower_hal...]
    pallas_call x0 -> x8, Pallas kernels: none -> 34.3 us  [the longest x3 14.2 us: x_transform(): pl.pallas_call(functools.partial(x_kernel, stage, pairs), in_specs=[smem]...]
    ppermute x2 -> x18, starting transfers between devices: 6.7 us -> 27.6 us  [sent(): lax.ppermute(piece, axis, [(i, i ^ d) for i in range(lax.axis_size(axis))])]
    rev x2 -> x0, local copies, waits for them, and re-layouts: 20.9 us -> none  [the longest x1 10.5 us: fold_last(): lower_half = lax.rev(source[:, :, halved:], (2,))]
    ppermute x2 -> x18, waiting for transfers between devices: 11.4 us -> 27.7 us  [sent(): lax.ppermute(piece, axis, [(i, i ^ d) for i in range(lax.axis_size(axis))])]
    another operation x1 -> x0, local copies, waits for them, and re-layouts: 11 us -> none  [fold_middle(): return jnp.stack([even_part, odd_part], axis=2).reshape(source.shape)]
    all_to_all x1 -> x0, local copies, waits for them, and re-layouts: 10.9 us -> none  [shards(): lax.all_to_all(spectrum_z, 'xy', split_axis=1, concat_axis=2, tiled=True)]
  transfers between devices with their start and end apart: 4 -> 18, of which waited for: 3 -> 8; matrix products, arithmetic and copies ran while one was open for 1% -> 0% of each run, Pallas kernels for 0% -> 24%
where the time goes in v2:
time: 90.3 us; the launch traced here: 90.2 us
  Pallas kernels  34.3 us (38%)
  waiting for transfers between devices  27.7 us (31%)
  starting transfers between devices  27.6 us (31%)
    ppermute x18, waiting for transfers between devices, sent(): lax.ppermute(piece, axis, [(i, i ^ d) for i in range(lax.axis_size(axis))])  27.7 us
    ppermute x18, starting transfers between devices, sent(): lax.ppermute(piece, axis, [(i, i ^ d) for i in range(lax.axis_size(axis))])  27.6 us
    pallas_call x3, Pallas kernels, x_transform(): pl.pallas_call(functools.partial(x_kernel, stage, pairs), in_specs=[smem]...  14.2 us
    pallas_call x3, Pallas kernels, divergence(): pl.pallas_call(functools.partial(divergence_kernel, tiles, spans, order,...  11.1 us
    pallas_call x2, Pallas kernels, z_transform(): pl.pallas_call(functools.partial(z_kernel, not neighbours), in_specs=[pl....  8.97 us
  transfers between devices with their start and end apart: 18, of which 8 were waited for; matrix products, arithmetic and copies ran while one was open for 0% of the time, Pallas kernels for 24%

profile of v2, /device:TPU:0, one launch (start us, length us, event | category | flops | bytes accessed | tf_op | source)
XLA Modules:
  0.0 90.2 jit_solution(14335733003656326392)
XLA Ops:
  0.1 3.2 %divergence.3 = (s16[272,256]{1,0:T(8,128)(2,1)S(1)}, s16[272,256]{1,0:T(8,128)(2,1)S(1)}, s16[272,256]{1,0:T(8,128)(2,1)S(1)}, s16[272,256]{1,0:T(8,128)(2,1)S(1)}) custom-call(s32[4]{0:T(128)S(1)} %pad_add_fusion.1.place.refs_0_, s32[8]{0:T(128)} %refs_7_.1, bf16[8,256,512]{2,1,0:T(8,128)(2,1)} %flux_x.5, bf16[8,256,512]{2,1,0:T(8,128)(2,1)} %flux_y.5, ...), custom_call_target="tpu_custom_call" | custom-call | bytes 11808000 | tf_op jit(solution)/shard_map/divergence/pallas_call | solution.py:284
  3.3 3.0 %collective-permute-start.1 = (s16[272,256]{1,0:T(8,128)(2,1)S(1)}, s16[272,256]{1,0:T(8,128)(2,1)S(1)}, u32[]{:S(2)}, u32[]{:S(2)}) collective-permute-start(s16[272,256]{1,0:T(8,128)(2,1)S(1)} %get-tuple-element.74), channel_id=1, source_target_pairs={{0,8},{4,12},{8,0},{12,4},{16,24},{20,28},{24,16},{28,20},{1,9},{5... | collective-permute-start | bytes 417800 | tf_op jit(solution)/shard_map/ppermute | solution.py:571
  6.3 1.5 %collective-permute-start.3 = (s16[272,256]{1,0:T(8,128)(2,1)S(1)}, s16[272,256]{1,0:T(8,128)(2,1)S(1)}, u32[]{:S(2)}, u32[]{:S(2)}) collective-permute-start(s16[272,256]{1,0:T(8,128)(2,1)S(1)} %get-tuple-element.76), channel_id=1, source_target_pairs={{0,16},{4,20},{8,24},{12,28},{16,0},{20,4},{24,8},{28,12},{1,17},{... | collective-permute-start | bytes 417800 | tf_op jit(solution)/shard_map/ppermute | solution.py:571
  7.8 1.5 %collective-permute-start.6 = (s16[272,256]{1,0:T(8,128)(2,1)S(1)}, s16[272,256]{1,0:T(8,128)(2,1)S(1)}, u32[]{:S(2)}, u32[]{:S(2)}) collective-permute-start(s16[272,256]{1,0:T(8,128)(2,1)S(1)} %get-tuple-element.79), channel_id=1, source_target_pairs={{0,28},{4,24},{8,20},{12,16},{16,12},{20,8},{24,4},{28,0},{1,29},{... | collective-permute-start | bytes 417800 | tf_op jit(solution)/shard_map/ppermute | solution.py:571
  9.3 3.2 %divergence.4 = (s16[272,256]{1,0:T(8,128)(2,1)S(1)}, s16[272,256]{1,0:T(8,128)(2,1)S(1)}, s16[272,256]{1,0:T(8,128)(2,1)S(1)}, s16[272,256]{1,0:T(8,128)(2,1)S(1)}) custom-call(s32[4]{0:T(128)S(1)} %pad_add_fusion.1.place.refs_0_, s32[8]{0:T(128)} %refs_7_.1, bf16[8,256,512]{2,1,0:T(8,128)(2,1)} %flux_x.5, bf16[8,256,512]{2,1,0:T(8,128)(2,1)} %flux_y.5, ...), custom_call_target="tpu_custom_call" | custom-call | bytes 11808000 | tf_op jit(solution)/shard_map/divergence/pallas_call | solution.py:284
  12.5 1.6 %collective-permute-start = (s16[272,256]{1,0:T(8,128)(2,1)S(1)}, s16[272,256]{1,0:T(8,128)(2,1)S(1)}, u32[]{:S(2)}, u32[]{:S(2)}) collective-permute-start(s16[272,256]{1,0:T(8,128)(2,1)S(1)} %get-tuple-element.73), channel_id=1, source_target_pairs={{0,4},{4,0},{8,12},{12,8},{16,20},{20,16},{24,28},{28,24},{1,5},{5... | collective-permute-start | bytes 417800 | tf_op jit(solution)/shard_map/ppermute | solution.py:571
  14.4 3.0 %collective-permute-done.3.refs_4_ = s16[272,256]{1,0:T(8,128)(2,1)S(1)} collective-permute-done((s16[272,256]{1,0:T(8,128)(2,1)S(1)}, s16[272,256]{1,0:T(8,128)(2,1)S(1)}, u32[]{:S(2)}, u32[]{:S(2)}) %collective-permute-start.3) | collective-permute-done | bytes 139296 | tf_op jit(solution)/shard_map/ppermute | solution.py:571
  17.4 4.8 %divergence.5 = (s16[2,272,256]{2,1,0:T(8,128)(2,1)S(1)}, s16[2,272,256]{2,1,0:T(8,128)(2,1)S(1)}, s16[2,272,256]{2,1,0:T(8,128)(2,1)S(1)}, s16[2,272,256]{2,1,0:T(8,128)(2,1)S(1)}) custom-call(s32[4]{0:T(128)S(1)} %pad_add_fusion.1.place.refs_0_, s32[8]{0:T(128)} %refs_7_.1, bf16[8,256,512]{2,1,0:T(8,128)(2,1)} %flux_x.5, bf16[8,256,512]{2,1,0:T(8,128)(2,1)} %flux_y.5, ...), custom_call_target="tpu_custom_call" | custom-call | bytes 19188000 | tf_op jit(solution)/shard_map/divergence/pallas_call | solution.py:284
  23.3 4.2 %z_transform.2 = (s16[528,256]{1,0:T(8,128)(2,1)S(1)}, s16[544,256]{1,0:T(8,128)(2,1)S(1)}, s16[192,256]{1,0:T(8,128)(2,1)S(1)}, s16[544,256]{1,0:T(8,128)(2,1)S(1)}, s16[336,256]{1,0:T(8,128)(2,1)S(1)}) custom-call(s32[4]{0:T(128)S(1)} %pad_add_fusion.1.place.refs_0_, s16[272,256]{1,0:T(8,128)(2,1)S(1)} %get-tuple-element.72.refs_0_, ...), custom_call_target="tpu_custom_call" | custom-call | bytes 15498000 | tf_op jit(solution)/shard_map/z_transform/pallas_call | solution.py:434
  27.6 1.6 %collective-permute-start.8 = (s16[544,256]{1,0:T(8,128)(2,1)S(1)}, s16[544,256]{1,0:T(8,128)(2,1)S(1)}, u32[]{:S(2)}, u32[]{:S(2)}) collective-permute-start(s16[544,256]{1,0:T(8,128)(2,1)S(1)} %get-tuple-element.88), channel_id=1, source_target_pairs={{0,1},{1,0},{2,3},{3,2},{4,5},{5,4},{6,7},{7,6},{8,9},{9,8},{10,11... | collective-permute-start | bytes 835592 | tf_op jit(solution)/shard_map/ppermute | solution.py:571
  30.2 2.5 %collective-permute-start.11 = (s16[544,256]{1,0:T(8,128)(2,1)S(1)}, s16[544,256]{1,0:T(8,128)(2,1)S(1)}, u32[]{:S(2)}, u32[]{:S(2)}) collective-permute-start(s16[544,256]{1,0:T(8,128)(2,1)S(1)} %get-tuple-element.92), channel_id=1, source_target_pairs={{0,3},{1,2},{2,1},{3,0},{4,7},{5,6},{6,5},{7,4},{8,11},{9,10},{10,... | collective-permute-start | bytes 835592 | tf_op jit(solution)/shard_map/ppermute | solution.py:571
  32.7 4.1 %collective-permute-done.7.refs_1_ = s16[2,272,256]{2,1,0:T(8,128)(2,1)S(1)} collective-permute-done((s16[2,272,256]{2,1,0:T(8,128)(2,1)S(1)}, s16[2,272,256]{2,1,0:T(8,128)(2,1)S(1)}, u32[]{:S(2)}, u32[]{:S(2)}) %collective-permute-start.7) | collective-permute-done | bytes 278560 | tf_op jit(solution)/shard_map/ppermute | solution.py:571
  37.0 1.4 %collective-permute-start.10 = (s16[2,272,256]{2,1,0:T(8,128)(2,1)S(1)}, s16[2,272,256]{2,1,0:T(8,128)(2,1)S(1)}, u32[]{:S(2)}, u32[]{:S(2)}) collective-permute-start(s16[2,272,256]{2,1,0:T(8,128)(2,1)S(1)} %get-tuple-element.91), channel_id=1, source_target_pairs={{0,24},{4,28},{8,16},{12,20},{16,8},{20,12},{24,0},{28,4},{1,25},{... | collective-permute-start | bytes 835592 | tf_op jit(solution)/shard_map/ppermute | solution.py:571
  38.5 3.4 %collective-permute-start.12 = (s16[192,256]{1,0:T(8,128)(2,1)S(1)}, s16[192,256]{1,0:T(8,128)(2,1)S(1)}, u32[]{:S(2)}, u32[]{:S(2)}) collective-permute-start(s16[192,256]{1,0:T(8,128)(2,1)S(1)} %get-tuple-element.93), channel_id=1, source_target_pairs={{0,2},{1,3},{2,0},{3,1},{4,6},{5,7},{6,4},{7,5},{8,10},{9,11},{10,... | collective-permute-start | bytes 294920 | tf_op jit(solution)/shard_map/ppermute | solution.py:571
  41.8 6.5 %collective-permute-done.12.refs_4_ = s16[192,256]{1,0:T(8,128)(2,1)S(1)} collective-permute-done((s16[192,256]{1,0:T(8,128)(2,1)S(1)}, s16[192,256]{1,0:T(8,128)(2,1)S(1)}, u32[]{:S(2)}, u32[]{:S(2)}) %collective-permute-start.12) | collective-permute-done | bytes 98336 | tf_op jit(solution)/shard_map/ppermute | solution.py:571
  48.6 1.7 %collective-permute-start.15 = (s16[336,256]{1,0:T(8,128)(2,1)S(1)}, s16[336,256]{1,0:T(8,128)(2,1)S(1)}, u32[]{:S(2)}, u32[]{:S(2)}) collective-permute-start(s16[336,256]{1,0:T(8,128)(2,1)S(1)} %get-tuple-element.104), channel_id=1, source_target_pairs={{0,2},{1,3},{2,0},{3,1},{4,6},{5,7},{6,4},{7,5},{8,10},{9,11},{10,... | collective-permute-start | bytes 516104 | tf_op jit(solution)/shard_map/ppermute | solution.py:571
  50.5 4.7 %z_transform.3 = (s16[528,256]{1,0:T(8,128)(2,1)S(1)}, s16[528,256]{1,0:T(8,128)(2,1)S(1)}, s16[528,256]{1,0:T(8,128)(2,1)S(1)}, s16[528,256]{1,0:T(8,128)(2,1)S(1)}) custom-call(s32[4]{0:T(128)S(1)} %pad_add_fusion.1.place.refs_0_, s16[2,272,256]{2,1,0:T(8,128)(2,1)S(1)} %get-tuple-element.94.refs_0_, ...), custom_call_target="tpu_custom_call" | custom-call | bytes 15498000 | tf_op jit(solution)/shard_map/z_transform/pallas_call | solution.py:434
  55.2 5.7 %collective-permute-start.17 = (s16[528,256]{1,0:T(8,128)(2,1)S(1)}, s16[528,256]{1,0:T(8,128)(2,1)S(1)}, u32[]{:S(2)}, u32[]{:S(2)}) collective-permute-start(s16[528,256]{1,0:T(8,128)(2,1)S(1)} %get-tuple-element.108), channel_id=1, source_target_pairs={{0,3},{1,2},{2,1},{3,0},{4,7},{5,6},{6,5},{7,4},{8,11},{9,10},{10,... | collective-permute-start | bytes 811016 | tf_op jit(solution)/shard_map/ppermute | solution.py:571
  60.9 6.4 %x_transform.3 = (f32[2,512,1024]{2,1,0:T(8,128)S(1)}, f32[2,512,1024]{2,1,0:T(8,128)S(1)}) custom-call(s32[4]{0:T(128)S(1)} %pad_add_fusion.1.place.refs_0_, s16[528,256]{1,0:T(8,128)(2,1)S(1)} %get-tuple-element.102.refs_1_, s16[544,256]{1,0:T(8,128)(2,1)S(1)} %collective-permute-done.11.refs_8_.refs_2_, ...), custom_call_target="tpu_custom_call" | custom-call | flops 3221225472 | bytes 8388608 | tf_op jit(solution)/shard_map/x_transform/pallas_call | solution.py:556
  67.4 2.2 %collective-permute-start.16 = (s16[528,256]{1,0:T(8,128)(2,1)S(1)}, s16[528,256]{1,0:T(8,128)(2,1)S(1)}, u32[]{:S(2)}, u32[]{:S(2)}) collective-permute-start(s16[528,256]{1,0:T(8,128)(2,1)S(1)} %get-tuple-element.106), channel_id=1, source_target_pairs={{0,2},{1,3},{2,0},{3,1},{4,6},{5,7},{6,4},{7,5},{8,10},{9,11},{10,... | collective-permute-start | bytes 811016 | tf_op jit(solution)/shard_map/ppermute | solution.py:571
  69.6 2.8 %x_transform.4.refs_4_ = f32[2,512,1024]{2,1,0:T(8,128)S(1)} custom-call(s32[4]{0:T(128)S(1)} %pad_add_fusion.1.place.refs_0_, s16[528,256]{1,0:T(8,128)(2,1)S(1)} %get-tuple-element.107.refs_1_, s16[528,256]{1,0:T(8,128)(2,1)S(1)} %collective-permute-done.17.refs_2_, bf16[2,2,2,256,1024]{4,3,2,1,0:T(8,128)(2,1)S(1)} %copy-done, ...), custom_call_target="tpu_custom_call" | custom-call | flops 1610612736 | bytes 8388608 | tf_op jit(solution)/shard_map/x_transform/pallas_call | solution.py:556
  72.4 5.7 %collective-permute-done.14.refs_1_ = s16[528,256]{1,0:T(8,128)(2,1)S(1)} collective-permute-done((s16[528,256]{1,0:T(8,128)(2,1)S(1)}, s16[528,256]{1,0:T(8,128)(2,1)S(1)}, u32[]{:S(2)}, u32[]{:S(2)}) %collective-permute-start.14) | collective-permute-done | bytes 270368 | tf_op jit(solution)/shard_map/ppermute | solution.py:571
  78.1 6.9 %collective-permute-done.16.refs_2_ = s16[528,256]{1,0:T(8,128)(2,1)S(1)} collective-permute-done((s16[528,256]{1,0:T(8,128)(2,1)S(1)}, s16[528,256]{1,0:T(8,128)(2,1)S(1)}, u32[]{:S(2)}, u32[]{:S(2)}) %collective-permute-start.16) | collective-permute-done | bytes 270368 | tf_op jit(solution)/shard_map/ppermute | solution.py:571
  85.0 5.0 %x_transform.5 = f32[8192,128]{1,0:T(8,128)} custom-call(s32[4]{0:T(128)S(1)} %pad_add_fusion.1.place.refs_0_, s16[528,256]{1,0:T(8,128)(2,1)S(1)} %collective-permute-done.14.refs_1_, s16[528,256]{1,0:T(8,128)(2,1)S(1)} %collective-permute-done.16.refs_2_, bf16[2,2,2,256,1024]{4,3,2,1,0:T(8,128)(2,1)S(1)} %copy-done, ...), custom_call_target="tpu_custom_call" | custom-call | flops 1610612736 | bytes 8388608 | tf_op jit(solution)/shard_map/x_transform/pallas_call | solution.py:556
  (38 shorter events, 3.2 us)
Async XLA Ops:
  3.3 10.8 %collective-permute-start.1 = (s16[272,256]{1,0:T(8,128)(2,1)S(1)}, s16[272,256]{1,0:T(8,128)(2,1)S(1)}, u32[]{:S(2)}, u32[]{:S(2)}) collective-permute-start(s16[272,256]{1,0:T(8,128)(2,1)S(1)} %get-tuple-element.74), channel_id=1, source_target_pairs={{0,8},{4,12},{8,0},{12,4},{16,24},{20,28},{24,16},{28,20},{1,9},{5... | collective-permute-start | bytes 417800 | tf_op jit(solution)/shard_map/ppermute | solution.py:571
  6.3 11.1 %collective-permute-start.3 = (s16[272,256]{1,0:T(8,128)(2,1)S(1)}, s16[272,256]{1,0:T(8,128)(2,1)S(1)}, u32[]{:S(2)}, u32[]{:S(2)}) collective-permute-start(s16[272,256]{1,0:T(8,128)(2,1)S(1)} %get-tuple-element.76), channel_id=1, source_target_pairs={{0,16},{4,20},{8,24},{12,28},{16,0},{20,4},{24,8},{28,12},{1,17},{... | collective-permute-start | bytes 417800 | tf_op jit(solution)/shard_map/ppermute | solution.py:571
  7.8 14.3 %collective-permute-start.5 = (s16[272,256]{1,0:T(8,128)(2,1)S(1)}, s16[272,256]{1,0:T(8,128)(2,1)S(1)}, u32[]{:S(2)}, u32[]{:S(2)}) collective-permute-start(s16[272,256]{1,0:T(8,128)(2,1)S(1)} %get-tuple-element.78), channel_id=1, source_target_pairs={{0,24},{4,28},{8,16},{12,20},{16,8},{20,12},{24,0},{28,4},{1,25},{... | collective-permute-start | bytes 417800 | tf_op jit(solution)/shard_map/ppermute | solution.py:571
  7.8 14.3 %collective-permute-start.6 = (s16[272,256]{1,0:T(8,128)(2,1)S(1)}, s16[272,256]{1,0:T(8,128)(2,1)S(1)}, u32[]{:S(2)}, u32[]{:S(2)}) collective-permute-start(s16[272,256]{1,0:T(8,128)(2,1)S(1)} %get-tuple-element.79), channel_id=1, source_target_pairs={{0,28},{4,24},{8,20},{12,16},{16,12},{20,8},{24,4},{28,0},{1,29},{... | collective-permute-start | bytes 417800 | tf_op jit(solution)/shard_map/ppermute | solution.py:571
  12.5 10.7 %copy-start.1 = (bf16[2,7,256,512]{3,2,1,0:T(8,128)(2,1)S(1)}, bf16[2,7,256,512]{3,2,1,0:T(8,128)(2,1)}, u32[]{:S(2)}) copy-start(bf16[2,7,256,512]{3,2,1,0:T(8,128)(2,1)} %constant.23.clone.refs_8_.refs_5_) | copy-start | bytes 11010052
  12.5 10.7 %copy-start.2 = (bf16[2,2,128,256]{3,2,1,0:T(8,128)(2,1)S(1)}, bf16[2,2,128,256]{3,2,1,0:T(8,128)(2,1)}, u32[]{:S(2)}) copy-start(bf16[2,2,128,256]{3,2,1,0:T(8,128)(2,1)} %constant.24.clone.refs_9_.refs_6_) | copy-start | bytes 786436
  12.5 9.6 %collective-permute-start = (s16[272,256]{1,0:T(8,128)(2,1)S(1)}, s16[272,256]{1,0:T(8,128)(2,1)S(1)}, u32[]{:S(2)}, u32[]{:S(2)}) collective-permute-start(s16[272,256]{1,0:T(8,128)(2,1)S(1)} %get-tuple-element.73), channel_id=1, source_target_pairs={{0,4},{4,0},{8,12},{12,8},{16,20},{20,16},{24,28},{28,24},{1,5},{5... | collective-permute-start | bytes 417800 | tf_op jit(solution)/shard_map/ppermute | solution.py:571
  14.1 8.1 %collective-permute-start.2 = (s16[272,256]{1,0:T(8,128)(2,1)S(1)}, s16[272,256]{1,0:T(8,128)(2,1)S(1)}, u32[]{:S(2)}, u32[]{:S(2)}) collective-permute-start(s16[272,256]{1,0:T(8,128)(2,1)S(1)} %get-tuple-element.75), channel_id=1, source_target_pairs={{0,12},{4,8},{8,4},{12,0},{16,28},{20,24},{24,20},{28,16},{1,13},{... | collective-permute-start | bytes 417800 | tf_op jit(solution)/shard_map/ppermute | solution.py:571
  17.4 5.9 %collective-permute-start.4 = (s16[272,256]{1,0:T(8,128)(2,1)S(1)}, s16[272,256]{1,0:T(8,128)(2,1)S(1)}, u32[]{:S(2)}, u32[]{:S(2)}) collective-permute-start(s16[272,256]{1,0:T(8,128)(2,1)S(1)} %get-tuple-element.77), channel_id=1, source_target_pairs={{0,20},{4,16},{8,28},{12,24},{16,4},{20,0},{24,12},{28,8},{1,21},{... | collective-permute-start | bytes 417800 | tf_op jit(solution)/shard_map/ppermute | solution.py:571
  27.5 33.4 %copy-start.3 = (s32[8]{0:T(128)S(1)}, s32[8]{0:T(128)}, u32[]{:S(2)}) copy-start(s32[8]{0:T(128)} %refs_7_.1) | copy-start | bytes 100
  27.5 33.4 %copy-start.4 = (bf16[2,2,2,256,1024]{4,3,2,1,0:T(8,128)(2,1)S(1)}, bf16[2,2,2,256,1024]{4,3,2,1,0:T(8,128)(2,1)}, u32[]{:S(2)}) copy-start(bf16[2,2,2,256,1024]{4,3,2,1,0:T(8,128)(2,1)} %constant.25.clone.refs_6_) | copy-start | bytes 12582916
  27.5 33.4 %copy-start.5 = (f32[2,1024]{1,0:T(2,128)S(1)}, f32[2,1024]{1,0:T(2,128)}, u32[]{:S(2)}) copy-start(f32[2,1024]{1,0:T(2,128)} %constant.26.clone.refs_8_) | copy-start | bytes 24580
  27.5 9.2 %collective-permute-start.7 = (s16[2,272,256]{2,1,0:T(8,128)(2,1)S(1)}, s16[2,272,256]{2,1,0:T(8,128)(2,1)S(1)}, u32[]{:S(2)}, u32[]{:S(2)}) collective-permute-start(s16[2,272,256]{2,1,0:T(8,128)(2,1)S(1)} %get-tuple-element.87), channel_id=1, source_target_pairs={{0,8},{4,12},{8,0},{12,4},{16,24},{20,28},{24,16},{28,20},{1,9},{5... | collective-permute-start | bytes 835592 | tf_op jit(solution)/shard_map/ppermute | solution.py:571
  27.6 9.4 %collective-permute-start.8 = (s16[544,256]{1,0:T(8,128)(2,1)S(1)}, s16[544,256]{1,0:T(8,128)(2,1)S(1)}, u32[]{:S(2)}, u32[]{:S(2)}) collective-permute-start(s16[544,256]{1,0:T(8,128)(2,1)S(1)} %get-tuple-element.88), channel_id=1, source_target_pairs={{0,1},{1,0},{2,3},{3,2},{4,5},{5,4},{6,7},{7,6},{8,9},{9,8},{10,11... | collective-permute-start | bytes 835592 | tf_op jit(solution)/shard_map/ppermute | solution.py:571
  29.3 19.1 %collective-permute-start.9 = (s16[2,272,256]{2,1,0:T(8,128)(2,1)S(1)}, s16[2,272,256]{2,1,0:T(8,128)(2,1)S(1)}, u32[]{:S(2)}, u32[]{:S(2)}) collective-permute-start(s16[2,272,256]{2,1,0:T(8,128)(2,1)S(1)} %get-tuple-element.90), channel_id=1, source_target_pairs={{0,16},{4,20},{8,24},{12,28},{16,0},{20,4},{24,8},{28,12},{1,17},{... | collective-permute-start | bytes 835592 | tf_op jit(solution)/shard_map/ppermute | solution.py:571
  30.2 18.2 %collective-permute-start.11 = (s16[544,256]{1,0:T(8,128)(2,1)S(1)}, s16[544,256]{1,0:T(8,128)(2,1)S(1)}, u32[]{:S(2)}, u32[]{:S(2)}) collective-permute-start(s16[544,256]{1,0:T(8,128)(2,1)S(1)} %get-tuple-element.92), channel_id=1, source_target_pairs={{0,3},{1,2},{2,1},{3,0},{4,7},{5,6},{6,5},{7,4},{8,11},{9,10},{10,... | collective-permute-start | bytes 835592 | tf_op jit(solution)/shard_map/ppermute | solution.py:571
  37.0 11.3 %collective-permute-start.10 = (s16[2,272,256]{2,1,0:T(8,128)(2,1)S(1)}, s16[2,272,256]{2,1,0:T(8,128)(2,1)S(1)}, u32[]{:S(2)}, u32[]{:S(2)}) collective-permute-start(s16[2,272,256]{2,1,0:T(8,128)(2,1)S(1)} %get-tuple-element.91), channel_id=1, source_target_pairs={{0,24},{4,28},{8,16},{12,20},{16,8},{20,12},{24,0},{28,4},{1,25},{... | collective-permute-start | bytes 835592 | tf_op jit(solution)/shard_map/ppermute | solution.py:571
  38.5 9.9 %collective-permute-start.12 = (s16[192,256]{1,0:T(8,128)(2,1)S(1)}, s16[192,256]{1,0:T(8,128)(2,1)S(1)}, u32[]{:S(2)}, u32[]{:S(2)}) collective-permute-start(s16[192,256]{1,0:T(8,128)(2,1)S(1)} %get-tuple-element.93), channel_id=1, source_target_pairs={{0,2},{1,3},{2,0},{3,1},{4,6},{5,7},{6,4},{7,5},{8,10},{9,11},{10,... | collective-permute-start | bytes 294920 | tf_op jit(solution)/shard_map/ppermute | solution.py:571
  48.5 2.0 %collective-permute-start.13 = (s16[4,272,256]{2,1,0:T(8,128)(2,1)S(1)}, s16[4,272,256]{2,1,0:T(8,128)(2,1)S(1)}, u32[]{:S(2)}, u32[]{:S(2)}) collective-permute-start(s16[4,272,256]{2,1,0:T(8,128)(2,1)S(1)} %pad_add_fusion), channel_id=1, source_target_pairs={{0,4},{4,0},{8,12},{12,8},{16,20},{20,16},{24,28},{28,24},{1,5},{5... | collective-permute-start | bytes 1671176 | tf_op jit(solution)/shard_map/ppermute | solution.py:571
  48.6 12.3 %collective-permute-start.15 = (s16[336,256]{1,0:T(8,128)(2,1)S(1)}, s16[336,256]{1,0:T(8,128)(2,1)S(1)}, u32[]{:S(2)}, u32[]{:S(2)}) collective-permute-start(s16[336,256]{1,0:T(8,128)(2,1)S(1)} %get-tuple-element.104), channel_id=1, source_target_pairs={{0,2},{1,3},{2,0},{3,1},{4,6},{5,7},{6,4},{7,5},{8,10},{9,11},{10,... | collective-permute-start | bytes 516104 | tf_op jit(solution)/shard_map/ppermute | solution.py:571
  55.2 14.4 %copy-start = (bf16[2,2,2,256,1024]{4,3,2,1,0:T(8,128)(2,1)S(1)}, bf16[2,2,2,256,1024]{4,3,2,1,0:T(8,128)(2,1)}, u32[]{:S(2)}) copy-start(bf16[2,2,2,256,1024]{4,3,2,1,0:T(8,128)(2,1)} %constant.27.clone.refs_3_) | copy-start | bytes 12582916
  55.2 14.4 %collective-permute-start.17 = (s16[528,256]{1,0:T(8,128)(2,1)S(1)}, s16[528,256]{1,0:T(8,128)(2,1)S(1)}, u32[]{:S(2)}, u32[]{:S(2)}) collective-permute-start(s16[528,256]{1,0:T(8,128)(2,1)S(1)} %get-tuple-element.108), channel_id=1, source_target_pairs={{0,3},{1,2},{2,1},{3,0},{4,7},{5,6},{6,5},{7,4},{8,11},{9,10},{10,... | collective-permute-start | bytes 811016 | tf_op jit(solution)/shard_map/ppermute | solution.py:571
  67.3 10.8 %collective-permute-start.14 = (s16[528,256]{1,0:T(8,128)(2,1)S(1)}, s16[528,256]{1,0:T(8,128)(2,1)S(1)}, u32[]{:S(2)}, u32[]{:S(2)}) collective-permute-start(s16[528,256]{1,0:T(8,128)(2,1)S(1)} %get-tuple-element.100), channel_id=1, source_target_pairs={{0,1},{1,0},{2,3},{3,2},{4,5},{5,4},{6,7},{7,6},{8,9},{9,8},{10,11... | collective-permute-start | bytes 811016 | tf_op jit(solution)/shard_map/ppermute | solution.py:571
  67.4 17.6 %collective-permute-start.16 = (s16[528,256]{1,0:T(8,128)(2,1)S(1)}, s16[528,256]{1,0:T(8,128)(2,1)S(1)}, u32[]{:S(2)}, u32[]{:S(2)}) collective-permute-start(s16[528,256]{1,0:T(8,128)(2,1)S(1)} %get-tuple-element.106), channel_id=1, source_target_pairs={{0,2},{1,3},{2,0},{3,1},{4,6},{5,7},{6,4},{7,5},{8,10},{9,11},{10,... | collective-permute-start | bytes 811016 | tf_op jit(solution)/shard_map/ppermute | solution.py:571

commit v3 on v2

--- a/solution.py
+++ b/solution.py
@@ -450,12 +450,10 @@
     )(place, *pieces, *tables, *neighbours)
 
 
-def x_kernel(stage, pairs, *refs):
+def x_kernel(stage, pairs, halved, *refs):
     place = refs[0]
     refs = list(refs[1:])
-    pieces = [[refs.pop(0), refs.pop(0)] for _ in pairs]
-    if stage == "first":
-        pieces[1][1] = (pieces[1][1], refs.pop(0))
+    pieces = [[(refs.pop(0), refs.pop(0)) if e in halved else refs.pop(0) for e in pair] for pair in pairs]
     table = refs[0]
     if stage == "first":
         frequency, col_part, out, factor_out, values, high, low = refs[1:]
@@ -531,10 +529,12 @@
 
 
 def x_transform(stage, place, pairs, pieces, table, extra):
-    chosen = [pieces[e] for pair in pairs for e in pair]
-    rows = chosen[0].shape[0] - META if stage != "last" else chosen[1].shape[0] - META
-    if stage == "first":
-        chosen.append(pieces[4])
+    halved = [e for e in pieces if isinstance(pieces[e], tuple)]
+    chosen = []
+    for pair in pairs:
+        for e in pair:
+            chosen += pieces[e] if e in halved else [pieces[e]]
+    rows = pieces[0].shape[0] - META
     chunk = chosen[0].shape[1]
     count = table.shape[4]
     vmem = pl.BlockSpec(memory_space=pltpu.VMEM)
@@ -554,7 +554,7 @@
         out_specs = pl.BlockSpec(memory_space=pltpu.HBM)
         scratch += [pltpu.VMEM((4, lines // 4, LANES), jnp.float32), pltpu.SemaphoreType.DMA((4,))]
     return pl.pallas_call(
-        functools.partial(x_kernel, stage, pairs),
+        functools.partial(x_kernel, stage, pairs, halved),
         in_specs=[smem] + [vmem] * (len(chosen) + 1) + ([smem, vmem] if stage == "first" else [vmem] * len(extra)),
         out_specs=out_specs,
         out_shape=out_shape,
@@ -594,13 +594,13 @@
     place_later, *pieces = lax.optimization_barrier((place, *pieces))
     first |= {d: sent(piece, "gz", d) if d else piece for d, piece in zip(late, pieces)}
     ahead = divergence(outer, outer_spans, range(BLOCKS), place_later, frequency_y, fluxes, False, True)
+    ahead, first = lax.optimization_barrier((ahead, first))
     first = z_transform(place, [first[d] for d in range(BLOCKS)], tables_z, x_count)
-    ahead, first = lax.optimization_barrier((ahead, first))
     first = {0: first[0], 1: sent(first[1], "xy", 1), 2: sent(first[2], "xy", 2), 3: sent(first[3], "xy", 3), 4: first[4]}
     second = [ahead[0]] + [sent(ahead[u], "gz", 2 * u) for u in (1, 2)]
-    last, second[1], first[1] = lax.optimization_barrier((ahead[3], second[1], first[1]))
+    last = ahead[3]
     second.append(sent(last, "gz", 6))
-    second, first[3], first[2] = lax.optimization_barrier((second, first[3], first[2]))
+    second, first[1], first[3], first[2] = lax.optimization_barrier((second, first[1], first[3], first[2]))
     first[4] = sent(first[4], "xy", 2)
     second.append(sent(jnp.concatenate([a[1:] for a in second], axis=0), "gz", 1))
     second = z_transform(place, second, tables_z, x_count, (first[1], first[3]))
@@ -613,9 +613,11 @@
     outside, inside = (0, 3), (1, 2)
     inner_table = x_tables(length_x, x_count // 2, x_width, inner)
     outer_table = x_tables(length_x, x_count // 2, x_width, outer)
-    total, factor = x_transform("first", place, (outside, inside), first, inner_table, (frequency_y, col_part))
+    first = {0: first[0], 1: first[1], 2: (first[2], first[4]), 3: first[3]}
+    total, factor = x_transform("first", place, (outside,), first, inner_table, (frequency_y, col_part))
     later, total = lax.optimization_barrier((later, total))
     second |= {2: sent(later, "xy", 2)}
+    total = x_transform("more", place, (inside,), first, inner_table, (total,))
     total = x_transform("more", place, (outside,), second, outer_table, (total,))
     flat = x_transform("last", place, (inside,), second, outer_table, (total, factor))
     tiles = halved // LANES

time: 90.3 us -> 88.7 us (0.982)
  waiting for transfers between devices: 27.7 us -> 26.1 us
    ppermute x18, waiting for transfers between devices: 27.7 us -> 26.1 us  [sent(): lax.ppermute(piece, axis, [(i, i ^ d) for i in range(lax.axis_size(axis))])]
    pallas_call x3 -> x4, Pallas kernels: 14.2 us -> 14.9 us  [x_transform(): pl.pallas_call(functools.partial(x_kernel, stage, pairs, halved), in_spec...]
  transfers between devices with their start and end apart: 18 -> 18, of which waited for: 8 -> 8; matrix products, arithmetic and copies ran while one was open for 0% -> 0% of each run, Pallas kernels for 24% -> 26%
where the time goes in v3:
time: 88.7 us; the launch traced here: 88.6 us
  Pallas kernels  35 us (39%)
  starting transfers between devices  26.9 us (30%)
  waiting for transfers between devices  26.1 us (29%)
    ppermute x18, starting transfers between devices, sent(): lax.ppermute(piece, axis, [(i, i ^ d) for i in range(lax.axis_size(axis))])  26.9 us
    ppermute x18, waiting for transfers between devices, sent(): lax.ppermute(piece, axis, [(i, i ^ d) for i in range(lax.axis_size(axis))])  26.1 us
    pallas_call x4, Pallas kernels, x_transform(): pl.pallas_call(functools.partial(x_kernel, stage, pairs, halved), in_spec...  14.9 us
    pallas_call x3, Pallas kernels, divergence(): pl.pallas_call(functools.partial(divergence_kernel, tiles, spans, order,...  11.1 us
    pallas_call x2, Pallas kernels, z_transform(): pl.pallas_call(functools.partial(z_kernel, not neighbours), in_specs=[pl....  8.97 us
  transfers between devices with their start and end apart: 18, of which 8 were waited for; matrix products, arithmetic and copies ran while one was open for 0% of the time, Pallas kernels for 26%

profile of v3, /device:TPU:0, one launch (start us, length us, event | category | flops | bytes accessed | tf_op | source)
XLA Modules:
  0.0 88.6 jit_solution(11366033068031139060)
XLA Ops:
  0.1 3.2 %divergence.3 = (s16[272,256]{1,0:T(8,128)(2,1)S(1)}, s16[272,256]{1,0:T(8,128)(2,1)S(1)}, s16[272,256]{1,0:T(8,128)(2,1)S(1)}, s16[272,256]{1,0:T(8,128)(2,1)S(1)}) custom-call(s32[4]{0:T(128)S(1)} %pad_add_fusion.1.place.refs_0_, s32[8]{0:T(128)} %refs_4_.2, bf16[8,256,512]{2,1,0:T(8,128)(2,1)} %flux_x.5, bf16[8,256,512]{2,1,0:T(8,128)(2,1)} %flux_y.5, ...), custom_call_target="tpu_custom_call" | custom-call | bytes 11808000 | tf_op jit(solution)/shard_map/divergence/pallas_call | solution.py:284
  3.3 3.0 %collective-permute-start.1 = (s16[272,256]{1,0:T(8,128)(2,1)S(1)}, s16[272,256]{1,0:T(8,128)(2,1)S(1)}, u32[]{:S(2)}, u32[]{:S(2)}) collective-permute-start(s16[272,256]{1,0:T(8,128)(2,1)S(1)} %get-tuple-element.75), channel_id=1, source_target_pairs={{0,8},{4,12},{8,0},{12,4},{16,24},{20,28},{24,16},{28,20},{1,9},{5... | collective-permute-start | bytes 417800 | tf_op jit(solution)/shard_map/ppermute | solution.py:571
  6.3 1.5 %collective-permute-start.3 = (s16[272,256]{1,0:T(8,128)(2,1)S(1)}, s16[272,256]{1,0:T(8,128)(2,1)S(1)}, u32[]{:S(2)}, u32[]{:S(2)}) collective-permute-start(s16[272,256]{1,0:T(8,128)(2,1)S(1)} %get-tuple-element.77), channel_id=1, source_target_pairs={{0,16},{4,20},{8,24},{12,28},{16,0},{20,4},{24,8},{28,12},{1,17},{... | collective-permute-start | bytes 417800 | tf_op jit(solution)/shard_map/ppermute | solution.py:571
  9.3 3.2 %divergence.4 = (s16[272,256]{1,0:T(8,128)(2,1)S(1)}, s16[272,256]{1,0:T(8,128)(2,1)S(1)}, s16[272,256]{1,0:T(8,128)(2,1)S(1)}, s16[272,256]{1,0:T(8,128)(2,1)S(1)}) custom-call(s32[4]{0:T(128)S(1)} %pad_add_fusion.1.place.refs_0_, s32[8]{0:T(128)} %refs_4_.2, bf16[8,256,512]{2,1,0:T(8,128)(2,1)} %flux_x.5, bf16[8,256,512]{2,1,0:T(8,128)(2,1)} %flux_y.5, ...), custom_call_target="tpu_custom_call" | custom-call | bytes 11808000 | tf_op jit(solution)/shard_map/divergence/pallas_call | solution.py:284
  12.5 1.6 %collective-permute-start = (s16[272,256]{1,0:T(8,128)(2,1)S(1)}, s16[272,256]{1,0:T(8,128)(2,1)S(1)}, u32[]{:S(2)}, u32[]{:S(2)}) collective-permute-start(s16[272,256]{1,0:T(8,128)(2,1)S(1)} %get-tuple-element.74), channel_id=1, source_target_pairs={{0,4},{4,0},{8,12},{12,8},{16,20},{20,16},{24,28},{28,24},{1,5},{5... | collective-permute-start | bytes 417800 | tf_op jit(solution)/shard_map/ppermute | solution.py:571
  14.4 3.0 %collective-permute-done.3.refs_4_ = s16[272,256]{1,0:T(8,128)(2,1)S(1)} collective-permute-done((s16[272,256]{1,0:T(8,128)(2,1)S(1)}, s16[272,256]{1,0:T(8,128)(2,1)S(1)}, u32[]{:S(2)}, u32[]{:S(2)}) %collective-permute-start.3) | collective-permute-done | bytes 139296 | tf_op jit(solution)/shard_map/ppermute | solution.py:571
  17.4 4.8 %divergence.5 = (s16[2,272,256]{2,1,0:T(8,128)(2,1)S(1)}, s16[2,272,256]{2,1,0:T(8,128)(2,1)S(1)}, s16[2,272,256]{2,1,0:T(8,128)(2,1)S(1)}, s16[2,272,256]{2,1,0:T(8,128)(2,1)S(1)}) custom-call(s32[4]{0:T(128)S(1)} %pad_add_fusion.1.place.refs_0_, s32[8]{0:T(128)} %refs_4_.2, bf16[8,256,512]{2,1,0:T(8,128)(2,1)} %flux_x.5, bf16[8,256,512]{2,1,0:T(8,128)(2,1)} %flux_y.5, ...), custom_call_target="tpu_custom_call" | custom-call | bytes 19188000 | tf_op jit(solution)/shard_map/divergence/pallas_call | solution.py:284
  23.3 4.2 %z_transform.2 = (s16[528,256]{1,0:T(8,128)(2,1)S(1)}, s16[544,256]{1,0:T(8,128)(2,1)S(1)}, s16[192,256]{1,0:T(8,128)(2,1)S(1)}, s16[544,256]{1,0:T(8,128)(2,1)S(1)}, s16[336,256]{1,0:T(8,128)(2,1)S(1)}) custom-call(s32[4]{0:T(128)S(1)} %pad_add_fusion.1.place.refs_0_, s16[272,256]{1,0:T(8,128)(2,1)S(1)} %get-tuple-element.85.refs_0_, ...), custom_call_target="tpu_custom_call" | custom-call | bytes 15498000 | tf_op jit(solution)/shard_map/z_transform/pallas_call | solution.py:434
  27.5 2.6 %collective-permute-start.12 = (s16[192,256]{1,0:T(8,128)(2,1)S(1)}, s16[192,256]{1,0:T(8,128)(2,1)S(1)}, u32[]{:S(2)}, u32[]{:S(2)}) collective-permute-start(s16[192,256]{1,0:T(8,128)(2,1)S(1)} %get-tuple-element.95), channel_id=1, source_target_pairs={{0,2},{1,3},{2,0},{3,1},{4,6},{5,7},{6,4},{7,5},{8,10},{9,11},{10,... | collective-permute-start | bytes 294920 | tf_op jit(solution)/shard_map/ppermute | solution.py:571
  31.2 2.5 %collective-permute-start.9 = (s16[2,272,256]{2,1,0:T(8,128)(2,1)S(1)}, s16[2,272,256]{2,1,0:T(8,128)(2,1)S(1)}, u32[]{:S(2)}, u32[]{:S(2)}) collective-permute-start(s16[2,272,256]{2,1,0:T(8,128)(2,1)S(1)} %get-tuple-element.84), channel_id=1, source_target_pairs={{0,24},{4,28},{8,16},{12,20},{16,8},{20,12},{24,0},{28,4},{1,25},{... | collective-permute-start | bytes 835592 | tf_op jit(solution)/shard_map/ppermute | solution.py:571
  33.6 1.6 %collective-permute-start.10 = (s16[544,256]{1,0:T(8,128)(2,1)S(1)}, s16[544,256]{1,0:T(8,128)(2,1)S(1)}, u32[]{:S(2)}, u32[]{:S(2)}) collective-permute-start(s16[544,256]{1,0:T(8,128)(2,1)S(1)} %get-tuple-element.93), channel_id=1, source_target_pairs={{0,1},{1,0},{2,3},{3,2},{4,5},{5,4},{6,7},{7,6},{8,9},{9,8},{10,11... | collective-permute-start | bytes 835592 | tf_op jit(solution)/shard_map/ppermute | solution.py:571
  35.9 3.6 %collective-permute-start.11 = (s16[544,256]{1,0:T(8,128)(2,1)S(1)}, s16[544,256]{1,0:T(8,128)(2,1)S(1)}, u32[]{:S(2)}, u32[]{:S(2)}) collective-permute-start(s16[544,256]{1,0:T(8,128)(2,1)S(1)} %get-tuple-element.94), channel_id=1, source_target_pairs={{0,3},{1,2},{2,1},{3,0},{4,7},{5,6},{6,5},{7,4},{8,11},{9,10},{10,... | collective-permute-start | bytes 835592 | tf_op jit(solution)/shard_map/ppermute | solution.py:571
  39.6 5.6 %collective-permute-done.8.refs_2_ = s16[2,272,256]{2,1,0:T(8,128)(2,1)S(1)} collective-permute-done((s16[2,272,256]{2,1,0:T(8,128)(2,1)S(1)}, s16[2,272,256]{2,1,0:T(8,128)(2,1)S(1)}, u32[]{:S(2)}, u32[]{:S(2)}) %collective-permute-start.8) | collective-permute-done | bytes 278560 | tf_op jit(solution)/shard_map/ppermute | solution.py:571
  45.2 2.5 %collective-permute-done.10.refs_7_.refs_1_ = s16[544,256]{1,0:T(8,128)(2,1)S(1)} collective-permute-done((s16[544,256]{1,0:T(8,128)(2,1)S(1)}, s16[544,256]{1,0:T(8,128)(2,1)S(1)}, u32[]{:S(2)}, u32[]{:S(2)}) %collective-permute-start.10) | collective-permute-done | bytes 278560 | tf_op jit(solution)/shard_map/ppermute | solution.py:571
  48.0 3.2 %collective-permute-start.17 = (s16[336,256]{1,0:T(8,128)(2,1)S(1)}, s16[336,256]{1,0:T(8,128)(2,1)S(1)}, u32[]{:S(2)}, u32[]{:S(2)}) collective-permute-start(s16[336,256]{1,0:T(8,128)(2,1)S(1)} %get-tuple-element.110), channel_id=1, source_target_pairs={{0,2},{1,3},{2,0},{3,1},{4,6},{5,7},{6,4},{7,5},{8,10},{9,11},{10,... | collective-permute-start | bytes 516104 | tf_op jit(solution)/shard_map/ppermute | solution.py:571
  51.2 4.7 %z_transform.3 = (s16[528,256]{1,0:T(8,128)(2,1)S(1)}, s16[528,256]{1,0:T(8,128)(2,1)S(1)}, s16[528,256]{1,0:T(8,128)(2,1)S(1)}, s16[528,256]{1,0:T(8,128)(2,1)S(1)}) custom-call(s32[4]{0:T(128)S(1)} %pad_add_fusion.1.place.refs_0_, s16[2,272,256]{2,1,0:T(8,128)(2,1)S(1)} %get-tuple-element.96.refs_0_, ...), custom_call_target="tpu_custom_call" | custom-call | bytes 15498000 | tf_op jit(solution)/shard_map/z_transform/pallas_call | solution.py:434
  55.9 2.7 %collective-permute-start.16 = (s16[528,256]{1,0:T(8,128)(2,1)S(1)}, s16[528,256]{1,0:T(8,128)(2,1)S(1)}, u32[]{:S(2)}, u32[]{:S(2)}) collective-permute-start(s16[528,256]{1,0:T(8,128)(2,1)S(1)} %get-tuple-element.108), channel_id=1, source_target_pairs={{0,3},{1,2},{2,1},{3,0},{4,7},{5,6},{6,5},{7,4},{8,11},{9,10},{10,... | collective-permute-start | bytes 811016 | tf_op jit(solution)/shard_map/ppermute | solution.py:571
  58.6 4.3 %x_transform.4 = (f32[2,512,1024]{2,1,0:T(8,128)S(1)}, f32[2,512,1024]{2,1,0:T(8,128)S(1)}) custom-call(s32[4]{0:T(128)S(1)} %pad_add_fusion.1.place.refs_0_, s16[528,256]{1,0:T(8,128)(2,1)S(1)} %get-tuple-element.104.refs_1_, s16[544,256]{1,0:T(8,128)(2,1)S(1)} %collective-permute-done.11.refs_8_.refs_2_, bf16[2,2,2,256,1024]{4,3,2,1,0:T(8,128)(2,1)S(1)} %copy-done.2, ...), custom_call_target="tpu_custom_call" | custom-call | flops 1610612736 | bytes 8388608 | tf_op jit(solution)/shard_map/x_transform/pallas_call | solution.py:556
  63.1 1.7 %collective-permute-start.15 = (s16[528,256]{1,0:T(8,128)(2,1)S(1)}, s16[528,256]{1,0:T(8,128)(2,1)S(1)}, u32[]{:S(2)}, u32[]{:S(2)}) collective-permute-start(s16[528,256]{1,0:T(8,128)(2,1)S(1)} %get-tuple-element.106), channel_id=1, source_target_pairs={{0,2},{1,3},{2,0},{3,1},{4,6},{5,7},{6,4},{7,5},{8,10},{9,11},{10,... | collective-permute-start | bytes 811016 | tf_op jit(solution)/shard_map/ppermute | solution.py:571
  64.8 2.8 %x_transform.5.refs_4_ = f32[2,512,1024]{2,1,0:T(8,128)S(1)} custom-call(s32[4]{0:T(128)S(1)} %pad_add_fusion.1.place.refs_0_, s16[544,256]{1,0:T(8,128)(2,1)S(1)} %collective-permute-done.10.refs_7_.refs_1_, s16[192,256]{1,0:T(8,128)(2,1)S(1)} %collective-permute-done.12.refs_2_, s16[336,256]{1,0:T(8,128)(2,1)S(1)} %collective-permute-done.17.refs_3_, ...), custom_call_target="tpu_custom_call" | custom-call | flops 1610612736 | bytes 8388608 | tf_op jit(solution)/shard_map/x_transform/pallas_call | solution.py:556
  67.6 2.9 %x_transform.6.refs_4_ = f32[2,512,1024]{2,1,0:T(8,128)S(1)} custom-call(s32[4]{0:T(128)S(1)} %pad_add_fusion.1.place.refs_0_, s16[528,256]{1,0:T(8,128)(2,1)S(1)} %get-tuple-element.107.refs_1_, s16[528,256]{1,0:T(8,128)(2,1)S(1)} %collective-permute-done.16.refs_2_, bf16[2,2,2,256,1024]{4,3,2,1,0:T(8,128)(2,1)S(1)} %copy-done, ...), custom_call_target="tpu_custom_call" | custom-call | flops 1610612736 | bytes 8388608 | tf_op jit(solution)/shard_map/x_transform/pallas_call | solution.py:556
  70.5 1.9 %collective-permute-done.14.refs_1_ = s16[528,256]{1,0:T(8,128)(2,1)S(1)} collective-permute-done((s16[528,256]{1,0:T(8,128)(2,1)S(1)}, s16[528,256]{1,0:T(8,128)(2,1)S(1)}, u32[]{:S(2)}, u32[]{:S(2)}) %collective-permute-start.14) | collective-permute-done | bytes 270368 | tf_op jit(solution)/shard_map/ppermute | solution.py:571
  72.4 11.1 %collective-permute-done.15.refs_2_ = s16[528,256]{1,0:T(8,128)(2,1)S(1)} collective-permute-done((s16[528,256]{1,0:T(8,128)(2,1)S(1)}, s16[528,256]{1,0:T(8,128)(2,1)S(1)}, u32[]{:S(2)}, u32[]{:S(2)}) %collective-permute-start.15) | collective-permute-done | bytes 270368 | tf_op jit(solution)/shard_map/ppermute | solution.py:571
  83.5 4.9 %x_transform.7 = f32[8192,128]{1,0:T(8,128)} custom-call(s32[4]{0:T(128)S(1)} %pad_add_fusion.1.place.refs_0_, s16[528,256]{1,0:T(8,128)(2,1)S(1)} %collective-permute-done.14.refs_1_, s16[528,256]{1,0:T(8,128)(2,1)S(1)} %collective-permute-done.15.refs_2_, bf16[2,2,2,256,1024]{4,3,2,1,0:T(8,128)(2,1)S(1)} %copy-done, ...), custom_call_target="tpu_custom_call" | custom-call | flops 1610612736 | bytes 8388608 | tf_op jit(solution)/shard_map/x_transform/pallas_call | solution.py:556
  (39 shorter events, 5.1 us)
Async XLA Ops:
  3.3 10.8 %collective-permute-start.1 = (s16[272,256]{1,0:T(8,128)(2,1)S(1)}, s16[272,256]{1,0:T(8,128)(2,1)S(1)}, u32[]{:S(2)}, u32[]{:S(2)}) collective-permute-start(s16[272,256]{1,0:T(8,128)(2,1)S(1)} %get-tuple-element.75), channel_id=1, source_target_pairs={{0,8},{4,12},{8,0},{12,4},{16,24},{20,28},{24,16},{28,20},{1,9},{5... | collective-permute-start | bytes 417800 | tf_op jit(solution)/shard_map/ppermute | solution.py:571
  6.3 11.1 %collective-permute-start.3 = (s16[272,256]{1,0:T(8,128)(2,1)S(1)}, s16[272,256]{1,0:T(8,128)(2,1)S(1)}, u32[]{:S(2)}, u32[]{:S(2)}) collective-permute-start(s16[272,256]{1,0:T(8,128)(2,1)S(1)} %get-tuple-element.77), channel_id=1, source_target_pairs={{0,16},{4,20},{8,24},{12,28},{16,0},{20,4},{24,8},{28,12},{1,17},{... | collective-permute-start | bytes 417800 | tf_op jit(solution)/shard_map/ppermute | solution.py:571
  7.8 14.3 %collective-permute-start.5 = (s16[272,256]{1,0:T(8,128)(2,1)S(1)}, s16[272,256]{1,0:T(8,128)(2,1)S(1)}, u32[]{:S(2)}, u32[]{:S(2)}) collective-permute-start(s16[272,256]{1,0:T(8,128)(2,1)S(1)} %get-tuple-element.79), channel_id=1, source_target_pairs={{0,24},{4,28},{8,16},{12,20},{16,8},{20,12},{24,0},{28,4},{1,25},{... | collective-permute-start | bytes 417800 | tf_op jit(solution)/shard_map/ppermute | solution.py:571
  7.8 14.3 %collective-permute-start.6 = (s16[272,256]{1,0:T(8,128)(2,1)S(1)}, s16[272,256]{1,0:T(8,128)(2,1)S(1)}, u32[]{:S(2)}, u32[]{:S(2)}) collective-permute-start(s16[272,256]{1,0:T(8,128)(2,1)S(1)} %get-tuple-element.80), channel_id=1, source_target_pairs={{0,28},{4,24},{8,20},{12,16},{16,12},{20,8},{24,4},{28,0},{1,29},{... | collective-permute-start | bytes 417800 | tf_op jit(solution)/shard_map/ppermute | solution.py:571
  12.5 10.7 %copy-start.1 = (bf16[2,7,256,512]{3,2,1,0:T(8,128)(2,1)S(1)}, bf16[2,7,256,512]{3,2,1,0:T(8,128)(2,1)}, u32[]{:S(2)}) copy-start(bf16[2,7,256,512]{3,2,1,0:T(8,128)(2,1)} %constant.23.clone.refs_8_.refs_5_) | copy-start | bytes 11010052
  12.5 10.7 %copy-start.3 = (bf16[2,2,128,256]{3,2,1,0:T(8,128)(2,1)S(1)}, bf16[2,2,128,256]{3,2,1,0:T(8,128)(2,1)}, u32[]{:S(2)}) copy-start(bf16[2,2,128,256]{3,2,1,0:T(8,128)(2,1)} %constant.24.clone.refs_9_.refs_6_) | copy-start | bytes 786436
  12.5 9.6 %collective-permute-start = (s16[272,256]{1,0:T(8,128)(2,1)S(1)}, s16[272,256]{1,0:T(8,128)(2,1)S(1)}, u32[]{:S(2)}, u32[]{:S(2)}) collective-permute-start(s16[272,256]{1,0:T(8,128)(2,1)S(1)} %get-tuple-element.74), channel_id=1, source_target_pairs={{0,4},{4,0},{8,12},{12,8},{16,20},{20,16},{24,28},{28,24},{1,5},{5... | collective-permute-start | bytes 417800 | tf_op jit(solution)/shard_map/ppermute | solution.py:571
  14.1 8.1 %collective-permute-start.2 = (s16[272,256]{1,0:T(8,128)(2,1)S(1)}, s16[272,256]{1,0:T(8,128)(2,1)S(1)}, u32[]{:S(2)}, u32[]{:S(2)}) collective-permute-start(s16[272,256]{1,0:T(8,128)(2,1)S(1)} %get-tuple-element.76), channel_id=1, source_target_pairs={{0,12},{4,8},{8,4},{12,0},{16,28},{20,24},{24,20},{28,16},{1,13},{... | collective-permute-start | bytes 417800 | tf_op jit(solution)/shard_map/ppermute | solution.py:571
  17.4 5.9 %collective-permute-start.4 = (s16[272,256]{1,0:T(8,128)(2,1)S(1)}, s16[272,256]{1,0:T(8,128)(2,1)S(1)}, u32[]{:S(2)}, u32[]{:S(2)}) collective-permute-start(s16[272,256]{1,0:T(8,128)(2,1)S(1)} %get-tuple-element.78), channel_id=1, source_target_pairs={{0,20},{4,16},{8,28},{12,24},{16,4},{20,0},{24,12},{28,8},{1,21},{... | collective-permute-start | bytes 417800 | tf_op jit(solution)/shard_map/ppermute | solution.py:571
  27.5 8.4 %collective-permute-start.12 = (s16[192,256]{1,0:T(8,128)(2,1)S(1)}, s16[192,256]{1,0:T(8,128)(2,1)S(1)}, u32[]{:S(2)}, u32[]{:S(2)}) collective-permute-start(s16[192,256]{1,0:T(8,128)(2,1)S(1)} %get-tuple-element.95), channel_id=1, source_target_pairs={{0,2},{1,3},{2,0},{3,1},{4,6},{5,7},{6,4},{7,5},{8,10},{9,11},{10,... | collective-permute-start | bytes 294920 | tf_op jit(solution)/shard_map/ppermute | solution.py:571
  30.2 9.5 %collective-permute-start.7 = (s16[2,272,256]{2,1,0:T(8,128)(2,1)S(1)}, s16[2,272,256]{2,1,0:T(8,128)(2,1)S(1)}, u32[]{:S(2)}, u32[]{:S(2)}) collective-permute-start(s16[2,272,256]{2,1,0:T(8,128)(2,1)S(1)} %get-tuple-element.82), channel_id=1, source_target_pairs={{0,8},{4,12},{8,0},{12,4},{16,24},{20,28},{24,16},{28,20},{1,9},{5... | collective-permute-start | bytes 835592 | tf_op jit(solution)/shard_map/ppermute | solution.py:571
  30.2 15.1 %collective-permute-start.8 = (s16[2,272,256]{2,1,0:T(8,128)(2,1)S(1)}, s16[2,272,256]{2,1,0:T(8,128)(2,1)S(1)}, u32[]{:S(2)}, u32[]{:S(2)}) collective-permute-start(s16[2,272,256]{2,1,0:T(8,128)(2,1)S(1)} %get-tuple-element.83), channel_id=1, source_target_pairs={{0,16},{4,20},{8,24},{12,28},{16,0},{20,4},{24,8},{28,12},{1,17},{... | collective-permute-start | bytes 835592 | tf_op jit(solution)/shard_map/ppermute | solution.py:571
  31.2 14.1 %collective-permute-start.9 = (s16[2,272,256]{2,1,0:T(8,128)(2,1)S(1)}, s16[2,272,256]{2,1,0:T(8,128)(2,1)S(1)}, u32[]{:S(2)}, u32[]{:S(2)}) collective-permute-start(s16[2,272,256]{2,1,0:T(8,128)(2,1)S(1)} %get-tuple-element.84), channel_id=1, source_target_pairs={{0,24},{4,28},{8,16},{12,20},{16,8},{20,12},{24,0},{28,4},{1,25},{... | collective-permute-start | bytes 835592 | tf_op jit(solution)/shard_map/ppermute | solution.py:571
  33.6 14.1 %collective-permute-start.10 = (s16[544,256]{1,0:T(8,128)(2,1)S(1)}, s16[544,256]{1,0:T(8,128)(2,1)S(1)}, u32[]{:S(2)}, u32[]{:S(2)}) collective-permute-start(s16[544,256]{1,0:T(8,128)(2,1)S(1)} %get-tuple-element.93), channel_id=1, source_target_pairs={{0,1},{1,0},{2,3},{3,2},{4,5},{5,4},{6,7},{7,6},{8,9},{9,8},{10,11... | collective-permute-start | bytes 835592 | tf_op jit(solution)/shard_map/ppermute | solution.py:571
  35.9 22.8 %copy-start.2 = (bf16[2,2,2,256,1024]{4,3,2,1,0:T(8,128)(2,1)S(1)}, bf16[2,2,2,256,1024]{4,3,2,1,0:T(8,128)(2,1)}, u32[]{:S(2)}) copy-start(bf16[2,2,2,256,1024]{4,3,2,1,0:T(8,128)(2,1)} %constant.25.clone.refs_3_.refs_4_) | copy-start | bytes 12582916
  35.9 22.8 %copy-start.4 = (s32[8]{0:T(128)S(1)}, s32[8]{0:T(128)}, u32[]{:S(2)}) copy-start(s32[8]{0:T(128)} %refs_4_.2) | copy-start | bytes 100
  35.9 22.8 %copy-start.5 = (f32[2,1024]{1,0:T(2,128)S(1)}, f32[2,1024]{1,0:T(2,128)}, u32[]{:S(2)}) copy-start(f32[2,1024]{1,0:T(2,128)} %constant.26.clone.refs_5_) | copy-start | bytes 24580
  35.9 11.9 %collective-permute-start.11 = (s16[544,256]{1,0:T(8,128)(2,1)S(1)}, s16[544,256]{1,0:T(8,128)(2,1)S(1)}, u32[]{:S(2)}, u32[]{:S(2)}) collective-permute-start(s16[544,256]{1,0:T(8,128)(2,1)S(1)} %get-tuple-element.94), channel_id=1, source_target_pairs={{0,3},{1,2},{2,1},{3,0},{4,7},{5,6},{6,5},{7,4},{8,11},{9,10},{10,... | collective-permute-start | bytes 835592 | tf_op jit(solution)/shard_map/ppermute | solution.py:571
  47.9 3.3 %collective-permute-start.13 = (s16[4,272,256]{2,1,0:T(8,128)(2,1)S(1)}, s16[4,272,256]{2,1,0:T(8,128)(2,1)S(1)}, u32[]{:S(2)}, u32[]{:S(2)}) collective-permute-start(s16[4,272,256]{2,1,0:T(8,128)(2,1)S(1)} %pad_add_fusion), channel_id=1, source_target_pairs={{0,4},{4,0},{8,12},{12,8},{16,20},{20,16},{24,28},{28,24},{1,5},{5... | collective-permute-start | bytes 1671176 | tf_op jit(solution)/shard_map/ppermute | solution.py:571
  48.0 16.8 %collective-permute-start.17 = (s16[336,256]{1,0:T(8,128)(2,1)S(1)}, s16[336,256]{1,0:T(8,128)(2,1)S(1)}, u32[]{:S(2)}, u32[]{:S(2)}) collective-permute-start(s16[336,256]{1,0:T(8,128)(2,1)S(1)} %get-tuple-element.110), channel_id=1, source_target_pairs={{0,2},{1,3},{2,0},{3,1},{4,6},{5,7},{6,4},{7,5},{8,10},{9,11},{10,... | collective-permute-start | bytes 516104 | tf_op jit(solution)/shard_map/ppermute | solution.py:571
  55.9 11.7 %collective-permute-start.16 = (s16[528,256]{1,0:T(8,128)(2,1)S(1)}, s16[528,256]{1,0:T(8,128)(2,1)S(1)}, u32[]{:S(2)}, u32[]{:S(2)}) collective-permute-start(s16[528,256]{1,0:T(8,128)(2,1)S(1)} %get-tuple-element.108), channel_id=1, source_target_pairs={{0,3},{1,2},{2,1},{3,0},{4,7},{5,6},{6,5},{7,4},{8,11},{9,10},{10,... | collective-permute-start | bytes 811016 | tf_op jit(solution)/shard_map/ppermute | solution.py:571
  63.0 9.5 %collective-permute-start.14 = (s16[528,256]{1,0:T(8,128)(2,1)S(1)}, s16[528,256]{1,0:T(8,128)(2,1)S(1)}, u32[]{:S(2)}, u32[]{:S(2)}) collective-permute-start(s16[528,256]{1,0:T(8,128)(2,1)S(1)} %get-tuple-element.102), channel_id=1, source_target_pairs={{0,1},{1,0},{2,3},{3,2},{4,5},{5,4},{6,7},{7,6},{8,9},{9,8},{10,11... | collective-permute-start | bytes 811016 | tf_op jit(solution)/shard_map/ppermute | solution.py:571
  63.0 4.5 %copy-start = (bf16[2,2,2,256,1024]{4,3,2,1,0:T(8,128)(2,1)S(1)}, bf16[2,2,2,256,1024]{4,3,2,1,0:T(8,128)(2,1)}, u32[]{:S(2)}) copy-start(bf16[2,2,2,256,1024]{4,3,2,1,0:T(8,128)(2,1)} %constant.27.clone.refs_3_) | copy-start | bytes 12582916
  63.1 20.4 %collective-permute-start.15 = (s16[528,256]{1,0:T(8,128)(2,1)S(1)}, s16[528,256]{1,0:T(8,128)(2,1)S(1)}, u32[]{:S(2)}, u32[]{:S(2)}) collective-permute-start(s16[528,256]{1,0:T(8,128)(2,1)S(1)} %get-tuple-element.106), channel_id=1, source_target_pairs={{0,2},{1,3},{2,0},{3,1},{4,6},{5,7},{6,4},{7,5},{8,10},{9,11},{10,... | collective-permute-start | bytes 811016 | tf_op jit(solution)/shard_map/ppermute | solution.py:571

commit v4 on v3

--- a/solution.py
+++ b/solution.py
@@ -405,6 +405,8 @@
         result[r] = value
     if gives_edge:
         outs = [outs[0], outs[1], (outs[2], outs[4]), outs[3]]
+    else:
+        last_two, outs = (outs[2], outs[4]), outs[:4]
     share = half // len(outs)
     per = share // GROUP
     for e, out in enumerate(outs):
@@ -414,10 +416,18 @@
             values = result[r, pl.ds(first, share), :].reshape(per, GROUP, chunk)
             codes, steps, _ = encoded(values)
             ref, first_row = part_of(out, r * share, CUT * share)
+            if not gives_edge and e == 2:
+                ref, first_row = last_two[r // BLOCKS], r % BLOCKS * share
             ref[first_row : first_row + share, :] = codes.reshape(share, chunk).astype(jnp.int16)
             metas.append(steps)
         if gives_edge and e % 2:
             metas.append(edges[...])
+        if not gives_edge and e == 2:
+            unused = jnp.zeros((META - BLOCKS, chunk), jnp.float32)
+            for n, ref in enumerate(last_two):
+                meta = jnp.concatenate([*metas[n * BLOCKS : (n + 1) * BLOCKS], unused], axis=0)
+                ref[BLOCKS * share :, :] = meta.astype(jnp.int32).astype(jnp.int16)
+            continue
         ref, first_row = part_of(out, RESIDUES * share, CUT * share)
         ref[first_row:, :] = jnp.concatenate(metas, axis=0).astype(jnp.int32).astype(jnp.int16)
 
@@ -430,6 +440,8 @@
     if not neighbours:
         share = length // RESIDUES // x_count
         out_rows = [*out_rows[:2], CUT * share, out_rows[3], out_rows[2] - CUT * share]
+    else:
+        out_rows = [*out_rows[:2], (out_rows[2] + META) // 2, out_rows[3], (out_rows[2] + META) // 2]
     vmem = pl.BlockSpec(memory_space=pltpu.VMEM)
     return pl.pallas_call(
         functools.partial(z_kernel, not neighbours),
@@ -450,7 +462,7 @@
     )(place, *pieces, *tables, *neighbours)
 
 
-def x_kernel(stage, pairs, halved, *refs):
+def x_kernel(stage, pairs, halved, side_rows, *refs):
     place = refs[0]
     refs = list(refs[1:])
     pieces = [[(refs.pop(0), refs.pop(0)) if e in halved else refs.pop(0) for e in pair] for pair in pairs]
@@ -458,26 +470,31 @@
     if stage == "first":
         frequency, col_part, out, factor_out, values, high, low = refs[1:]
     elif stage == "last":
-        total, factor, out, values, high, low, finished, sent = refs[1:]
+        total, factor, *refs = refs[1:]
+        out, values, high, low, finished, copied = refs[-6:]
     else:
         total, out, values, high, low = refs[1:]
     x_rank, x_count = place[2], 4
     rows, chunk = values.shape[3], values.shape[2] * LANES
-    share = rows // RESIDUES
+    residues = range(RESIDUES) if side_rows is None else range(side_rows * BLOCKS, (side_rows + 1) * BLOCKS)
+    share = rows // len(residues)
     per = share // GROUP
     lefts = []
     for i, pair in enumerate(pairs):
         for piece, e in zip(pieces[i], pair):
             source = x_rank ^ e
             side = jnp.where(source >= x_count // 2, 1, 0)
-            ref, first_row = part_of(piece, rows, CUT * share)
+            short = side_rows is not None and e == pair[1]
+            ref, first_row = part_of(piece, BLOCKS * share if short else RESIDUES * share, CUT * share)
             steps = ref[first_row : first_row + META, :].astype(jnp.int32).astype(jnp.float32)
-            for r in range(RESIDUES):
-                ref, first_row = part_of(piece, r * share, CUT * share)
-                part, _ = decoded(ref[first_row : first_row + share, :], steps[r * per : (r + 1) * per])
+            for i_r, r in enumerate(residues):
+                at = i_r if short else r
+                ref, first_row = part_of(piece, at * share, CUT * share)
+                part, _ = decoded(ref[first_row : first_row + share, :], steps[at * per : (at + 1) * per])
                 part = part.reshape(share, chunk)
                 for t in range(chunk // LANES):
-                    values[i, side, t, pl.ds(r, share, stride=RESIDUES), :] = part[:, t * LANES : (t + 1) * LANES]
+                    start = i_r // BLOCKS * (BLOCKS * share) + i_r % BLOCKS
+                    values[i, side, t, pl.ds(start, share, stride=BLOCKS), :] = part[:, t * LANES : (t + 1) * LANES]
         left = x_rank ^ pair[0]
         lefts.append(jnp.minimum(left, x_count - 1 - left))
         for t in range(chunk // LANES):
@@ -490,20 +507,25 @@
     if stage == "first":
         turn = jnp.full((8, LANES), frequency[place[0]], jnp.int32).astype(jnp.float32)
         sine = jnp.sin(turn * (math.pi / (2 * NY)))[:1]
-        kz_index = x_rank * rows + lax.broadcasted_iota(jnp.int32, (rows, LANES), 0)
+        half_row = lax.broadcasted_iota(jnp.int32, (rows // 2, LANES), 0)
+        half_kz = x_rank * rows + half_row + BLOCKS * lax.shift_right_logical(half_row, 3)
+        kz_index = jnp.concatenate([half_kz, half_kz + BLOCKS], axis=0)
         row_part = -(4.0 * sine * sine + eigenvalue(kz_index, rows * x_count) + SCREEN_WEIGHT)
     dot = functools.partial(jnp.dot, preferred_element_type=jnp.float32)
     count = table.shape[4]
     width = 256
     per_row = 2 * count // LANES
-    bands = 4 if stage == "last" else 1
+    copies = []
+    bands = finished.shape[0] if stage == "last" else 1
     band = rows // bands
     for n in range(bands):
         here = slice(n * band, (n + 1) * band)
+        if stage == "last":
+            there = slice(side_rows * rows + n * band, side_rows * rows + (n + 1) * band)
         for p in range(2):
             for c in range(count // width):
                 cols = slice(c * width, (c + 1) * width)
-                value = None if stage == "first" else total[p, here, cols]
+                value = None if stage == "first" else total[p, there if stage == "last" else here, cols]
                 for i, left in enumerate(lefts):
                     for data, level in ((high, 0), (low, 0), (high, 1)):
                         term = dot(data[i, p, here, :], table[level, p, left, :, cols])
@@ -514,27 +536,36 @@
                 if stage != "last":
                     out[p, :, cols] = value
                     continue
-                value *= factor[p, here, cols]
+                value *= factor[p, there, cols]
                 for t in range(width // LANES):
                     tile = c * (width // LANES) + t
                     part = value[:, t * LANES : (t + 1) * LANES]
                     finished[n, pl.ds(2 * tile + p, band, stride=per_row), :] = part
         if stage == "last":
-            lines = pl.ds(n * band * per_row, band * per_row)
-            pltpu.make_async_copy(finished.at[n], out.at[lines], sent.at[n]).start()
-    if stage == "last":
-        for n in range(bands):
-            lines = pl.ds(n * band * per_row, band * per_row)
-            pltpu.make_async_copy(finished.at[n], out.at[lines], sent.at[n]).wait()
-
-
-def x_transform(stage, place, pairs, pieces, table, extra):
+            block = BLOCKS * per_row
+            for m in range(band // BLOCKS):
+                to = pl.ds((2 * (n * (band // BLOCKS) + m) + side_rows) * block, block)
+                source = finished.at[n, pl.ds(m * block, block)]
+                copies.append(pltpu.make_async_copy(source, out.at[to], copied.at[len(copies)]))
+                copies[-1].start()
+    for copy in copies:
+        copy.wait()
+
+
+def x_transform(stage, place, pairs, pieces, table, extra, side_rows=None, written=None):
     halved = [e for e in pieces if isinstance(pieces[e], tuple)]
     chosen = []
     for pair in pairs:
         for e in pair:
             chosen += pieces[e] if e in halved else [pieces[e]]
     rows = pieces[0].shape[0] - META
+    line_count = rows * 2 * table.shape[4] // LANES
+    aliases = {}
+    if stage == "last":
+        rows //= 2
+    if written is not None:
+        extra = (*extra, written)
+        aliases = {1 + len(chosen) + 1 + 2: 0}
     chunk = chosen[0].shape[1]
     count = table.shape[4]
     vmem = pl.BlockSpec(memory_space=pltpu.VMEM)
@@ -549,15 +580,17 @@
     if stage == "first":
         out_shape, out_specs = [sums, sums], [vmem, vmem]
     elif stage == "last":
-        lines = rows * 2 * count // LANES
-        out_shape = jax.ShapeDtypeStruct((lines, LANES), jnp.float32)
+        out_shape = jax.ShapeDtypeStruct((line_count, LANES), jnp.float32)
         out_specs = pl.BlockSpec(memory_space=pltpu.HBM)
-        scratch += [pltpu.VMEM((4, lines // 4, LANES), jnp.float32), pltpu.SemaphoreType.DMA((4,))]
+        bands = 2
+        scratch += [pltpu.VMEM((bands, line_count // 2 // bands, LANES), jnp.float32)]
+        scratch += [pltpu.SemaphoreType.DMA((rows // BLOCKS,))]
     return pl.pallas_call(
-        functools.partial(x_kernel, stage, pairs, halved),
-        in_specs=[smem] + [vmem] * (len(chosen) + 1) + ([smem, vmem] if stage == "first" else [vmem] * len(extra)),
+        functools.partial(x_kernel, stage, pairs, halved, side_rows),
+        in_specs=[smem] + [vmem] * (len(chosen) + 1) + ([smem, vmem] if stage == "first" else [vmem] * min(len(extra), 2) + [out_specs] * len(aliases)),
         out_specs=out_specs,
         out_shape=out_shape,
+        input_output_aliases=aliases,
         scratch_shapes=scratch,
         compiler_params=pltpu.CompilerParams(vmem_limit_bytes=SCOPED),
         cost_estimate=pl.CostEstimate(
@@ -604,7 +637,7 @@
     first[4] = sent(first[4], "xy", 2)
     second.append(sent(jnp.concatenate([a[1:] for a in second], axis=0), "gz", 1))
     second = z_transform(place, second, tables_z, x_count, (first[1], first[3]))
-    later = second[2]
+    later, latest = second[2], second[4]
     second = {0: second[0]} | {e: sent(second[e], "xy", e) for e in (3, 1)}
     kz_count = length_z // x_count
     halved = length_x // 2
@@ -619,7 +652,11 @@
     second |= {2: sent(later, "xy", 2)}
     total = x_transform("more", place, (inside,), first, inner_table, (total,))
     total = x_transform("more", place, (outside,), second, outer_table, (total,))
-    flat = x_transform("last", place, (inside,), second, outer_table, (total, factor))
+    latest, total = lax.optimization_barrier((latest, total))
+    latest = sent(latest, "xy", 2)
+    flat = x_transform("last", place, (inside,), second, outer_table, (total, factor), 0)
+    second[2] = latest
+    flat = x_transform("last", place, (inside,), second, outer_table, (total, factor), 1, flat)
     tiles = halved // LANES
     return flat.reshape(1, kz_count, tiles, 2, LANES).transpose(0, 1, 3, 2, 4).reshape(1, kz_count, 2, halved)
 

time: 88.7 us -> 87.5 us (0.986)
  waiting for transfers between devices: 26.1 us -> 16.3 us
  starting transfers between devices: 26.9 us -> 34.2 us
  Pallas kernels: 35 us -> 36.4 us
    ppermute x18 -> x19, waiting for transfers between devices: 26.1 us -> 16.3 us  [sent(): lax.ppermute(piece, axis, [(i, i ^ d) for i in range(lax.axis_size(axis))])]
    ppermute x18 -> x19, starting transfers between devices: 26.9 us -> 34.2 us  [sent(): lax.ppermute(piece, axis, [(i, i ^ d) for i in range(lax.axis_size(axis))])]
    pallas_call x4 -> x5, Pallas kernels: 14.9 us -> 16.3 us  [x_transform(): pl.pallas_call(functools.partial(x_kernel, stage, pairs, halved, side_row...]
  transfers between devices with their start and end apart: 18 -> 19, of which waited for: 8 -> 8; matrix products, arithmetic and copies ran while one was open for 0% -> 0% of each run, Pallas kernels for 26% -> 29%
where the time goes in v4:
time: 87.5 us; the launch traced here: 87.4 us
  Pallas kernels  36.4 us (42%)
  starting transfers between devices  34.2 us (39%)
  waiting for transfers between devices  16.3 us (19%)
    ppermute x19, starting transfers between devices, sent(): lax.ppermute(piece, axis, [(i, i ^ d) for i in range(lax.axis_size(axis))])  34.2 us
    pallas_call x5, Pallas kernels, x_transform(): pl.pallas_call(functools.partial(x_kernel, stage, pairs, halved, side_row...  16.3 us
    ppermute x19, waiting for transfers between devices, sent(): lax.ppermute(piece, axis, [(i, i ^ d) for i in range(lax.axis_size(axis))])  16.3 us
    pallas_call x3, Pallas kernels, divergence(): pl.pallas_call(functools.partial(divergence_kernel, tiles, spans, order,...  11.1 us
    pallas_call x2, Pallas kernels, z_transform(): pl.pallas_call(functools.partial(z_kernel, not neighbours), in_specs=[pl....  8.98 us
  transfers between devices with their start and end apart: 19, of which 8 were waited for; matrix products, arithmetic and copies ran while one was open for 0% of the time, Pallas kernels for 29%

profile of v4, /device:TPU:0, one launch (start us, length us, event | category | flops | bytes accessed | tf_op | source)
XLA Modules:
  0.0 87.4 jit_solution(10001883906686166040)
XLA Ops:
  0.1 3.2 %divergence.3 = (s16[272,256]{1,0:T(8,128)(2,1)S(1)}, s16[272,256]{1,0:T(8,128)(2,1)S(1)}, s16[272,256]{1,0:T(8,128)(2,1)S(1)}, s16[272,256]{1,0:T(8,128)(2,1)S(1)}) custom-call(s32[4]{0:T(128)S(1)} %pad_add_fusion.1.place.refs_0_, s32[8]{0:T(128)} %refs_4_.2, bf16[8,256,512]{2,1,0:T(8,128)(2,1)} %flux_x.5, bf16[8,256,512]{2,1,0:T(8,128)(2,1)} %flux_y.5, ...), custom_call_target="tpu_custom_call" | custom-call | bytes 11808000 | tf_op jit(solution)/shard_map/divergence/pallas_call | solution.py:284
  3.3 3.0 %collective-permute-start.1 = (s16[272,256]{1,0:T(8,128)(2,1)S(1)}, s16[272,256]{1,0:T(8,128)(2,1)S(1)}, u32[]{:S(2)}, u32[]{:S(2)}) collective-permute-start(s16[272,256]{1,0:T(8,128)(2,1)S(1)} %get-tuple-element.78), channel_id=1, source_target_pairs={{0,8},{4,12},{8,0},{12,4},{16,24},{20,28},{24,16},{28,20},{1,9},{5... | collective-permute-start | bytes 417800 | tf_op jit(solution)/shard_map/ppermute | solution.py:604
  9.3 3.2 %divergence.4 = (s16[272,256]{1,0:T(8,128)(2,1)S(1)}, s16[272,256]{1,0:T(8,128)(2,1)S(1)}, s16[272,256]{1,0:T(8,128)(2,1)S(1)}, s16[272,256]{1,0:T(8,128)(2,1)S(1)}) custom-call(s32[4]{0:T(128)S(1)} %pad_add_fusion.1.place.refs_0_, s32[8]{0:T(128)} %refs_4_.2, bf16[8,256,512]{2,1,0:T(8,128)(2,1)} %flux_x.5, bf16[8,256,512]{2,1,0:T(8,128)(2,1)} %flux_y.5, ...), custom_call_target="tpu_custom_call" | custom-call | bytes 11808000 | tf_op jit(solution)/shard_map/divergence/pallas_call | solution.py:284
  12.5 1.6 %collective-permute-start = (s16[272,256]{1,0:T(8,128)(2,1)S(1)}, s16[272,256]{1,0:T(8,128)(2,1)S(1)}, u32[]{:S(2)}, u32[]{:S(2)}) collective-permute-start(s16[272,256]{1,0:T(8,128)(2,1)S(1)} %get-tuple-element.77), channel_id=1, source_target_pairs={{0,4},{4,0},{8,12},{12,8},{16,20},{20,16},{24,28},{28,24},{1,5},{5... | collective-permute-start | bytes 417800 | tf_op jit(solution)/shard_map/ppermute | solution.py:604
  14.4 3.0 %collective-permute-done.3.refs_4_ = s16[272,256]{1,0:T(8,128)(2,1)S(1)} collective-permute-done((s16[272,256]{1,0:T(8,128)(2,1)S(1)}, s16[272,256]{1,0:T(8,128)(2,1)S(1)}, u32[]{:S(2)}, u32[]{:S(2)}) %collective-permute-start.3) | collective-permute-done | bytes 139296 | tf_op jit(solution)/shard_map/ppermute | solution.py:604
  17.4 4.8 %divergence.5 = (s16[2,272,256]{2,1,0:T(8,128)(2,1)S(1)}, s16[2,272,256]{2,1,0:T(8,128)(2,1)S(1)}, s16[2,272,256]{2,1,0:T(8,128)(2,1)S(1)}, s16[2,272,256]{2,1,0:T(8,128)(2,1)S(1)}) custom-call(s32[4]{0:T(128)S(1)} %pad_add_fusion.1.place.refs_0_, s32[8]{0:T(128)} %refs_4_.2, bf16[8,256,512]{2,1,0:T(8,128)(2,1)} %flux_x.5, bf16[8,256,512]{2,1,0:T(8,128)(2,1)} %flux_y.5, ...), custom_call_target="tpu_custom_call" | custom-call | bytes 19188000 | tf_op jit(solution)/shard_map/divergence/pallas_call | solution.py:284
  23.3 4.2 %z_transform.2 = (s16[528,256]{1,0:T(8,128)(2,1)S(1)}, s16[544,256]{1,0:T(8,128)(2,1)S(1)}, s16[192,256]{1,0:T(8,128)(2,1)S(1)}, s16[544,256]{1,0:T(8,128)(2,1)S(1)}, s16[336,256]{1,0:T(8,128)(2,1)S(1)}) custom-call(s32[4]{0:T(128)S(1)} %pad_add_fusion.1.place.refs_0_, s16[272,256]{1,0:T(8,128)(2,1)S(1)} %get-tuple-element.88.refs_0_, ...), custom_call_target="tpu_custom_call" | custom-call | bytes 15498000 | tf_op jit(solution)/shard_map/z_transform/pallas_call | solution.py:446
  27.5 2.6 %collective-permute-start.12 = (s16[192,256]{1,0:T(8,128)(2,1)S(1)}, s16[192,256]{1,0:T(8,128)(2,1)S(1)}, u32[]{:S(2)}, u32[]{:S(2)}) collective-permute-start(s16[192,256]{1,0:T(8,128)(2,1)S(1)} %get-tuple-element.98), channel_id=1, source_target_pairs={{0,2},{1,3},{2,0},{3,1},{4,6},{5,7},{6,4},{7,5},{8,10},{9,11},{10,... | collective-permute-start | bytes 294920 | tf_op jit(solution)/shard_map/ppermute | solution.py:604
  31.2 2.5 %collective-permute-start.9 = (s16[2,272,256]{2,1,0:T(8,128)(2,1)S(1)}, s16[2,272,256]{2,1,0:T(8,128)(2,1)S(1)}, u32[]{:S(2)}, u32[]{:S(2)}) collective-permute-start(s16[2,272,256]{2,1,0:T(8,128)(2,1)S(1)} %get-tuple-element.87), channel_id=1, source_target_pairs={{0,24},{4,28},{8,16},{12,20},{16,8},{20,12},{24,0},{28,4},{1,25},{... | collective-permute-start | bytes 835592 | tf_op jit(solution)/shard_map/ppermute | solution.py:604
  33.6 1.6 %collective-permute-start.10 = (s16[544,256]{1,0:T(8,128)(2,1)S(1)}, s16[544,256]{1,0:T(8,128)(2,1)S(1)}, u32[]{:S(2)}, u32[]{:S(2)}) collective-permute-start(s16[544,256]{1,0:T(8,128)(2,1)S(1)} %get-tuple-element.96), channel_id=1, source_target_pairs={{0,1},{1,0},{2,3},{3,2},{4,5},{5,4},{6,7},{7,6},{8,9},{9,8},{10,11... | collective-permute-start | bytes 835592 | tf_op jit(solution)/shard_map/ppermute | solution.py:604
  35.9 3.6 %collective-permute-start.11 = (s16[544,256]{1,0:T(8,128)(2,1)S(1)}, s16[544,256]{1,0:T(8,128)(2,1)S(1)}, u32[]{:S(2)}, u32[]{:S(2)}) collective-permute-start(s16[544,256]{1,0:T(8,128)(2,1)S(1)} %get-tuple-element.97), channel_id=1, source_target_pairs={{0,3},{1,2},{2,1},{3,0},{4,7},{5,6},{6,5},{7,4},{8,11},{9,10},{10,... | collective-permute-start | bytes 835592 | tf_op jit(solution)/shard_map/ppermute | solution.py:604
  39.6 5.6 %collective-permute-done.8.refs_2_ = s16[2,272,256]{2,1,0:T(8,128)(2,1)S(1)} collective-permute-done((s16[2,272,256]{2,1,0:T(8,128)(2,1)S(1)}, s16[2,272,256]{2,1,0:T(8,128)(2,1)S(1)}, u32[]{:S(2)}, u32[]{:S(2)}) %collective-permute-start.8) | collective-permute-done | bytes 278560 | tf_op jit(solution)/shard_map/ppermute | solution.py:604
  45.2 2.5 %collective-permute-done.10.refs_7_.refs_1_ = s16[544,256]{1,0:T(8,128)(2,1)S(1)} collective-permute-done((s16[544,256]{1,0:T(8,128)(2,1)S(1)}, s16[544,256]{1,0:T(8,128)(2,1)S(1)}, u32[]{:S(2)}, u32[]{:S(2)}) %collective-permute-start.10) | collective-permute-done | bytes 278560 | tf_op jit(solution)/shard_map/ppermute | solution.py:604
  48.0 3.2 %collective-permute-start.16 = (s16[336,256]{1,0:T(8,128)(2,1)S(1)}, s16[336,256]{1,0:T(8,128)(2,1)S(1)}, u32[]{:S(2)}, u32[]{:S(2)}) collective-permute-start(s16[336,256]{1,0:T(8,128)(2,1)S(1)} %get-tuple-element.110), channel_id=1, source_target_pairs={{0,2},{1,3},{2,0},{3,1},{4,6},{5,7},{6,4},{7,5},{8,10},{9,11},{10,... | collective-permute-start | bytes 516104 | tf_op jit(solution)/shard_map/ppermute | solution.py:604
  51.2 4.7 %z_transform.3 = (s16[528,256]{1,0:T(8,128)(2,1)S(1)}, s16[528,256]{1,0:T(8,128)(2,1)S(1)}, s16[272,256]{1,0:T(8,128)(2,1)S(1)}, s16[528,256]{1,0:T(8,128)(2,1)S(1)}, s16[272,256]{1,0:T(8,128)(2,1)S(1)}) custom-call(s32[4]{0:T(128)S(1)} %pad_add_fusion.1.place.refs_0_, s16[2,272,256]{2,1,0:T(8,128)(2,1)S(1)} %get-tuple-element.99.refs_0_, ...), custom_call_target="tpu_custom_call" | custom-call | bytes 15498000 | tf_op jit(solution)/shard_map/z_transform/pallas_call | solution.py:446
  55.9 2.7 %collective-permute-start.15 = (s16[528,256]{1,0:T(8,128)(2,1)S(1)}, s16[528,256]{1,0:T(8,128)(2,1)S(1)}, u32[]{:S(2)}, u32[]{:S(2)}) collective-permute-start(s16[528,256]{1,0:T(8,128)(2,1)S(1)} %get-tuple-element.108), channel_id=1, source_target_pairs={{0,3},{1,2},{2,1},{3,0},{4,7},{5,6},{6,5},{7,4},{8,11},{9,10},{10,... | collective-permute-start | bytes 811016 | tf_op jit(solution)/shard_map/ppermute | solution.py:604
  58.7 4.1 %x_transform.5 = (f32[2,512,1024]{2,1,0:T(8,128)S(1)}, f32[2,512,1024]{2,1,0:T(8,128)S(1)}) custom-call(s32[4]{0:T(128)S(1)} %pad_add_fusion.1.place.refs_0_, s16[528,256]{1,0:T(8,128)(2,1)S(1)} %get-tuple-element.112.refs_1_, s16[544,256]{1,0:T(8,128)(2,1)S(1)} %collective-permute-done.11.refs_8_.refs_2_, bf16[2,2,2,256,1024]{4,3,2,1,0:T(8,128)(2,1)S(1)} %copy-done.2, ...), custom_call_target="tpu_custom_call" | custom-call | flops 1610612736 | bytes 8388608 | tf_op jit(solution)/shard_map/x_transform/pallas_call | solution.py:588
  62.9 1.7 %collective-permute-start.18 = (s16[272,256]{1,0:T(8,128)(2,1)S(1)}, s16[272,256]{1,0:T(8,128)(2,1)S(1)}, u32[]{:S(2)}, u32[]{:S(2)}) collective-permute-start(s16[272,256]{1,0:T(8,128)(2,1)S(1)} %get-tuple-element.118), channel_id=1, source_target_pairs={{0,2},{1,3},{2,0},{3,1},{4,6},{5,7},{6,4},{7,5},{8,10},{9,11},{10,... | collective-permute-start | bytes 417800 | tf_op jit(solution)/shard_map/ppermute | solution.py:604
  64.6 2.7 %x_transform.6.refs_4_ = f32[2,512,1024]{2,1,0:T(8,128)S(1)} custom-call(s32[4]{0:T(128)S(1)} %pad_add_fusion.1.place.refs_0_, s16[544,256]{1,0:T(8,128)(2,1)S(1)} %collective-permute-done.10.refs_7_.refs_1_, s16[192,256]{1,0:T(8,128)(2,1)S(1)} %collective-permute-done.12.refs_2_, s16[336,256]{1,0:T(8,128)(2,1)S(1)} %collective-permute-done.16.refs_3_, ...), custom_call_target="tpu_custom_call" | custom-call | flops 1610612736 | bytes 8388608 | tf_op jit(solution)/shard_map/x_transform/pallas_call | solution.py:588
  67.3 2.7 %x_transform.7.refs_4_ = f32[2,512,1024]{2,1,0:T(8,128)S(1)} custom-call(s32[4]{0:T(128)S(1)} %pad_add_fusion.1.place.refs_0_, s16[528,256]{1,0:T(8,128)(2,1)S(1)} %get-tuple-element.107.refs_1_, s16[528,256]{1,0:T(8,128)(2,1)S(1)} %collective-permute-done.15.refs_2_, bf16[2,2,2,256,1024]{4,3,2,1,0:T(8,128)(2,1)S(1)} %copy-done, ...), custom_call_target="tpu_custom_call" | custom-call | flops 1610612736 | bytes 8388608 | tf_op jit(solution)/shard_map/x_transform/pallas_call | solution.py:588
  70.0 7.3 %collective-permute-start.17 = (s16[272,256]{1,0:T(8,128)(2,1)S(1)}, s16[272,256]{1,0:T(8,128)(2,1)S(1)}, u32[]{:S(2)}, u32[]{:S(2)}) collective-permute-start(s16[272,256]{1,0:T(8,128)(2,1)S(1)} %get-tuple-element.115), channel_id=1, source_target_pairs={{0,2},{1,3},{2,0},{3,1},{4,6},{5,7},{6,4},{7,5},{8,10},{9,11},{10,... | collective-permute-start | bytes 417800 | tf_op jit(solution)/shard_map/ppermute | solution.py:604
  77.3 2.4 %collective-permute-done.18.refs_2_ = s16[272,256]{1,0:T(8,128)(2,1)S(1)} collective-permute-done((s16[272,256]{1,0:T(8,128)(2,1)S(1)}, s16[272,256]{1,0:T(8,128)(2,1)S(1)}, u32[]{:S(2)}, u32[]{:S(2)}) %collective-permute-start.18) | collective-permute-done | bytes 139296 | tf_op jit(solution)/shard_map/ppermute | solution.py:604
  79.7 3.4 %x_transform.8.refs_6_ = f32[8192,128]{1,0:T(8,128)} custom-call(s32[4]{0:T(128)S(1)} %pad_add_fusion.1.place.refs_0_, s16[528,256]{1,0:T(8,128)(2,1)S(1)} %collective-permute-done.14.refs_1_, s16[272,256]{1,0:T(8,128)(2,1)S(1)} %collective-permute-done.18.refs_2_, bf16[2,2,2,256,1024]{4,3,2,1,0:T(8,128)(2,1)S(1)} %copy-done, ...), custom_call_target="tpu_custom_call" | custom-call | flops 805306368 | bytes 4194304 | tf_op jit(solution)/shard_map/x_transform/pallas_call | solution.py:588
  83.8 3.4 %x_transform.9 = f32[8192,128]{1,0:T(8,128)} custom-call(s32[4]{0:T(128)S(1)} %pad_add_fusion.1.place.refs_0_, s16[528,256]{1,0:T(8,128)(2,1)S(1)} %collective-permute-done.14.refs_1_, s16[272,256]{1,0:T(8,128)(2,1)S(1)} %collective-permute-done.17.refs_2_, bf16[2,2,2,256,1024]{4,3,2,1,0:T(8,128)(2,1)S(1)} %copy-done, ...), custom_call_target="tpu_custom_call", output_to_operand_aliasing={{}: (6, {})} | custom-call | flops 805306368 | bytes 4194304 | tf_op jit(solution)/shard_map/x_transform/pallas_call | solution.py:588
  (42 shorter events, 7.3 us)
Async XLA Ops:
  3.3 10.8 %collective-permute-start.1 = (s16[272,256]{1,0:T(8,128)(2,1)S(1)}, s16[272,256]{1,0:T(8,128)(2,1)S(1)}, u32[]{:S(2)}, u32[]{:S(2)}) collective-permute-start(s16[272,256]{1,0:T(8,128)(2,1)S(1)} %get-tuple-element.78), channel_id=1, source_target_pairs={{0,8},{4,12},{8,0},{12,4},{16,24},{20,28},{24,16},{28,20},{1,9},{5... | collective-permute-start | bytes 417800 | tf_op jit(solution)/shard_map/ppermute | solution.py:604
  6.3 11.1 %collective-permute-start.3 = (s16[272,256]{1,0:T(8,128)(2,1)S(1)}, s16[272,256]{1,0:T(8,128)(2,1)S(1)}, u32[]{:S(2)}, u32[]{:S(2)}) collective-permute-start(s16[272,256]{1,0:T(8,128)(2,1)S(1)} %get-tuple-element.80), channel_id=1, source_target_pairs={{0,16},{4,20},{8,24},{12,28},{16,0},{20,4},{24,8},{28,12},{1,17},{... | collective-permute-start | bytes 417800 | tf_op jit(solution)/shard_map/ppermute | solution.py:604
  7.8 14.3 %collective-permute-start.5 = (s16[272,256]{1,0:T(8,128)(2,1)S(1)}, s16[272,256]{1,0:T(8,128)(2,1)S(1)}, u32[]{:S(2)}, u32[]{:S(2)}) collective-permute-start(s16[272,256]{1,0:T(8,128)(2,1)S(1)} %get-tuple-element.82), channel_id=1, source_target_pairs={{0,24},{4,28},{8,16},{12,20},{16,8},{20,12},{24,0},{28,4},{1,25},{... | collective-permute-start | bytes 417800 | tf_op jit(solution)/shard_map/ppermute | solution.py:604
  7.8 14.3 %collective-permute-start.6 = (s16[272,256]{1,0:T(8,128)(2,1)S(1)}, s16[272,256]{1,0:T(8,128)(2,1)S(1)}, u32[]{:S(2)}, u32[]{:S(2)}) collective-permute-start(s16[272,256]{1,0:T(8,128)(2,1)S(1)} %get-tuple-element.83), channel_id=1, source_target_pairs={{0,28},{4,24},{8,20},{12,16},{16,12},{20,8},{24,4},{28,0},{1,29},{... | collective-permute-start | bytes 417800 | tf_op jit(solution)/shard_map/ppermute | solution.py:604
  12.5 10.7 %copy-start.1 = (bf16[2,7,256,512]{3,2,1,0:T(8,128)(2,1)S(1)}, bf16[2,7,256,512]{3,2,1,0:T(8,128)(2,1)}, u32[]{:S(2)}) copy-start(bf16[2,7,256,512]{3,2,1,0:T(8,128)(2,1)} %constant.23.clone.refs_8_.refs_5_) | copy-start | bytes 11010052
  12.5 10.7 %copy-start.3 = (bf16[2,2,128,256]{3,2,1,0:T(8,128)(2,1)S(1)}, bf16[2,2,128,256]{3,2,1,0:T(8,128)(2,1)}, u32[]{:S(2)}) copy-start(bf16[2,2,128,256]{3,2,1,0:T(8,128)(2,1)} %constant.24.clone.refs_9_.refs_6_) | copy-start | bytes 786436
  12.5 9.6 %collective-permute-start = (s16[272,256]{1,0:T(8,128)(2,1)S(1)}, s16[272,256]{1,0:T(8,128)(2,1)S(1)}, u32[]{:S(2)}, u32[]{:S(2)}) collective-permute-start(s16[272,256]{1,0:T(8,128)(2,1)S(1)} %get-tuple-element.77), channel_id=1, source_target_pairs={{0,4},{4,0},{8,12},{12,8},{16,20},{20,16},{24,28},{28,24},{1,5},{5... | collective-permute-start | bytes 417800 | tf_op jit(solution)/shard_map/ppermute | solution.py:604
  14.1 8.1 %collective-permute-start.2 = (s16[272,256]{1,0:T(8,128)(2,1)S(1)}, s16[272,256]{1,0:T(8,128)(2,1)S(1)}, u32[]{:S(2)}, u32[]{:S(2)}) collective-permute-start(s16[272,256]{1,0:T(8,128)(2,1)S(1)} %get-tuple-element.79), channel_id=1, source_target_pairs={{0,12},{4,8},{8,4},{12,0},{16,28},{20,24},{24,20},{28,16},{1,13},{... | collective-permute-start | bytes 417800 | tf_op jit(solution)/shard_map/ppermute | solution.py:604
  17.4 5.9 %collective-permute-start.4 = (s16[272,256]{1,0:T(8,128)(2,1)S(1)}, s16[272,256]{1,0:T(8,128)(2,1)S(1)}, u32[]{:S(2)}, u32[]{:S(2)}) collective-permute-start(s16[272,256]{1,0:T(8,128)(2,1)S(1)} %get-tuple-element.81), channel_id=1, source_target_pairs={{0,20},{4,16},{8,28},{12,24},{16,4},{20,0},{24,12},{28,8},{1,21},{... | collective-permute-start | bytes 417800 | tf_op jit(solution)/shard_map/ppermute | solution.py:604
  27.5 8.4 %collective-permute-start.12 = (s16[192,256]{1,0:T(8,128)(2,1)S(1)}, s16[192,256]{1,0:T(8,128)(2,1)S(1)}, u32[]{:S(2)}, u32[]{:S(2)}) collective-permute-start(s16[192,256]{1,0:T(8,128)(2,1)S(1)} %get-tuple-element.98), channel_id=1, source_target_pairs={{0,2},{1,3},{2,0},{3,1},{4,6},{5,7},{6,4},{7,5},{8,10},{9,11},{10,... | collective-permute-start | bytes 294920 | tf_op jit(solution)/shard_map/ppermute | solution.py:604
  30.2 9.5 %collective-permute-start.7 = (s16[2,272,256]{2,1,0:T(8,128)(2,1)S(1)}, s16[2,272,256]{2,1,0:T(8,128)(2,1)S(1)}, u32[]{:S(2)}, u32[]{:S(2)}) collective-permute-start(s16[2,272,256]{2,1,0:T(8,128)(2,1)S(1)} %get-tuple-element.85), channel_id=1, source_target_pairs={{0,8},{4,12},{8,0},{12,4},{16,24},{20,28},{24,16},{28,20},{1,9},{5... | collective-permute-start | bytes 835592 | tf_op jit(solution)/shard_map/ppermute | solution.py:604
  30.2 15.1 %collective-permute-start.8 = (s16[2,272,256]{2,1,0:T(8,128)(2,1)S(1)}, s16[2,272,256]{2,1,0:T(8,128)(2,1)S(1)}, u32[]{:S(2)}, u32[]{:S(2)}) collective-permute-start(s16[2,272,256]{2,1,0:T(8,128)(2,1)S(1)} %get-tuple-element.86), channel_id=1, source_target_pairs={{0,16},{4,20},{8,24},{12,28},{16,0},{20,4},{24,8},{28,12},{1,17},{... | collective-permute-start | bytes 835592 | tf_op jit(solution)/shard_map/ppermute | solution.py:604
  31.2 14.1 %collective-permute-start.9 = (s16[2,272,256]{2,1,0:T(8,128)(2,1)S(1)}, s16[2,272,256]{2,1,0:T(8,128)(2,1)S(1)}, u32[]{:S(2)}, u32[]{:S(2)}) collective-permute-start(s16[2,272,256]{2,1,0:T(8,128)(2,1)S(1)} %get-tuple-element.87), channel_id=1, source_target_pairs={{0,24},{4,28},{8,16},{12,20},{16,8},{20,12},{24,0},{28,4},{1,25},{... | collective-permute-start | bytes 835592 | tf_op jit(solution)/shard_map/ppermute | solution.py:604
  33.6 14.1 %collective-permute-start.10 = (s16[544,256]{1,0:T(8,128)(2,1)S(1)}, s16[544,256]{1,0:T(8,128)(2,1)S(1)}, u32[]{:S(2)}, u32[]{:S(2)}) collective-permute-start(s16[544,256]{1,0:T(8,128)(2,1)S(1)} %get-tuple-element.96), channel_id=1, source_target_pairs={{0,1},{1,0},{2,3},{3,2},{4,5},{5,4},{6,7},{7,6},{8,9},{9,8},{10,11... | collective-permute-start | bytes 835592 | tf_op jit(solution)/shard_map/ppermute | solution.py:604
  35.9 22.8 %copy-start.2 = (bf16[2,2,2,256,1024]{4,3,2,1,0:T(8,128)(2,1)S(1)}, bf16[2,2,2,256,1024]{4,3,2,1,0:T(8,128)(2,1)}, u32[]{:S(2)}) copy-start(bf16[2,2,2,256,1024]{4,3,2,1,0:T(8,128)(2,1)} %constant.25.clone.refs_3_.refs_4_) | copy-start | bytes 12582916
  35.9 22.8 %copy-start.4 = (s32[8]{0:T(128)S(1)}, s32[8]{0:T(128)}, u32[]{:S(2)}) copy-start(s32[8]{0:T(128)} %refs_4_.2) | copy-start | bytes 100
  35.9 22.8 %copy-start.5 = (f32[2,1024]{1,0:T(2,128)S(1)}, f32[2,1024]{1,0:T(2,128)}, u32[]{:S(2)}) copy-start(f32[2,1024]{1,0:T(2,128)} %constant.26.clone.refs_5_) | copy-start | bytes 24580
  35.9 11.9 %collective-permute-start.11 = (s16[544,256]{1,0:T(8,128)(2,1)S(1)}, s16[544,256]{1,0:T(8,128)(2,1)S(1)}, u32[]{:S(2)}, u32[]{:S(2)}) collective-permute-start(s16[544,256]{1,0:T(8,128)(2,1)S(1)} %get-tuple-element.97), channel_id=1, source_target_pairs={{0,3},{1,2},{2,1},{3,0},{4,7},{5,6},{6,5},{7,4},{8,11},{9,10},{10,... | collective-permute-start | bytes 835592 | tf_op jit(solution)/shard_map/ppermute | solution.py:604
  47.9 3.2 %collective-permute-start.13 = (s16[4,272,256]{2,1,0:T(8,128)(2,1)S(1)}, s16[4,272,256]{2,1,0:T(8,128)(2,1)S(1)}, u32[]{:S(2)}, u32[]{:S(2)}) collective-permute-start(s16[4,272,256]{2,1,0:T(8,128)(2,1)S(1)} %pad_add_fusion), channel_id=1, source_target_pairs={{0,4},{4,0},{8,12},{12,8},{16,20},{20,16},{24,28},{28,24},{1,5},{5... | collective-permute-start | bytes 1671176 | tf_op jit(solution)/shard_map/ppermute | solution.py:604
  48.0 16.6 %collective-permute-start.16 = (s16[336,256]{1,0:T(8,128)(2,1)S(1)}, s16[336,256]{1,0:T(8,128)(2,1)S(1)}, u32[]{:S(2)}, u32[]{:S(2)}) collective-permute-start(s16[336,256]{1,0:T(8,128)(2,1)S(1)} %get-tuple-element.110), channel_id=1, source_target_pairs={{0,2},{1,3},{2,0},{3,1},{4,6},{5,7},{6,4},{7,5},{8,10},{9,11},{10,... | collective-permute-start | bytes 516104 | tf_op jit(solution)/shard_map/ppermute | solution.py:604
  55.9 11.3 %collective-permute-start.15 = (s16[528,256]{1,0:T(8,128)(2,1)S(1)}, s16[528,256]{1,0:T(8,128)(2,1)S(1)}, u32[]{:S(2)}, u32[]{:S(2)}) collective-permute-start(s16[528,256]{1,0:T(8,128)(2,1)S(1)} %get-tuple-element.108), channel_id=1, source_target_pairs={{0,3},{1,2},{2,1},{3,0},{4,7},{5,6},{6,5},{7,4},{8,11},{9,10},{10,... | collective-permute-start | bytes 811016 | tf_op jit(solution)/shard_map/ppermute | solution.py:604
  62.8 16.9 %collective-permute-start.14 = (s16[528,256]{1,0:T(8,128)(2,1)S(1)}, s16[528,256]{1,0:T(8,128)(2,1)S(1)}, u32[]{:S(2)}, u32[]{:S(2)}) collective-permute-start(s16[528,256]{1,0:T(8,128)(2,1)S(1)} %get-tuple-element.105), channel_id=1, source_target_pairs={{0,1},{1,0},{2,3},{3,2},{4,5},{5,4},{6,7},{7,6},{8,9},{9,8},{10,11... | collective-permute-start | bytes 811016 | tf_op jit(solution)/shard_map/ppermute | solution.py:604
  62.9 16.8 %collective-permute-start.18 = (s16[272,256]{1,0:T(8,128)(2,1)S(1)}, s16[272,256]{1,0:T(8,128)(2,1)S(1)}, u32[]{:S(2)}, u32[]{:S(2)}) collective-permute-start(s16[272,256]{1,0:T(8,128)(2,1)S(1)} %get-tuple-element.118), channel_id=1, source_target_pairs={{0,2},{1,3},{2,0},{3,1},{4,6},{5,7},{6,4},{7,5},{8,10},{9,11},{10,... | collective-permute-start | bytes 417800 | tf_op jit(solution)/shard_map/ppermute | solution.py:604
  70.0 13.9 %collective-permute-start.17 = (s16[272,256]{1,0:T(8,128)(2,1)S(1)}, s16[272,256]{1,0:T(8,128)(2,1)S(1)}, u32[]{:S(2)}, u32[]{:S(2)}) collective-permute-start(s16[272,256]{1,0:T(8,128)(2,1)S(1)} %get-tuple-element.115), channel_id=1, source_target_pairs={{0,2},{1,3},{2,0},{3,1},{4,6},{5,7},{6,4},{7,5},{8,10},{9,11},{10,... | collective-permute-start | bytes 417800 | tf_op jit(solution)/shard_map/ppermute | solution.py:604
  (1 other events, 4.4 us)

commit v5 on v4

--- a/solution.py
+++ b/solution.py
@@ -389,7 +389,7 @@
         keep(5, 1, start, s - t)
         return carry
 
-    lax.fori_loop(0, rows // strip, combine, 0)
+    lax.fori_loop(0, rows // strip, combine, 0, unroll=4)
     dot = functools.partial(jnp.dot, preferred_element_type=jnp.float32)
     half = result.shape[1]
     for r in range(1, BLOCKS):

time: 87.5 us -> 87.3 us (level)
  no operation moved by 1% of the time
where the time goes in v5:
time: 87.3 us; the launch traced here: 87.1 us
  Pallas kernels  36.1 us (41%)
  starting transfers between devices  34.4 us (39%)
  waiting for transfers between devices  16 us (18%)
    ppermute x19, starting transfers between devices, sent(): lax.ppermute(piece, axis, [(i, i ^ d) for i in range(lax.axis_size(axis))])  34.4 us
    pallas_call x5, Pallas kernels, x_transform(): pl.pallas_call(functools.partial(x_kernel, stage, pairs, halved, side_row...  16.3 us
    ppermute x19, waiting for transfers between devices, sent(): lax.ppermute(piece, axis, [(i, i ^ d) for i in range(lax.axis_size(axis))])  16 us
    pallas_call x3, Pallas kernels, divergence(): pl.pallas_call(functools.partial(divergence_kernel, tiles, spans, order,...  11.1 us
    pallas_call x2, Pallas kernels, z_transform(): pl.pallas_call(functools.partial(z_kernel, not neighbours), in_specs=[pl....  8.73 us
  transfers between devices with their start and end apart: 19, of which 8 were waited for; matrix products, arithmetic and copies ran while one was open for 0% of the time, Pallas kernels for 29%

profile of v5, /device:TPU:0, one launch (start us, length us, event | category | flops | bytes accessed | tf_op | source)
XLA Modules:
  0.0 87.1 jit_solution(12592175927503437346)
XLA Ops:
  0.1 3.2 %divergence.3 = (s16[272,256]{1,0:T(8,128)(2,1)S(1)}, s16[272,256]{1,0:T(8,128)(2,1)S(1)}, s16[272,256]{1,0:T(8,128)(2,1)S(1)}, s16[272,256]{1,0:T(8,128)(2,1)S(1)}) custom-call(s32[4]{0:T(128)S(1)} %pad_add_fusion.1.place.refs_0_, s32[8]{0:T(128)} %refs_4_.2, bf16[8,256,512]{2,1,0:T(8,128)(2,1)} %flux_x.5, bf16[8,256,512]{2,1,0:T(8,128)(2,1)} %flux_y.5, ...), custom_call_target="tpu_custom_call" | custom-call | bytes 11808000 | tf_op jit(solution)/shard_map/divergence/pallas_call | solution.py:284
  3.3 3.0 %collective-permute-start.1 = (s16[272,256]{1,0:T(8,128)(2,1)S(1)}, s16[272,256]{1,0:T(8,128)(2,1)S(1)}, u32[]{:S(2)}, u32[]{:S(2)}) collective-permute-start(s16[272,256]{1,0:T(8,128)(2,1)S(1)} %get-tuple-element.78), channel_id=1, source_target_pairs={{0,8},{4,12},{8,0},{12,4},{16,24},{20,28},{24,16},{28,20},{1,9},{5... | collective-permute-start | bytes 417800 | tf_op jit(solution)/shard_map/ppermute | solution.py:604
  9.3 3.2 %divergence.4 = (s16[272,256]{1,0:T(8,128)(2,1)S(1)}, s16[272,256]{1,0:T(8,128)(2,1)S(1)}, s16[272,256]{1,0:T(8,128)(2,1)S(1)}, s16[272,256]{1,0:T(8,128)(2,1)S(1)}) custom-call(s32[4]{0:T(128)S(1)} %pad_add_fusion.1.place.refs_0_, s32[8]{0:T(128)} %refs_4_.2, bf16[8,256,512]{2,1,0:T(8,128)(2,1)} %flux_x.5, bf16[8,256,512]{2,1,0:T(8,128)(2,1)} %flux_y.5, ...), custom_call_target="tpu_custom_call" | custom-call | bytes 11808000 | tf_op jit(solution)/shard_map/divergence/pallas_call | solution.py:284
  12.5 1.6 %collective-permute-start = (s16[272,256]{1,0:T(8,128)(2,1)S(1)}, s16[272,256]{1,0:T(8,128)(2,1)S(1)}, u32[]{:S(2)}, u32[]{:S(2)}) collective-permute-start(s16[272,256]{1,0:T(8,128)(2,1)S(1)} %get-tuple-element.77), channel_id=1, source_target_pairs={{0,4},{4,0},{8,12},{12,8},{16,20},{20,16},{24,28},{28,24},{1,5},{5... | collective-permute-start | bytes 417800 | tf_op jit(solution)/shard_map/ppermute | solution.py:604
  14.4 3.0 %collective-permute-done.3.refs_4_ = s16[272,256]{1,0:T(8,128)(2,1)S(1)} collective-permute-done((s16[272,256]{1,0:T(8,128)(2,1)S(1)}, s16[272,256]{1,0:T(8,128)(2,1)S(1)}, u32[]{:S(2)}, u32[]{:S(2)}) %collective-permute-start.3) | collective-permute-done | bytes 139296 | tf_op jit(solution)/shard_map/ppermute | solution.py:604
  17.4 4.8 %divergence.5 = (s16[2,272,256]{2,1,0:T(8,128)(2,1)S(1)}, s16[2,272,256]{2,1,0:T(8,128)(2,1)S(1)}, s16[2,272,256]{2,1,0:T(8,128)(2,1)S(1)}, s16[2,272,256]{2,1,0:T(8,128)(2,1)S(1)}) custom-call(s32[4]{0:T(128)S(1)} %pad_add_fusion.1.place.refs_0_, s32[8]{0:T(128)} %refs_4_.2, bf16[8,256,512]{2,1,0:T(8,128)(2,1)} %flux_x.5, bf16[8,256,512]{2,1,0:T(8,128)(2,1)} %flux_y.5, ...), custom_call_target="tpu_custom_call" | custom-call | bytes 19188000 | tf_op jit(solution)/shard_map/divergence/pallas_call | solution.py:284
  23.3 4.1 %z_transform.2 = (s16[528,256]{1,0:T(8,128)(2,1)S(1)}, s16[544,256]{1,0:T(8,128)(2,1)S(1)}, s16[192,256]{1,0:T(8,128)(2,1)S(1)}, s16[544,256]{1,0:T(8,128)(2,1)S(1)}, s16[336,256]{1,0:T(8,128)(2,1)S(1)}) custom-call(s32[4]{0:T(128)S(1)} %pad_add_fusion.1.place.refs_0_, s16[272,256]{1,0:T(8,128)(2,1)S(1)} %get-tuple-element.88.refs_0_, ...), custom_call_target="tpu_custom_call" | custom-call | bytes 15498000 | tf_op jit(solution)/shard_map/z_transform/pallas_call | solution.py:446
  27.4 2.6 %collective-permute-start.12 = (s16[192,256]{1,0:T(8,128)(2,1)S(1)}, s16[192,256]{1,0:T(8,128)(2,1)S(1)}, u32[]{:S(2)}, u32[]{:S(2)}) collective-permute-start(s16[192,256]{1,0:T(8,128)(2,1)S(1)} %get-tuple-element.98), channel_id=1, source_target_pairs={{0,2},{1,3},{2,0},{3,1},{4,6},{5,7},{6,4},{7,5},{8,10},{9,11},{10,... | collective-permute-start | bytes 294920 | tf_op jit(solution)/shard_map/ppermute | solution.py:604
  31.0 2.5 %collective-permute-start.9 = (s16[2,272,256]{2,1,0:T(8,128)(2,1)S(1)}, s16[2,272,256]{2,1,0:T(8,128)(2,1)S(1)}, u32[]{:S(2)}, u32[]{:S(2)}) collective-permute-start(s16[2,272,256]{2,1,0:T(8,128)(2,1)S(1)} %get-tuple-element.87), channel_id=1, source_target_pairs={{0,24},{4,28},{8,16},{12,20},{16,8},{20,12},{24,0},{28,4},{1,25},{... | collective-permute-start | bytes 835592 | tf_op jit(solution)/shard_map/ppermute | solution.py:604
  33.5 1.6 %collective-permute-start.10 = (s16[544,256]{1,0:T(8,128)(2,1)S(1)}, s16[544,256]{1,0:T(8,128)(2,1)S(1)}, u32[]{:S(2)}, u32[]{:S(2)}) collective-permute-start(s16[544,256]{1,0:T(8,128)(2,1)S(1)} %get-tuple-element.96), channel_id=1, source_target_pairs={{0,1},{1,0},{2,3},{3,2},{4,5},{5,4},{6,7},{7,6},{8,9},{9,8},{10,11... | collective-permute-start | bytes 835592 | tf_op jit(solution)/shard_map/ppermute | solution.py:604
  35.7 3.6 %collective-permute-start.11 = (s16[544,256]{1,0:T(8,128)(2,1)S(1)}, s16[544,256]{1,0:T(8,128)(2,1)S(1)}, u32[]{:S(2)}, u32[]{:S(2)}) collective-permute-start(s16[544,256]{1,0:T(8,128)(2,1)S(1)} %get-tuple-element.97), channel_id=1, source_target_pairs={{0,3},{1,2},{2,1},{3,0},{4,7},{5,6},{6,5},{7,4},{8,11},{9,10},{10,... | collective-permute-start | bytes 835592 | tf_op jit(solution)/shard_map/ppermute | solution.py:604
  39.5 5.6 %collective-permute-done.8.refs_2_ = s16[2,272,256]{2,1,0:T(8,128)(2,1)S(1)} collective-permute-done((s16[2,272,256]{2,1,0:T(8,128)(2,1)S(1)}, s16[2,272,256]{2,1,0:T(8,128)(2,1)S(1)}, u32[]{:S(2)}, u32[]{:S(2)}) %collective-permute-start.8) | collective-permute-done | bytes 278560 | tf_op jit(solution)/shard_map/ppermute | solution.py:604
  45.1 2.5 %collective-permute-done.10.refs_7_.refs_1_ = s16[544,256]{1,0:T(8,128)(2,1)S(1)} collective-permute-done((s16[544,256]{1,0:T(8,128)(2,1)S(1)}, s16[544,256]{1,0:T(8,128)(2,1)S(1)}, u32[]{:S(2)}, u32[]{:S(2)}) %collective-permute-start.10) | collective-permute-done | bytes 278560 | tf_op jit(solution)/shard_map/ppermute | solution.py:604
  47.9 3.2 %collective-permute-start.16 = (s16[336,256]{1,0:T(8,128)(2,1)S(1)}, s16[336,256]{1,0:T(8,128)(2,1)S(1)}, u32[]{:S(2)}, u32[]{:S(2)}) collective-permute-start(s16[336,256]{1,0:T(8,128)(2,1)S(1)} %get-tuple-element.110), channel_id=1, source_target_pairs={{0,2},{1,3},{2,0},{3,1},{4,6},{5,7},{6,4},{7,5},{8,10},{9,11},{10,... | collective-permute-start | bytes 516104 | tf_op jit(solution)/shard_map/ppermute | solution.py:604
  51.0 4.6 %z_transform.3 = (s16[528,256]{1,0:T(8,128)(2,1)S(1)}, s16[528,256]{1,0:T(8,128)(2,1)S(1)}, s16[272,256]{1,0:T(8,128)(2,1)S(1)}, s16[528,256]{1,0:T(8,128)(2,1)S(1)}, s16[272,256]{1,0:T(8,128)(2,1)S(1)}) custom-call(s32[4]{0:T(128)S(1)} %pad_add_fusion.1.place.refs_0_, s16[2,272,256]{2,1,0:T(8,128)(2,1)S(1)} %get-tuple-element.99.refs_0_, ...), custom_call_target="tpu_custom_call" | custom-call | bytes 15498000 | tf_op jit(solution)/shard_map/z_transform/pallas_call | solution.py:446
  55.7 2.7 %collective-permute-start.15 = (s16[528,256]{1,0:T(8,128)(2,1)S(1)}, s16[528,256]{1,0:T(8,128)(2,1)S(1)}, u32[]{:S(2)}, u32[]{:S(2)}) collective-permute-start(s16[528,256]{1,0:T(8,128)(2,1)S(1)} %get-tuple-element.108), channel_id=1, source_target_pairs={{0,3},{1,2},{2,1},{3,0},{4,7},{5,6},{6,5},{7,4},{8,11},{9,10},{10,... | collective-permute-start | bytes 811016 | tf_op jit(solution)/shard_map/ppermute | solution.py:604
  58.4 4.1 %x_transform.5 = (f32[2,512,1024]{2,1,0:T(8,128)S(1)}, f32[2,512,1024]{2,1,0:T(8,128)S(1)}) custom-call(s32[4]{0:T(128)S(1)} %pad_add_fusion.1.place.refs_0_, s16[528,256]{1,0:T(8,128)(2,1)S(1)} %get-tuple-element.112.refs_1_, s16[544,256]{1,0:T(8,128)(2,1)S(1)} %collective-permute-done.11.refs_8_.refs_2_, bf16[2,2,2,256,1024]{4,3,2,1,0:T(8,128)(2,1)S(1)} %copy-done.2, ...), custom_call_target="tpu_custom_call" | custom-call | flops 1610612736 | bytes 8388608 | tf_op jit(solution)/shard_map/x_transform/pallas_call | solution.py:588
  62.7 1.7 %collective-permute-start.18 = (s16[272,256]{1,0:T(8,128)(2,1)S(1)}, s16[272,256]{1,0:T(8,128)(2,1)S(1)}, u32[]{:S(2)}, u32[]{:S(2)}) collective-permute-start(s16[272,256]{1,0:T(8,128)(2,1)S(1)} %get-tuple-element.118), channel_id=1, source_target_pairs={{0,2},{1,3},{2,0},{3,1},{4,6},{5,7},{6,4},{7,5},{8,10},{9,11},{10,... | collective-permute-start | bytes 417800 | tf_op jit(solution)/shard_map/ppermute | solution.py:604
  64.3 2.7 %x_transform.6.refs_4_ = f32[2,512,1024]{2,1,0:T(8,128)S(1)} custom-call(s32[4]{0:T(128)S(1)} %pad_add_fusion.1.place.refs_0_, s16[544,256]{1,0:T(8,128)(2,1)S(1)} %collective-permute-done.10.refs_7_.refs_1_, s16[192,256]{1,0:T(8,128)(2,1)S(1)} %collective-permute-done.12.refs_2_, s16[336,256]{1,0:T(8,128)(2,1)S(1)} %collective-permute-done.16.refs_3_, ...), custom_call_target="tpu_custom_call" | custom-call | flops 1610612736 | bytes 8388608 | tf_op jit(solution)/shard_map/x_transform/pallas_call | solution.py:588
  67.0 2.7 %x_transform.7.refs_4_ = f32[2,512,1024]{2,1,0:T(8,128)S(1)} custom-call(s32[4]{0:T(128)S(1)} %pad_add_fusion.1.place.refs_0_, s16[528,256]{1,0:T(8,128)(2,1)S(1)} %get-tuple-element.107.refs_1_, s16[528,256]{1,0:T(8,128)(2,1)S(1)} %collective-permute-done.15.refs_2_, bf16[2,2,2,256,1024]{4,3,2,1,0:T(8,128)(2,1)S(1)} %copy-done, ...), custom_call_target="tpu_custom_call" | custom-call | flops 1610612736 | bytes 8388608 | tf_op jit(solution)/shard_map/x_transform/pallas_call | solution.py:588
  69.7 7.5 %collective-permute-start.17 = (s16[272,256]{1,0:T(8,128)(2,1)S(1)}, s16[272,256]{1,0:T(8,128)(2,1)S(1)}, u32[]{:S(2)}, u32[]{:S(2)}) collective-permute-start(s16[272,256]{1,0:T(8,128)(2,1)S(1)} %get-tuple-element.115), channel_id=1, source_target_pairs={{0,2},{1,3},{2,0},{3,1},{4,6},{5,7},{6,4},{7,5},{8,10},{9,11},{10,... | collective-permute-start | bytes 417800 | tf_op jit(solution)/shard_map/ppermute | solution.py:604
  77.3 2.2 %collective-permute-done.18.refs_2_ = s16[272,256]{1,0:T(8,128)(2,1)S(1)} collective-permute-done((s16[272,256]{1,0:T(8,128)(2,1)S(1)}, s16[272,256]{1,0:T(8,128)(2,1)S(1)}, u32[]{:S(2)}, u32[]{:S(2)}) %collective-permute-start.18) | collective-permute-done | bytes 139296 | tf_op jit(solution)/shard_map/ppermute | solution.py:604
  79.4 3.4 %x_transform.8.refs_6_ = f32[8192,128]{1,0:T(8,128)} custom-call(s32[4]{0:T(128)S(1)} %pad_add_fusion.1.place.refs_0_, s16[528,256]{1,0:T(8,128)(2,1)S(1)} %collective-permute-done.14.refs_1_, s16[272,256]{1,0:T(8,128)(2,1)S(1)} %collective-permute-done.18.refs_2_, bf16[2,2,2,256,1024]{4,3,2,1,0:T(8,128)(2,1)S(1)} %copy-done, ...), custom_call_target="tpu_custom_call" | custom-call | flops 805306368 | bytes 4194304 | tf_op jit(solution)/shard_map/x_transform/pallas_call | solution.py:588
  83.6 3.4 %x_transform.9 = f32[8192,128]{1,0:T(8,128)} custom-call(s32[4]{0:T(128)S(1)} %pad_add_fusion.1.place.refs_0_, s16[528,256]{1,0:T(8,128)(2,1)S(1)} %collective-permute-done.14.refs_1_, s16[272,256]{1,0:T(8,128)(2,1)S(1)} %collective-permute-done.17.refs_2_, bf16[2,2,2,256,1024]{4,3,2,1,0:T(8,128)(2,1)S(1)} %copy-done, ...), custom_call_target="tpu_custom_call", output_to_operand_aliasing={{}: (6, {})} | custom-call | flops 805306368 | bytes 4194304 | tf_op jit(solution)/shard_map/x_transform/pallas_call | solution.py:588
  (42 shorter events, 7.3 us)
Async XLA Ops:
  3.3 10.8 %collective-permute-start.1 = (s16[272,256]{1,0:T(8,128)(2,1)S(1)}, s16[272,256]{1,0:T(8,128)(2,1)S(1)}, u32[]{:S(2)}, u32[]{:S(2)}) collective-permute-start(s16[272,256]{1,0:T(8,128)(2,1)S(1)} %get-tuple-element.78), channel_id=1, source_target_pairs={{0,8},{4,12},{8,0},{12,4},{16,24},{20,28},{24,16},{28,20},{1,9},{5... | collective-permute-start | bytes 417800 | tf_op jit(solution)/shard_map/ppermute | solution.py:604
  6.3 11.1 %collective-permute-start.3 = (s16[272,256]{1,0:T(8,128)(2,1)S(1)}, s16[272,256]{1,0:T(8,128)(2,1)S(1)}, u32[]{:S(2)}, u32[]{:S(2)}) collective-permute-start(s16[272,256]{1,0:T(8,128)(2,1)S(1)} %get-tuple-element.80), channel_id=1, source_target_pairs={{0,16},{4,20},{8,24},{12,28},{16,0},{20,4},{24,8},{28,12},{1,17},{... | collective-permute-start | bytes 417800 | tf_op jit(solution)/shard_map/ppermute | solution.py:604
  7.8 14.3 %collective-permute-start.5 = (s16[272,256]{1,0:T(8,128)(2,1)S(1)}, s16[272,256]{1,0:T(8,128)(2,1)S(1)}, u32[]{:S(2)}, u32[]{:S(2)}) collective-permute-start(s16[272,256]{1,0:T(8,128)(2,1)S(1)} %get-tuple-element.82), channel_id=1, source_target_pairs={{0,24},{4,28},{8,16},{12,20},{16,8},{20,12},{24,0},{28,4},{1,25},{... | collective-permute-start | bytes 417800 | tf_op jit(solution)/shard_map/ppermute | solution.py:604
  7.8 14.3 %collective-permute-start.6 = (s16[272,256]{1,0:T(8,128)(2,1)S(1)}, s16[272,256]{1,0:T(8,128)(2,1)S(1)}, u32[]{:S(2)}, u32[]{:S(2)}) collective-permute-start(s16[272,256]{1,0:T(8,128)(2,1)S(1)} %get-tuple-element.83), channel_id=1, source_target_pairs={{0,28},{4,24},{8,20},{12,16},{16,12},{20,8},{24,4},{28,0},{1,29},{... | collective-permute-start | bytes 417800 | tf_op jit(solution)/shard_map/ppermute | solution.py:604
  12.5 10.7 %copy-start.1 = (bf16[2,7,256,512]{3,2,1,0:T(8,128)(2,1)S(1)}, bf16[2,7,256,512]{3,2,1,0:T(8,128)(2,1)}, u32[]{:S(2)}) copy-start(bf16[2,7,256,512]{3,2,1,0:T(8,128)(2,1)} %constant.23.clone.refs_8_.refs_5_) | copy-start | bytes 11010052
  12.5 10.7 %copy-start.3 = (bf16[2,2,128,256]{3,2,1,0:T(8,128)(2,1)S(1)}, bf16[2,2,128,256]{3,2,1,0:T(8,128)(2,1)}, u32[]{:S(2)}) copy-start(bf16[2,2,128,256]{3,2,1,0:T(8,128)(2,1)} %constant.24.clone.refs_9_.refs_6_) | copy-start | bytes 786436
  12.5 9.6 %collective-permute-start = (s16[272,256]{1,0:T(8,128)(2,1)S(1)}, s16[272,256]{1,0:T(8,128)(2,1)S(1)}, u32[]{:S(2)}, u32[]{:S(2)}) collective-permute-start(s16[272,256]{1,0:T(8,128)(2,1)S(1)} %get-tuple-element.77), channel_id=1, source_target_pairs={{0,4},{4,0},{8,12},{12,8},{16,20},{20,16},{24,28},{28,24},{1,5},{5... | collective-permute-start | bytes 417800 | tf_op jit(solution)/shard_map/ppermute | solution.py:604
  14.1 8.1 %collective-permute-start.2 = (s16[272,256]{1,0:T(8,128)(2,1)S(1)}, s16[272,256]{1,0:T(8,128)(2,1)S(1)}, u32[]{:S(2)}, u32[]{:S(2)}) collective-permute-start(s16[272,256]{1,0:T(8,128)(2,1)S(1)} %get-tuple-element.79), channel_id=1, source_target_pairs={{0,12},{4,8},{8,4},{12,0},{16,28},{20,24},{24,20},{28,16},{1,13},{... | collective-permute-start | bytes 417800 | tf_op jit(solution)/shard_map/ppermute | solution.py:604
  17.4 5.9 %collective-permute-start.4 = (s16[272,256]{1,0:T(8,128)(2,1)S(1)}, s16[272,256]{1,0:T(8,128)(2,1)S(1)}, u32[]{:S(2)}, u32[]{:S(2)}) collective-permute-start(s16[272,256]{1,0:T(8,128)(2,1)S(1)} %get-tuple-element.81), channel_id=1, source_target_pairs={{0,20},{4,16},{8,28},{12,24},{16,4},{20,0},{24,12},{28,8},{1,21},{... | collective-permute-start | bytes 417800 | tf_op jit(solution)/shard_map/ppermute | solution.py:604
  27.4 8.4 %collective-permute-start.12 = (s16[192,256]{1,0:T(8,128)(2,1)S(1)}, s16[192,256]{1,0:T(8,128)(2,1)S(1)}, u32[]{:S(2)}, u32[]{:S(2)}) collective-permute-start(s16[192,256]{1,0:T(8,128)(2,1)S(1)} %get-tuple-element.98), channel_id=1, source_target_pairs={{0,2},{1,3},{2,0},{3,1},{4,6},{5,7},{6,4},{7,5},{8,10},{9,11},{10,... | collective-permute-start | bytes 294920 | tf_op jit(solution)/shard_map/ppermute | solution.py:604
  30.0 9.5 %collective-permute-start.7 = (s16[2,272,256]{2,1,0:T(8,128)(2,1)S(1)}, s16[2,272,256]{2,1,0:T(8,128)(2,1)S(1)}, u32[]{:S(2)}, u32[]{:S(2)}) collective-permute-start(s16[2,272,256]{2,1,0:T(8,128)(2,1)S(1)} %get-tuple-element.85), channel_id=1, source_target_pairs={{0,8},{4,12},{8,0},{12,4},{16,24},{20,28},{24,16},{28,20},{1,9},{5... | collective-permute-start | bytes 835592 | tf_op jit(solution)/shard_map/ppermute | solution.py:604
  30.0 15.1 %collective-permute-start.8 = (s16[2,272,256]{2,1,0:T(8,128)(2,1)S(1)}, s16[2,272,256]{2,1,0:T(8,128)(2,1)S(1)}, u32[]{:S(2)}, u32[]{:S(2)}) collective-permute-start(s16[2,272,256]{2,1,0:T(8,128)(2,1)S(1)} %get-tuple-element.86), channel_id=1, source_target_pairs={{0,16},{4,20},{8,24},{12,28},{16,0},{20,4},{24,8},{28,12},{1,17},{... | collective-permute-start | bytes 835592 | tf_op jit(solution)/shard_map/ppermute | solution.py:604
  31.0 14.1 %collective-permute-start.9 = (s16[2,272,256]{2,1,0:T(8,128)(2,1)S(1)}, s16[2,272,256]{2,1,0:T(8,128)(2,1)S(1)}, u32[]{:S(2)}, u32[]{:S(2)}) collective-permute-start(s16[2,272,256]{2,1,0:T(8,128)(2,1)S(1)} %get-tuple-element.87), channel_id=1, source_target_pairs={{0,24},{4,28},{8,16},{12,20},{16,8},{20,12},{24,0},{28,4},{1,25},{... | collective-permute-start | bytes 835592 | tf_op jit(solution)/shard_map/ppermute | solution.py:604
  33.5 14.1 %collective-permute-start.10 = (s16[544,256]{1,0:T(8,128)(2,1)S(1)}, s16[544,256]{1,0:T(8,128)(2,1)S(1)}, u32[]{:S(2)}, u32[]{:S(2)}) collective-permute-start(s16[544,256]{1,0:T(8,128)(2,1)S(1)} %get-tuple-element.96), channel_id=1, source_target_pairs={{0,1},{1,0},{2,3},{3,2},{4,5},{5,4},{6,7},{7,6},{8,9},{9,8},{10,11... | collective-permute-start | bytes 835592 | tf_op jit(solution)/shard_map/ppermute | solution.py:604
  35.7 22.7 %copy-start.2 = (bf16[2,2,2,256,1024]{4,3,2,1,0:T(8,128)(2,1)S(1)}, bf16[2,2,2,256,1024]{4,3,2,1,0:T(8,128)(2,1)}, u32[]{:S(2)}) copy-start(bf16[2,2,2,256,1024]{4,3,2,1,0:T(8,128)(2,1)} %constant.25.clone.refs_3_.refs_4_) | copy-start | bytes 12582916
  35.7 22.7 %copy-start.4 = (s32[8]{0:T(128)S(1)}, s32[8]{0:T(128)}, u32[]{:S(2)}) copy-start(s32[8]{0:T(128)} %refs_4_.2) | copy-start | bytes 100
  35.7 22.7 %copy-start.5 = (f32[2,1024]{1,0:T(2,128)S(1)}, f32[2,1024]{1,0:T(2,128)}, u32[]{:S(2)}) copy-start(f32[2,1024]{1,0:T(2,128)} %constant.26.clone.refs_5_) | copy-start | bytes 24580
  35.7 11.9 %collective-permute-start.11 = (s16[544,256]{1,0:T(8,128)(2,1)S(1)}, s16[544,256]{1,0:T(8,128)(2,1)S(1)}, u32[]{:S(2)}, u32[]{:S(2)}) collective-permute-start(s16[544,256]{1,0:T(8,128)(2,1)S(1)} %get-tuple-element.97), channel_id=1, source_target_pairs={{0,3},{1,2},{2,1},{3,0},{4,7},{5,6},{6,5},{7,4},{8,11},{9,10},{10,... | collective-permute-start | bytes 835592 | tf_op jit(solution)/shard_map/ppermute | solution.py:604
  47.8 3.2 %collective-permute-start.13 = (s16[4,272,256]{2,1,0:T(8,128)(2,1)S(1)}, s16[4,272,256]{2,1,0:T(8,128)(2,1)S(1)}, u32[]{:S(2)}, u32[]{:S(2)}) collective-permute-start(s16[4,272,256]{2,1,0:T(8,128)(2,1)S(1)} %pad_add_fusion), channel_id=1, source_target_pairs={{0,4},{4,0},{8,12},{12,8},{16,20},{20,16},{24,28},{28,24},{1,5},{5... | collective-permute-start | bytes 1671176 | tf_op jit(solution)/shard_map/ppermute | solution.py:604
  47.9 16.5 %collective-permute-start.16 = (s16[336,256]{1,0:T(8,128)(2,1)S(1)}, s16[336,256]{1,0:T(8,128)(2,1)S(1)}, u32[]{:S(2)}, u32[]{:S(2)}) collective-permute-start(s16[336,256]{1,0:T(8,128)(2,1)S(1)} %get-tuple-element.110), channel_id=1, source_target_pairs={{0,2},{1,3},{2,0},{3,1},{4,6},{5,7},{6,4},{7,5},{8,10},{9,11},{10,... | collective-permute-start | bytes 516104 | tf_op jit(solution)/shard_map/ppermute | solution.py:604
  55.7 11.3 %collective-permute-start.15 = (s16[528,256]{1,0:T(8,128)(2,1)S(1)}, s16[528,256]{1,0:T(8,128)(2,1)S(1)}, u32[]{:S(2)}, u32[]{:S(2)}) collective-permute-start(s16[528,256]{1,0:T(8,128)(2,1)S(1)} %get-tuple-element.108), channel_id=1, source_target_pairs={{0,3},{1,2},{2,1},{3,0},{4,7},{5,6},{6,5},{7,4},{8,11},{9,10},{10,... | collective-permute-start | bytes 811016 | tf_op jit(solution)/shard_map/ppermute | solution.py:604
  62.6 16.9 %collective-permute-start.14 = (s16[528,256]{1,0:T(8,128)(2,1)S(1)}, s16[528,256]{1,0:T(8,128)(2,1)S(1)}, u32[]{:S(2)}, u32[]{:S(2)}) collective-permute-start(s16[528,256]{1,0:T(8,128)(2,1)S(1)} %get-tuple-element.105), channel_id=1, source_target_pairs={{0,1},{1,0},{2,3},{3,2},{4,5},{5,4},{6,7},{7,6},{8,9},{9,8},{10,11... | collective-permute-start | bytes 811016 | tf_op jit(solution)/shard_map/ppermute | solution.py:604
  62.7 16.8 %collective-permute-start.18 = (s16[272,256]{1,0:T(8,128)(2,1)S(1)}, s16[272,256]{1,0:T(8,128)(2,1)S(1)}, u32[]{:S(2)}, u32[]{:S(2)}) collective-permute-start(s16[272,256]{1,0:T(8,128)(2,1)S(1)} %get-tuple-element.118), channel_id=1, source_target_pairs={{0,2},{1,3},{2,0},{3,1},{4,6},{5,7},{6,4},{7,5},{8,10},{9,11},{10,... | collective-permute-start | bytes 417800 | tf_op jit(solution)/shard_map/ppermute | solution.py:604
  69.7 13.9 %collective-permute-start.17 = (s16[272,256]{1,0:T(8,128)(2,1)S(1)}, s16[272,256]{1,0:T(8,128)(2,1)S(1)}, u32[]{:S(2)}, u32[]{:S(2)}) collective-permute-start(s16[272,256]{1,0:T(8,128)(2,1)S(1)} %get-tuple-element.115), channel_id=1, source_target_pairs={{0,2},{1,3},{2,0},{3,1},{4,6},{5,7},{6,4},{7,5},{8,10},{9,11},{10,... | collective-permute-start | bytes 417800 | tf_op jit(solution)/shard_map/ppermute | solution.py:604
  (1 other events, 4.4 us)
